TPU v7x, 32 devices: a whole 2x2x4 slice. The times are simulated.
32 devices in a mesh: dp: 8 (over z, y), mp: 4 (over x, core).
Axes of the slice: x: 2, y: 2, z: 4, core: 2. Of those that a mesh axis runs over, the one named last changes fastest.
Arguments:
- tokens_in: bfloat16 [8192, 768], P('dp'), may hold values from -6 to 6
- first_values: bfloat16 [8192, 768], P('dp', 'mp'), may hold values from -8 to 8
- skip_source: int32 [12], replicated, may hold values from 0 to 12, as said below
- grad_out: bfloat16 [8192, 768], P('dp'), may hold values from -6 to 6
- qkv_weight: float32 [768, 2304], P('dp', 'mp'), may hold values from -0.3125 to 0.3125
- proj_weight: float32 [768, 768], P('mp', 'dp'), may hold values from -0.875 to 0.875
- fc_weight: float32 [768, 3072], P('dp', 'mp'), may hold values from -0.21875 to 0.21875
- down_weight: float32 [3072, 768], P('mp', 'dp'), may hold values from -0.15625 to 0.15625
- norm_params: float32 [4, 768], P(None, 'dp'), may hold values from -0.5 to 1.5, as said below
- qkv_moment: float32 [768, 2304], P('dp', 'mp'), may hold values from -128 to 128
- proj_moment: float32 [768, 768], P('mp', 'dp'), may hold values from -20 to 20
- fc_moment: float32 [768, 3072], P('dp', 'mp'), may hold values from -32 to 32
- down_moment: float32 [3072, 768], P('mp', 'dp'), may hold values from -40 to 40
- norm_moment: float32 [4, 768], P(None, 'dp'), may hold values from -128 to 128
- qkv_second: float32 [768, 2304], P('dp', 'mp'), may hold values from 32.768 to 131.072
- proj_second: float32 [768, 768], P('mp', 'dp'), may hold values from 1.007616 to 4.01408
- fc_second: float32 [768, 3072], P('dp', 'mp'), may hold values from 2.048 to 8.192
- down_second: float32 [3072, 768], P('mp', 'dp'), may hold values from 3.44064 to 13.9264
- norm_second: float32 [4, 768], P(None, 'dp'), may hold values from 32.768 to 131.072
Outputs:
- block_out: bfloat16 [8192, 768], P(('dp', 'mp'))
- input_grad: float32 [8192, 768], P(('dp', 'mp'))
- first_grad: float32 [8192, 768], P('dp', 'mp')
- qkv_weight_out: float32 [768, 2304], P('dp', 'mp')
- qkv_moment_out: float32 [768, 2304], P('dp', 'mp')
- qkv_second_out: float32 [768, 2304], P('dp', 'mp')
- proj_weight_out: float32 [768, 768], P('mp', 'dp')
- proj_moment_out: float32 [768, 768], P('mp', 'dp')
- proj_second_out: float32 [768, 768], P('mp', 'dp')
- fc_weight_out: float32 [768, 3072], P('dp', 'mp')
- fc_moment_out: float32 [768, 3072], P('dp', 'mp')
- fc_second_out: float32 [768, 3072], P('dp', 'mp')
- down_weight_out: float32 [3072, 768], P('mp', 'dp')
- down_moment_out: float32 [3072, 768], P('mp', 'dp')
- down_second_out: float32 [3072, 768], P('mp', 'dp')
- norm_params_out: float32 [4, 768], P(None, 'dp')
- norm_moment_out: float32 [4, 768], P(None, 'dp')
- norm_second_out: float32 [4, 768], P(None, 'dp')
Inputs may be any that keep to these rules, and one draw needn't show every extreme that they name: `skip_source`: exactly 6 entries are below 12, and these are distinct; which heads reuse first-layer values is drawn. `norm_params`: rows 0 and 2 are gains, rows 1 and 3 shifts.
All inputs are finite; a program needn't handle non-finite values.
Results may differ from a plain program's by a relative error of at most 0.012.
The roundings to bfloat16 on the way count: a program that leaves them out, or rounds other values in their place, can miss the bound.
Values may be sent and summed in bfloat16 or wider, within the bound.
No kernel may reach another device: no remote copies, remote signals or barrier semaphores. Data moves between devices by JAX's collectives and lax.ppermute only.
A program may use at most 128 MiB of HBM per device.

v0:
```python
import functools

import jax
import jax.numpy as jnp
import numpy as np
from jax import lax
from jax.experimental import pallas as pl
from jax.experimental.pallas import tpu as pltpu
from jax.sharding import PartitionSpec as P

H = 12
HD = 64
ADAM_STEP = 5
EPS = 1e-05
MASKED = -1e30
RB = 256
LANES = 128
RING = (0, 2, 4, 6, 7, 5, 3, 1)
OFFSETS = (0, -1, -2, -3, -4, 1, 2, 3)
GELU_A = 0.7978845608028654
GELU_B = 0.044715
RATES = {"qkv": 0.06, "proj": 0.15, "fc": 0.04, "down": 0.03, "norm": 0.3}

bf16 = jnp.bfloat16
f32 = jnp.float32


def dot(a, b):
    return jnp.dot(a, b, preferred_element_type=f32)


def dot_nt(a, b):
    return lax.dot_general(a, b, (((1,), (1,)), ((), ())), preferred_element_type=f32)


def dot_tn(a, b):
    return lax.dot_general(a, b, (((0,), (0,)), ((), ())), preferred_element_type=f32)


class Place:
    def __init__(self):
        self.mp, self.dp = lax.axis_index("mp"), lax.axis_index("dp")

    def __getitem__(self, k):
        if k < 4:
            return (self.mp % 2, self.mp // 2, self.mp, self.dp)[k]
        if lax.axis_size("dp") != len(RING):
            return 0
        z, y = self.dp // 2, self.dp % 2
        at = (jnp.where(y == 0, z, 7 - z) + OFFSETS[k - 4] + 8) % 8
        return jnp.where(at < 4, 2 * at, 2 * (7 - at) + 1)


HERE = object()


def call(kernel, name, scalars, ins, outs, scratch=(), vmem=16, far=False):
    if HERE in scalars:
        inner = kernel
        kernel = lambda *refs: inner(Place(), *refs)
        scalars = scalars[1:]
    smem = pl.BlockSpec(memory_space=pltpu.SMEM)
    full = pl.BlockSpec(memory_space=pltpu.VMEM)
    given = pl.BlockSpec(memory_space=pltpu.HBM) if far else full
    return pl.pallas_call(
        kernel,
        in_specs=[smem] * len(scalars) + [given] * len(ins),
        out_specs=[full] * len(outs),
        out_shape=[jax.ShapeDtypeStruct(sh, dt) for sh, dt in outs],
        scratch_shapes=list(scratch),
        compiler_params=pltpu.CompilerParams(vmem_limit_bytes=vmem * 1024 * 1024),
        cost_estimate=pl.CostEstimate(flops=1, bytes_accessed=1, transcendentals=0),
        name=name,
    )(*scalars, *ins)


def block(index, size=RB):
    if isinstance(index, int):
        return slice(index * size, (index + 1) * size)
    return pl.ds(pl.multiple_of(index * size, size), size)


def fetch(pairs, sems):
    copies = [pltpu.make_async_copy(src, dst, sems.at[k]) for k, (src, dst) in enumerate(pairs)]
    for copy in copies:
        copy.start()
    for copy in copies:
        copy.wait()


def prep_one_kernel(q_ref, n_ref, out, q, norms, turn, sems):
    rows, cols = q.shape
    turn[...] = jnp.zeros(turn.shape, f32)
    fetch([(q_ref, q), (n_ref, norms)], sems)
    turn[: norms.shape[0], :rows] = norms[...]
    out[:, :cols] = q[...].astype(bf16)
    out[:, cols:] = turn[...].T[:rows, : out.shape[1] - cols].astype(bf16)


def prep_two_kernel(p_ref, f_ref, d_ref, proj, fc, down, p, f, d, turn, sems):
    rows = proj.shape[0]
    turn[...] = jnp.zeros(turn.shape, f32)
    fetch([(p_ref, p), (f_ref, f), (d_ref, d)], sems)
    turn[:, :rows] = p[...]
    proj[...] = turn[...].T[:rows].astype(bf16)
    fc[...] = f[...].astype(bf16)
    down[...] = d[...].astype(bf16)


def join_kernel(f_ref, own, across, out):
    hid, cw = f_ref.shape[1], own.shape[1]
    out[:, :hid] = f_ref[...]
    out[:, hid:] = jnp.concatenate([own[...], across[...]], 1)


def norm_stats(values):
    center = values - jnp.mean(values, axis=-1, keepdims=True)
    scale = lax.rsqrt(jnp.mean(center * center, axis=-1, keepdims=True) + EPS)
    return center * scale, scale


def unit_kernel(x_ref, unit_ref):
    for i in range(x_ref.shape[0] // RB):
        at = slice(i * RB, (i + 1) * RB)
        unit_ref[at] = norm_stats(x_ref[at].astype(f32))[0]


def fetch_kernel(src, out, sem):
    copy = pltpu.make_async_copy(src, out, sem)
    copy.start()
    copy.wait()


def loop(count, body):
    lax.fori_loop(0, count, lambda i, carry: (body(i), carry)[1], 0)


def qkv_kernel(n, heads, info, unit_ref, *refs):
    pieces, (a1_ref, m_ref, v_ref, w_ref, norm_ref) = refs[:n], refs[n:]
    cols = m_ref.shape[1]
    base = cols // LANES * LANES
    rows = w_ref.shape[0] // n
    for k, piece in enumerate(pieces):
        w_ref[block(info[4 + k], rows), :] = piece[...]
    turned = w_ref[:, base : base + LANES].astype(f32).T
    norm_ref[...] = turned[cols - base : cols - base + 8]

    def step(i):
        at = block(i)
        a1 = (unit_ref[at, :] * norm_ref[0:1] + norm_ref[1:2]).astype(bf16)
        a1_ref[at, :] = a1
        mixed = dot(a1, w_ref[:, :cols])
        m_ref[at, :] = mixed.astype(bf16)
        for h in range(heads):
            fresh = mixed[:, (3 * h + 2) * HD : (3 * h + 3) * HD]
            v_ref[h * HD : (h + 1) * HD, at] = fresh.T.astype(bf16)

    loop(m_ref.shape[0] // RB, step)


def values_kernel(heads, info, src, fresh, f0, f1, f2, f3, v_ref):
    mp = info[2]
    for h in range(heads):
        source = src[mp * heads + h]
        held = source // heads
        mine = slice(h * HD, (h + 1) * HD)

        @pl.when(source >= H)
        def _():
            v_ref[mine, :] = fresh[mine, :]

        for r, first in enumerate((f0, f1, f2, f3)):

            @pl.when((source < H) & (held == mp ^ r))
            def _():
                v_ref[mine, :] = first[block(source - held * heads, HD), :]


def masked_tile():
    keys = lax.broadcasted_iota(jnp.int32, (RB, RB), 0)
    queries = lax.broadcasted_iota(jnp.int32, (RB, RB), 1)
    return keys <= queries


def attend_kernel(heads, base, m_ref, v_ref, c_ref, lse_ref, keys_ref, query_ref, turned):
    keep = masked_tile()
    blocks = c_ref.shape[0] // RB
    top = base + blocks * RB
    lse_ref[...] = jnp.zeros(lse_ref.shape, f32)
    for h in range(heads):
        keys_ref[h] = m_ref[:top, (3 * h + 1) * HD : (3 * h + 2) * HD]
        query_ref[h] = m_ref[base:top, 3 * h * HD : (3 * h + 1) * HD] * bf16(HD**-0.5)

    def step(h):
        mine = block(h, HD)
        for i in range(blocks):
            lo = base + i * RB
            hi = lo + RB
            at = slice(i * RB, (i + 1) * RB)
            query = query_ref[h, at]
            diag = jnp.where(keep, dot_nt(keys_ref[h, lo:hi], query), MASKED)
            peak = jnp.max(diag, 0, keepdims=True)
            if lo:
                left = dot_nt(keys_ref[h, :lo], query)
                peak = jnp.maximum(peak, jnp.max(left, 0, keepdims=True))
            diag = jnp.exp(diag - peak)
            total = jnp.sum(diag, 0, keepdims=True)
            if lo:
                left = jnp.exp(left - peak)
                total += jnp.sum(left, 0, keepdims=True)
            inverse = 1.0 / total
            context = dot(v_ref[mine, lo:hi], (diag * inverse).astype(bf16))
            if lo:
                context += dot(v_ref[mine, :lo], (left * inverse).astype(bf16))
            turned[mine, at] = context
            lse_ref[pl.ds(h, 1), at] = peak + jnp.log(total)

    loop(heads, step)
    c_ref[...] = turned[...].T.astype(bf16)


def assemble_two_kernel(n, info, *refs):
    pieces, (wf, own, across, turn) = refs[:n], refs[n:]
    width, hid = wf.shape
    cw = own.shape[0]
    rows = width // n
    for k, piece in enumerate(pieces):
        at = block(info[4 + k], rows)
        wf[at, :] = piece[:, :hid]
        turn[at, :] = piece[:, hid:]
    pair = turn[...].T
    own[...] = pair[:cw]
    across[...] = pair[cw:]


def assemble_three_kernel(n, info, *refs):
    pieces, (wd,) = refs[:n], refs[n:]
    rows = wd.shape[0] // n
    for k, piece in enumerate(pieces):
        wd[block(info[4 + k], rows), :] = piece[...]


def mlp_kernel(part, x_ref, norm_ref, c0, c1, c2, c3, w0, w1, w2, w3, wf, r_ref, unit_ref, a2_ref, g_ref, slope_ref):
    def step(i):
        at = block(i)
        resid = x_ref[block(2 * part + i), :].astype(f32) + (
            (dot(c0[at, :], w0[...]) + dot(c1[at, :], w1[...]))
            + (dot(c2[at, :], w2[...]) + dot(c3[at, :], w3[...]))
        )
        r_ref[at, :] = resid
        unit, _ = norm_stats(resid)
        unit_ref[at, :] = unit
        a2 = (unit * norm_ref[2:3] + norm_ref[3:4]).astype(bf16)
        a2_ref[at, :] = a2
        u = dot(a2, wf[...])
        square = u * u
        t = jnp.tanh(GELU_A * u * (1.0 + GELU_B * square))
        g_ref[at, :] = (0.5 * u * (1.0 + t)).astype(bf16)
        slope_ref[at, :] = 0.5 * (1.0 + t) + 0.5 * u * (1.0 - t * t) * (
            GELU_A * (1.0 + 3.0 * GELU_B * square)
        )

    loop(2, step)


def mlp_back_kernel(part, info, e_ref, unit_ref, slope_ref, wf, wd, du_ref, top, bottom, keep, nacc):
    core = info[0]
    nacc[...] = jnp.zeros(nacc.shape, f32)

    def step(i):
        spot = core if i else 1 - core
        at = block(spot)
        du = (dot(e_ref[block(2 * part + spot), :], wd[...]) * slope_ref[at, :]).astype(bf16)
        du_ref[at, :] = du
        grad = dot_nt(du, wf[...])
        nacc[2:3] += jnp.sum(grad * unit_ref[at, :], 0, keepdims=True)
        nacc[3:4] += jnp.sum(grad, 0, keepdims=True)
        keep[...] = grad

        @pl.when(i < 1)
        def _():
            top[...] = grad[: RB // 2].astype(bf16)
            bottom[...] = grad[RB // 2 :].astype(bf16)

    for i in range(2):
        step(i)


def mlp_out_kernel(info, g_ref, wd, ysend, ykeep):
    ykeep[...] = dot_nt(g_ref[block(info[0]), :], wd[...])
    ysend[...] = dot_nt(g_ref[block(1 - info[0]), :], wd[...]).astype(bf16)


def add_kernel(keep, top, bottom, out):
    out[: RB // 2] = (keep[: RB // 2] + top[...].astype(f32)).astype(bf16)
    out[RB // 2 :] = (keep[RB // 2 :] + bottom[...].astype(f32)).astype(bf16)


def starts(info, full, fw, bw):
    rows = fw.shape[0]
    fw[...] = full[block(info[4 + OFFSETS.index(-4)], rows), :].astype(bf16)
    bw[...] = full[block(info[4 + OFFSETS.index(-3)], rows), :].astype(bf16)


def mlp_grad_kernel(info, a2a, a2b, dua, dub, e_ref, ga, gb, out, fw, bw):
    hid = dua.shape[1]
    half = dua.shape[0]

    def step(j):
        at = block(j)
        out[at, :hid] = (dot_tn(a2a[:, at], dua[...]) + dot_tn(a2b[:, at], dub[...])).astype(out.dtype)
        out[at, hid:] = (dot_tn(e_ref[:half, at], ga[...]) + dot_tn(e_ref[half:, at], gb[...])).astype(out.dtype)

    for j in range(out.shape[0] // RB):
        step(j)
    starts(info, out, fw, bw)


def hop_kernel(ahead, behind, info, full, a, b, a_out, b_out):
    rows = a.shape[0]
    for offset, value, out in ((ahead, a, a_out), (behind, b, b_out)):
        term = full[block(info[4 + OFFSETS.index(offset)], rows), :]
        out[...] = (value[...].astype(f32) + term.astype(f32)).astype(bf16)


def hop_last_kernel(info, full, a, a_out):
    term = full[block(info[4 + OFFSETS.index(1)], a.shape[0]), :]
    a_out[...] = (a[...].astype(f32) + term.astype(f32)).astype(bf16)


def norm_back(unit, scale, gain, grad):
    dy = grad * gain
    return scale * (
        dy - jnp.mean(dy, -1, keepdims=True) - unit * jnp.mean(dy * unit, -1, keepdims=True)
    )


def norm_two_kernel(part, info, r_ref, own, received, e_ref, norm_ref, dr_ref, top, bottom):
    unit, scale = norm_stats(r_ref[block(info[0]), :])
    grad = own[...].astype(f32) + received[...].astype(f32)
    e = e_ref[block(2 * part + info[0]), :].astype(f32)
    dr = e + norm_back(unit, scale, norm_ref[2:3], grad)
    dr_ref[...] = dr
    top[...] = dr[: RB // 2].astype(bf16)
    bottom[...] = dr[RB // 2 :].astype(bf16)


def attend_back_kernel(heads, base, blocks, stage, info, src, m_ref, v_ref, *refs):
    if stage < 2:
        halves, refs = refs[:4], refs[4:]
    else:
        ab_in, refs = refs[0], refs[1:]
    wp, lse_ref, c_ref, *refs = refs
    if stage:
        dk_in, dv_in, *refs = refs
    if stage == 0:
        ab_ref, dq_ref, dk_ref, dv_ref = refs
    elif stage == 1:
        ab_ref, dq_ref, dk_ref, dv_ref = refs
    else:
        dq_first, dq_second, dm_ref, dvr_ref = refs
    keep = masked_tile()
    core = info[0]
    if stage < 2:
        for k in range(2):
            ab_ref[block(2 * core + k, RB // 2), :] = halves[k][...]
            ab_ref[block(2 * (1 - core) + k, RB // 2), :] = halves[2 + k][...]
        source, skip = ab_ref, 0
    else:
        source, skip = ab_in, ab_in.shape[0] - blocks * RB
    top = base + blocks * RB
    tiles = top // RB
    dctx = [dot_nt(source[skip + i * RB : skip + (i + 1) * RB], wp[...]).astype(bf16) for i in range(blocks)]
    first = c_ref.shape[0] - blocks * RB if stage == 2 else 0
    own_rows = [slice(first + i * RB, first + (i + 1) * RB) for i in range(blocks)]
    terms = [(d.astype(f32) * c_ref[at].astype(f32)).T for d, at in zip(dctx, own_rows)]
    dq_t = [[None] * heads for _ in range(blocks)]
    dks, dvs = [], []
    for h in range(heads):
        lane = slice(h * HD, (h + 1) * HD)
        keys = m_ref[:top, (3 * h + 1) * HD : (3 * h + 2) * HD]
        keys_t = keys.T
        values = v_ref[h * HD : (h + 1) * HD, :top].T
        dk = [None] * tiles
        dv = [None] * tiles
        if stage:
            for t in range(base // RB):
                dk[t] = dk_in[t * RB : (t + 1) * RB, lane]
                dv[t] = dv_in[t * RB : (t + 1) * RB, lane]
        for i in range(blocks):
            lo = base + i * RB
            hi = lo + RB
            query = m_ref[lo:hi, 3 * h * HD : (3 * h + 1) * HD] * bf16(HD**-0.5)
            dc = dctx[i][:, lane]
            lse = lse_ref[h : h + 1, own_rows[i]]
            prob = jnp.exp(dot_nt(keys[:hi], query) - lse)
            own = jnp.where(keep, prob[lo:], 0.0)
            prob = jnp.concatenate([prob[:lo], own], 0) if lo else own
            dprob = dot_nt(values[:hi], dc)
            inner = jnp.sum(terms[i][lane], 0, keepdims=True)
            more_v = dot(prob.astype(bf16), dc)
            ds = (prob * (dprob - inner)).astype(bf16)
            more_k = dot(ds, query)
            dq_t[i][h] = dot(keys_t[:, :hi], ds) * HD**-0.5
            for t in range(hi // RB):
                spot = slice(t * RB, (t + 1) * RB)
                dv[t] = more_v[spot] if dv[t] is None else dv[t] + more_v[spot]
                dk[t] = more_k[spot] if dk[t] is None else dk[t] + more_k[spot]
        dks.append(dk)
        dvs.append(dv)
    dq = [jnp.concatenate(dq_t[i], 0).T for i in range(blocks)]
    if stage < 2:
        for i in range(blocks):
            dq_ref[i * RB : (i + 1) * RB] = dq[i]
        for t in range(tiles):
            dk_ref[t * RB : (t + 1) * RB] = jnp.concatenate([dks[h][t] for h in range(heads)], 1)
            dv_ref[t * RB : (t + 1) * RB] = jnp.concatenate([dvs[h][t] for h in range(heads)], 1)
        return
    mp = info[2]
    fresh = [jnp.where(src[mp * heads + h] < H, 0.0, 1.0) for h in range(heads)]
    split = dq_first.shape[0]
    for t in range(tiles):
        spot = slice(t * RB, (t + 1) * RB)
        parts = []
        for h in range(heads):
            lane = slice(h * HD, (h + 1) * HD)
            if t * RB < split:
                dqh = dq_first[spot, lane]
            elif t * RB < base:
                dqh = dq_second[t * RB - split : (t + 1) * RB - split, lane]
            else:
                dqh = dq[t - base // RB][:, lane]
            parts += [dqh, dks[h][t], dvs[h][t] * fresh[h]]
            dvr_ref[h * HD : (h + 1) * HD, spot] = dvs[h][t].T.astype(bf16)
        dm_ref[spot, :] = jnp.concatenate(parts, 1).astype(bf16)


def input_kernel(info, dm_ref, w_ref, unit_ref, na, nb, s0, s1, keep, sums):
    core = info[0]
    cols = dm_ref.shape[1]
    gain = jnp.zeros((1, unit_ref.shape[1]), f32)
    shift = gain
    for own in range(2):
        for half, out in enumerate((s0, s1)):
            at = block(2 * half + (core if own else 1 - core))
            grad = dot_nt(dm_ref[at, :], w_ref[:, :cols])
            gain += jnp.sum(grad * unit_ref[at, :], 0, keepdims=True)
            shift += jnp.sum(grad, 0, keepdims=True)
            if own:
                keep[block(half)] = grad
            else:
                out[...] = grad.astype(bf16)
    sums[...] = na[...] + nb[...]
    sums[0:1] = gain
    sums[1:2] = shift


def to_rows_kernel(info, keep, r0, r1, mine, sent):
    low = info[1] == 0
    first = keep[:RB] + r0[...].astype(f32)
    second = keep[RB:] + r1[...].astype(f32)
    mine[...] = jnp.where(low, first, second)
    sent[...] = jnp.where(low, second, first).astype(bf16)


def output_rows_kernel(info, ka, kb, ra, rb, mine, sent):
    low = info[1] == 0
    first = ka[...] + ra[...].astype(f32)
    second = kb[...] + rb[...].astype(f32)
    mine[...] = jnp.where(low, first, second)
    sent[...] = jnp.where(low, second, first).astype(bf16)


def output_kernel(info, ra, rb, mine, received, out):
    at = block(info[0])
    resid = jnp.where(info[1] == 0, ra[at, :], rb[at, :])
    out[...] = (resid + mine[...] + received[...].astype(f32)).astype(bf16)


def qkv_grad_kernel(info, a1_ref, dm_ref, aba, abb, ca, cb, sums, out, fw, bw, turn):
    cols, width = dm_ref.shape[1], sums.shape[1]
    turn[...] = jnp.zeros(turn.shape, f32)
    turn[: sums.shape[0]] = sums[...]

    def step(j):
        at = block(j)
        grad = dot_tn(a1_ref[:, at], dm_ref[...])
        proj = dot_tn(aba[:, at], ca[...]) + dot_tn(abb[:, at], cb[...])
        out[at, : out.shape[1] - LANES] = jnp.concatenate([grad, proj], 1).astype(out.dtype)
        out[at, out.shape[1] - LANES :] = turn[:, at].T.astype(out.dtype)

    for j in range(out.shape[0] // RB):
        step(j)
    starts(info, out, fw, bw)


def norm_one_kernel(info, x_ref, own, received, dra, drb, norm_ref, out):
    unit, scale = norm_stats(x_ref[block(info[2]), :].astype(f32))
    grad = own[...] + received[...].astype(f32)
    dr = jnp.where(info[1] == 0, dra[...], drb[...])
    out[...] = dr + norm_back(unit, scale, norm_ref[0:1], grad)


def first_kernel(heads, info, src, d0, d1, d2, d3, out):
    mp = info[2]
    out[...] = jnp.zeros(out.shape, f32)
    for g in range(heads):
        user = jnp.int32(H)
        for h in range(H):
            user = jnp.where(src[h] == mp * heads + g, h, user)
        held = user // heads
        for r, ref in enumerate((d0, d1, d2, d3)):

            @pl.when((user < H) & (held == mp ^ r))
            def _():
                out[g * HD : (g + 1) * HD, :] = ref[block(user - held * heads, HD), :].astype(f32)


def adamw(master, moment, second, grad, rate, weighted):
    moment_new = 0.9 * moment + 0.1 * grad
    second_new = 0.999 * second + 0.001 * grad * grad
    mean_hat = moment_new / (1.0 - 0.9**ADAM_STEP)
    var_hat = second_new / (1.0 - 0.999**ADAM_STEP)
    master_new = master - rate * (mean_hat / (jnp.sqrt(var_hat) + 1e-08) + weighted * master)
    return (master_new, moment_new, second_new)


def adam_kernel(names, turned, info, full, a, b, *refs):
    ins, outs = refs[:6], refs[6:12]
    rows = a.shape[0]
    grad = a[...].astype(f32) + b[...].astype(f32)
    grad += full[block(info[4], rows), :].astype(f32)
    cols = ins[0].shape[1]
    if turned:
        grad = grad[:, : cols + ins[3].shape[0]]
    second = grad[:, cols:]
    if turned:
        second = jnp.concatenate([second, jnp.zeros((LANES - rows, second.shape[1]), f32)], 0).T[:, :rows]
    for k, (name, part) in enumerate(zip(names, (grad[:, :cols], second))):
        new = adamw(*[r[...] for r in ins[3 * k : 3 * k + 3]], part, RATES[name], 0.1)
        for ref, value in zip(outs[3 * k : 3 * k + 3], new):
            ref[...] = value


def norm_sum_kernel(info, full, a, b, out, turn):
    rows, width = a.shape
    at = slice(width - LANES, width)
    grad = a[:, at].astype(f32) + b[:, at].astype(f32) + full[block(info[4], rows), at].astype(f32)
    turn[...] = jnp.zeros(turn.shape, f32)
    turn[:rows] = grad
    out[...] = turn[...].T[:8]


def norm_adam_kernel(sums, received, w, m, s, w_out, m_out, s_out):
    rows, cols = w.shape
    grad = (sums[...] + received[...])[:rows, :cols]
    new = adamw(w[...], m[...], s[...], grad, RATES["norm"], 0.0)
    for ref, value in zip((w_out, m_out, s_out), new):
        ref[...] = value


def sum_kernel(a, b, out):
    out[...] = a[...] + b[...]


def swap_core(value):
    return lax.ppermute(value, "mp", [(i, i ^ 1) for i in range(4)])


def swap_x(value):
    return lax.ppermute(value, "mp", [(i, i ^ 2) for i in range(4)])


FORWARD = [(RING[i], RING[(i + 1) % 8]) for i in range(8)]
BACKWARD = [(b, a) for a, b in FORWARD]


def ahead(value):
    return lax.ppermute(value, "dp", FORWARD)


def behind(value):
    return lax.ppermute(value, "dp", BACKWARD)


def after(value, *others):
    return lax.optimization_barrier((value,) + others)[0]


class Gather:
    def __init__(self, piece):
        self.ring = lax.axis_size("dp") == len(RING)
        self.start = self.a = self.b = piece
        self.ahead, self.behind = [], []

    def step(self, *gates):
        if not self.ring:
            return
        self.a, self.b = lax.optimization_barrier((self.a, self.b) + gates)[:2]
        self.a = ahead(self.a)
        self.ahead.append(self.a)
        if len(self.behind) < 3:
            self.b = behind(self.b)
            self.behind.append(self.b)

    def pieces(self):
        if not self.ring:
            return [lax.all_gather(self.start, "dp", axis=0, tiled=True)]
        return [self.start] + self.ahead + self.behind


class Scatter:
    def __init__(self, name, info, full, fw, bw):
        self.ring = lax.axis_size("dp") == len(RING)
        self.name, self.info, self.full, self.a, self.b = name, info, full, fw, bw
        self.steps = 0

    def step(self, *gates):
        if not self.ring:
            return
        self.a = after(self.a, *gates)
        k = 4 - self.steps
        shape = (self.a.shape, bf16)
        if k in (3, 2):
            kernel = functools.partial(hop_kernel, k, 1 - k)
            self.a, self.b = call(kernel, f"{self.name}_hop{k}", (self.info,), [self.full, self.a, self.b], [shape] * 2)
        if k == 1:
            (self.a,) = call(hop_last_kernel, f"{self.name}_hop1", (self.info,), [self.full, self.a], [shape])
        self.last = self.a
        self.a = ahead(self.a)
        if k > 1:
            self.b = behind(self.b)
        self.steps += 1

    def ends(self):
        return (self.a, self.b) if self.ring else None


def update(name, info, full, ends, firsts, seconds, turned):
    first, second = name
    outs = [(w.shape, f32) for w in firsts + seconds]
    if ends is not None:
        new = call(
            functools.partial(adam_kernel, name, turned),
            f"adam_{first}",
            (info,),
            [full, *ends, *firsts, *seconds],
            outs,
        )
        return tuple(new[:3]), tuple(new[3:])
    grad = lax.psum_scatter(full.astype(f32), "dp", scatter_dimension=0, tiled=True)
    cols = firsts[0].shape[1]
    other = grad[:, cols : cols + seconds[0].shape[0 if turned else 1]]
    return (
        adamw(*firsts, grad[:, :cols], RATES[first], 0.1),
        adamw(*seconds, other.T if turned else other, RATES[second], 0.1),
    )


def local(
    tokens_in,
    first_values,
    skip_source,
    grad_out,
    qkv_weight,
    proj_weight,
    fc_weight,
    down_weight,
    norm_params,
    qkv_moment,
    proj_moment,
    fc_moment,
    down_moment,
    norm_moment,
    qkv_second,
    proj_second,
    fc_second,
    down_second,
    norm_second,
):
    n = lax.axis_size("dp")
    ring = n == len(RING)
    pieces = n if ring else 1
    count, width = tokens_in.shape
    cols = qkv_weight.shape[1]
    heads = cols // (3 * HD)
    cw = heads * HD
    hid = fc_weight.shape[1]
    wide = -(-(cols + 4) // LANES) * LANES
    half = count // 2
    shard = qkv_weight.shape[0]
    info = HERE
    src = skip_source

    if ring:
        (ring_one,) = call(
            prep_one_kernel,
            "prep_one",
            (),
            [qkv_weight, norm_params],
            [((shard, wide), bf16)],
            scratch=[
                pltpu.VMEM((shard, cols), f32),
                pltpu.VMEM(norm_params.shape, f32),
                pltpu.VMEM((LANES, LANES), f32),
                pltpu.SemaphoreType.DMA((2,)),
            ],
            vmem=60,
            far=True,
        )
        proj_t, fc_low, down_t = call(
            prep_two_kernel,
            "prep_two",
            (),
            [after(proj_weight, ring_one), fc_weight, down_weight.T],
            [((shard, cw), bf16), ((shard, hid), bf16), ((shard, hid), bf16)],
            scratch=[
                pltpu.VMEM((cw, shard), f32),
                pltpu.VMEM((shard, hid), f32),
                pltpu.VMEM((shard, hid), f32),
                pltpu.VMEM((cw, LANES), f32),
                pltpu.SemaphoreType.DMA((3,)),
            ],
            vmem=56,
            far=True,
        )
    else:
        blank = jnp.zeros((shard, wide - cols - 4), bf16)
        ring_one = jnp.concatenate([qkv_weight.astype(bf16), norm_params.T.astype(bf16), blank], 1)
        proj_t, fc_low, down_t = proj_weight.T.astype(bf16), fc_weight.astype(bf16), down_weight.T.astype(bf16)
    fence = lambda *values: lax.optimization_barrier(values)
    fence = lambda *values: lax.optimization_barrier(values)
    one = Gather(ring_one)
    one.step()
    one.a, one.b, proj_t, tokens = fence(one.a, one.b, proj_t, tokens_in)
    one.step()
    proj_x = swap_x(proj_t)
    (unit_one,) = call(unit_kernel, "unit", (), [tokens], [((count, width), f32)])
    one.a, one.b, proj_x, unit_one = fence(one.a, one.b, proj_x, unit_one)
    one.step()
    if ring:
        (ring_two,) = call(
            join_kernel, "join", (), [fc_low, proj_t, proj_x], [((shard, hid + 2 * cw), bf16)]
        )
    else:
        ring_two = jnp.concatenate([fc_low, proj_t, proj_x], 1)
    two, three = Gather(ring_two), Gather(down_t)
    two.step()
    first_t = after(first_values.T, unit_one)
    first_x, first_c = swap_x(first_t), swap_core(first_t)
    one.a, one.b = fence(one.a, one.b)
    one.step()
    one.a, two.a, two.b, unit_one, first_x, three.a = fence(one.a, two.a, two.b, unit_one, first_x, three.a)
    if ring:
        one.ahead[-1] = one.a
    first_xc = swap_core(first_x)
    two.step()
    three.step()

    a1, mixed, fresh, qkv_full, norms = call(
        functools.partial(qkv_kernel, pieces, heads),
        "qkv",
        (info,),
        [unit_one, *one.pieces()],
        [
            ((count, width), bf16),
            ((count, cols), bf16),
            ((cw, count), bf16),
            ((width, wide), bf16),
            ((8, width), f32),
        ],
    )
    (values,) = call(
        functools.partial(values_kernel, heads),
        "values",
        (info, src),
        [fresh, first_t, first_c, first_x, first_xc],
        [((cw, count), bf16)],
    )

    def attend(part, mixed):
        return call(
            functools.partial(attend_kernel, heads, part * half),
            f"attend{part}",
            (),
            [mixed, values],
            [((half, cw), bf16), ((8, half), f32)],
            scratch=[
                pltpu.VMEM((heads, (part + 1) * half, HD), bf16),
                pltpu.VMEM((heads, half, HD), bf16),
                pltpu.VMEM((cw, half), f32),
            ],
        )

    ctx_a, lse_a = attend(0, mixed)
    two.a, two.b, three.a, three.b, ctx_a = fence(two.a, two.b, three.a, three.b, ctx_a)
    two.step()
    three.step()
    xa = swap_x(ctx_a)
    ctx_b, lse_b = attend(1, after(mixed, ctx_a))
    two.a, two.b, three.a, three.b, xa, ctx_b = fence(two.a, two.b, three.a, three.b, xa, ctx_b)
    two.step()
    three.step()
    xb = swap_x(ctx_b)
    (grad_out,) = call(
        fetch_kernel,
        "fetch",
        (),
        [after(grad_out, ctx_b)],
        [(grad_out.shape, bf16)],
        scratch=[pltpu.SemaphoreType.DMA],
        vmem=4,
        far=True,
    )
    start, xb, two_last, three.a, three.b, grad_out = fence(two.start, xb, two.a, three.a, three.b, grad_out)
    ca, xca, cb, xcb = swap_core(ctx_a), swap_core(xa), swap_core(ctx_b), swap_core(xb)
    three.step()
    context, lse = (ctx_a, ctx_b), (lse_a, lse_b)
    wf, own_w, across_w = call(
        functools.partial(assemble_two_kernel, pieces),
        "assemble_two",
        (info,),
        [start, *two.pieces()[1:]] if ring else two.pieces(),
        [((width, hid), bf16), ((cw, width), bf16), ((cw, width), bf16)],
        scratch=[pltpu.VMEM((width, 2 * cw), bf16)],
    )
    pair = own_w, swap_core(own_w), across_w, swap_core(across_w)

    def mlp(part, norms, contexts):
        return call(
            functools.partial(mlp_kernel, part),
            f"mlp{part}",
            (),
            [tokens, norms, *contexts, *pair, wf],
            [
                ((half, width), f32),
                ((half, width), f32),
                ((half, width), bf16),
                ((half, hid), bf16),
                ((half, hid), f32),
            ],
        )

    def mlp_back(part, grad):
        return call(
            functools.partial(mlp_back_kernel, part),
            f"mlp_back{part}",
            (info,),
            [grad, unit_two[part], slope[part], wf, wd],
            [((half, hid), bf16)] + [((RB // 2, width), bf16)] * 2 + [((RB, width), f32), ((8, width), f32)],
        )

    def mlp_out(part, gate):
        return call(
            mlp_out_kernel,
            f"mlp_out{part}",
            (info,),
            [after(act[part], gate), wd],
            [((RB, width), bf16), ((RB, width), f32)],
        )

    def add(part, keep, *received):
        return call(add_kernel, f"add{part}", (), [keep, *received], [((RB, width), bf16)])[0]

    forward_a = mlp(0, norms, (ctx_a, ca, xa, xca))
    forward_b = mlp(1, after(norms, forward_a[0]), (ctx_b, cb, xb, xcb))
    resid, unit_two, a2, act, slope = zip(forward_a, forward_b)
    start, last = fence(three.start, act[1])
    (wd,) = call(
        functools.partial(assemble_three_kernel, pieces),
        "assemble_three",
        (info,),
        [start, *three.pieces()[1:]] if ring else three.pieces(),
        [((width, hid), bf16)],
    )
    dpre_a, top_a, bottom_a, dkeep_a, nacc_a = mlp_back(0, after(grad_out, act[1]))
    received_a = swap_core(top_a), swap_core(bottom_a)
    dpre_b, top_b, bottom_b, dkeep_b, nacc_b = mlp_back(1, after(grad_out, dpre_a))
    mine_a = add(0, after(dkeep_a, dpre_b), *received_a)
    received_b = swap_core(top_b), swap_core(bottom_b)
    across_a = swap_x(mine_a)

    piece = lambda w: [((width // pieces if ring else 16, w), bf16)] * 2
    mlp_grad, mlp_fw, mlp_bw = call(
        mlp_grad_kernel,
        "mlp_grad",
        (info,),
        [after(a2[0], mine_a), a2[1], dpre_a, dpre_b, grad_out, act[0], act[1]],
        [((width, 2 * hid), bf16 if ring else f32)] + piece(2 * hid),
    )
    mlp_sum = Scatter("mlp", info, mlp_grad, mlp_fw, mlp_bw)
    mlp_sum.step()
    mine_b = add(1, after(dkeep_b, mlp_grad), *received_b)
    across_b = swap_x(mine_b)
    def norm_two(part, mine, across):
        return call(
            functools.partial(norm_two_kernel, part),
            f"norm_two{part}",
            (info,),
            [resid[part], mine, across, grad_out, norms],
            [((RB, width), f32)] + [((RB // 2, width), bf16)] * 2,
        )

    def attend_back(stage, base, blocks, given, part, before, outs):
        return call(
            functools.partial(attend_back_kernel, heads, base, blocks, stage),
            f"attend_back{stage}",
            (info, src),
            [mixed, values, *given, own_w, lse[part], context[part], *before],
            outs,
            vmem=24,
        )

    dr_a, *ab_a = norm_two(0, after(mine_a, mine_b), across_a)
    partner = [swap_core(v) for v in ab_a]
    ab_one, dq_a, dk, dv = attend_back(
        0, 0, 2, [*ab_a, *partner], 0, [], [((half, width), bf16)] + [((half, cw), f32)] * 3
    )
    mlp_sum.a, mlp_sum.b, dq_a = fence(mlp_sum.a, mlp_sum.b, dq_a)
    mlp_sum.step()
    ysend_a, ykeep_a = mlp_out(0, dq_a)
    ysend_b, ykeep_b = mlp_out(1, ysend_a)
    yreceived_a, yreceived_b = swap_core(ysend_a), swap_core(ysend_b)
    rows_mine, rows_sent = call(
        output_rows_kernel,
        "output_rows",
        (info,),
        [ykeep_a, ykeep_b, yreceived_a, yreceived_b],
        [((RB, width), f32), ((RB, width), bf16)],
    )
    dr_b, *ab_b = norm_two(1, after(mine_b, ysend_b), across_b)
    partner = [swap_core(v) for v in ab_b]
    rows_received = swap_x(after(rows_sent, dr_b))
    top = half + RB
    ab_two, dq_b, dk, dv = attend_back(
        1, half, 1, [*ab_b, *partner], 1, [dk, dv], [((half, width), bf16), ((RB, cw), f32)] + [((top, cw), f32)] * 2
    )
    mlp_sum.a, mlp_sum.b, dq_b = fence(mlp_sum.a, mlp_sum.b, dq_b)
    mlp_sum.step()
    dmixed, dreused = attend_back(
        2,
        top,
        1,
        [ab_two],
        1,
        [after(dk, mlp_sum.last) if ring else dk, dv, dq_a, dq_b],
        [((count, cols), bf16), ((cw, count), bf16)],
    )

    *isend, ikeep, sums = call(
        input_kernel,
        "input",
        (info,),
        [dmixed, qkv_full, unit_one, nacc_a, nacc_b],
        [((RB, width), bf16)] * 2 + [((half, width), f32), ((8, width), f32)],
    )
    qkv_grad, qkv_fw, qkv_bw = call(
        qkv_grad_kernel,
        "qkv_grad",
        (info,),
        [a1, dmixed, ab_one, ab_two, context[0], context[1], sums],
        [((width, cols + cw + LANES), bf16 if ring else f32)] + piece(cols + cw + LANES),
        scratch=[pltpu.VMEM((LANES, width), f32)],
    )
    qkv_sum = Scatter("qkv", info, qkv_grad, qkv_fw, qkv_bw)
    mlp_sum.a, mlp_sum.b, qkv_sum.a, qkv_sum.b, rows_received = fence(
        mlp_sum.a, mlp_sum.b, qkv_sum.a, qkv_sum.b, rows_received
    )
    mlp_sum.step()
    qkv_sum.step()
    gathered = [swap_core(v) for v in isend]
    mine, sent = call(
        to_rows_kernel, "to_rows", (info,), [ikeep, *gathered], [((RB, width), f32), ((RB, width), bf16)]
    )
    across, dx = swap_x(sent), swap_x(dreused)
    qkv_sum.a, qkv_sum.b, sent = fence(qkv_sum.a, qkv_sum.b, sent)
    qkv_sum.step()
    (block_out,) = call(
        output_kernel,
        "output",
        (info,),
        [resid[0], resid[1], rows_mine, rows_received],
        [((RB, width), bf16)],
    )
    qkv_sum.a, qkv_sum.b, mlp_sum.a, block_out = fence(qkv_sum.a, qkv_sum.b, mlp_sum.a, block_out)
    qkv_sum.step()
    fc_new, down_new = update(
        ("fc", "down"),
        info,
        mlp_grad,
        mlp_sum.ends(),
        [fc_weight, fc_moment, fc_second],
        [down_weight.T, down_moment.T, down_second.T],
        False,
    )
    qkv_sum.a, qkv_sum.b, across, dx, *fc_new = fence(qkv_sum.a, qkv_sum.b, across, dx, *fc_new)
    down_new = tuple(v.T for v in down_new)
    qkv_sum.step()
    (input_grad,) = call(
        norm_one_kernel,
        "norm_one",
        (info,),
        [tokens, mine, across, dr_a, dr_b, norms],
        [((RB, width), f32)],
    )
    dx, dreused = fence(dx, dreused)
    dc, dxc = swap_core(dreused), swap_core(dx)
    (first_grad,) = call(
        functools.partial(first_kernel, heads),
        "first",
        (info, src),
        [dreused, dc, dx, dxc],
        [((cw, count), f32)],
    )
    qkv_sum.a, input_grad, first_grad = fence(qkv_sum.a, input_grad, first_grad)
    if ring:
        (sums,) = call(
            norm_sum_kernel,
            "norm_sum",
            (info,),
            [qkv_grad, *qkv_sum.ends()],
            [((8, LANES), f32)],
            scratch=[pltpu.VMEM((LANES, LANES), f32)],
        )
        (sums,) = call(sum_kernel, "sum", (), [sums, swap_core(sums)], [(sums.shape, f32)])
        received = swap_x(sums)
    qkv_new, proj_new = update(
        ("qkv", "proj"),
        info,
        qkv_grad,
        qkv_sum.ends(),
        [qkv_weight, qkv_moment, qkv_second],
        [proj_weight, proj_moment, proj_second],
        True,
    )
    if ring:
        norm_new = call(
            norm_adam_kernel,
            "adam_norm",
            (),
            [sums, received, norm_params, norm_moment, norm_second],
            [(norm_params.shape, f32)] * 3,
        )
    else:
        own = lax.psum_scatter(lax.psum(sums, "mp"), "dp", scatter_dimension=1, tiled=True)[:4]
        norm_new = adamw(norm_params, norm_moment, norm_second, own, RATES["norm"], 0.0)
    return (block_out, input_grad, first_grad.T, *qkv_new, *proj_new, *fc_new, *down_new, *norm_new)


def solution(mesh):
    both = P("dp", "mp")
    turned = P("mp", "dp")
    rows = P("dp", None)
    every = P(None, "dp")
    state = (both, turned, both, turned, every)
    return jax.shard_map(
        local,
        mesh=mesh,
        in_specs=(rows, both, P(), rows) + state * 3,
        out_specs=(P(("dp", "mp"), None), P(("dp", "mp"), None), both)
        + (both,) * 3
        + (turned,) * 3
        + (both,) * 3
        + (turned,) * 3
        + (every,) * 3,
        check_vma=False,
    )
```

profile of v0, /device:TPU:0, one launch (start us, length us, event | category | flops | bytes accessed | tf_op | source)
XLA Modules:
  0.0 149.5 jit_solution(4892653821454735701)
XLA Ops:
  0.7 1.8 %prep_one.1.refs_1_ = bf16[96,640]{1,0:T(8,128)(2,1)} custom-call(f32[96,576]{1,0:T(8,128)} %refs_3_.3, f32[4,96]{1,0:T(4,128)} %w.1), custom_call_target="tpu_custom_call" | custom-call | flops 1 | bytes 1 | tf_op jit(solution)/shard_map/prep_one/pallas_call | solution.py:65
  2.4 3.1 %collective-permute-start = (bf16[96,640]{1,0:T(8,128)(2,1)}, bf16[96,640]{1,0:T(8,128)(2,1)S(1)}, u32[]{:S(2)}, u32[]{:S(2)}) collective-permute-start(bf16[96,640]{1,0:T(8,128)(2,1)} %prep_one.1.refs_1_), channel_id=1, source_target_pairs={{0,8},{8,16},{16,24},{24,28},{28,20},{20,12},{12,4},{4,0},{1,9},{9... | collective-permute-start | bytes 368648 | tf_op jit(solution)/shard_map/ppermute | solution.py:579
  5.5 1.9 %prep_two.1 = (bf16[96,192]{1,0:T(8,128)(2,1)}, bf16[96,768]{1,0:T(8,128)(2,1)}, bf16[96,768]{1,0:T(8,128)(2,1)}) custom-call(f32[192,96]{1,0:T(8,128)} %refs_6_.1, f32[96,768]{1,0:T(8,128)} %refs_3_.2, f32[96,768]{1,0:T(8,128)} %bitcast.8), custom_call_target="tpu_custom_call" | custom-call | flops 1 | bytes 1 | tf_op jit(solution)/shard_map/prep_two/pallas_call | solution.py:65
  7.4 1.6 %collective-permute-done.refs_2_ = bf16[96,640]{1,0:T(8,128)(2,1)S(1)} collective-permute-done((bf16[96,640]{1,0:T(8,128)(2,1)}, bf16[96,640]{1,0:T(8,128)(2,1)S(1)}, u32[]{:S(2)}, u32[]{:S(2)}) %collective-permute-start) | collective-permute-done | bytes 122912 | tf_op jit(solution)/shard_map/ppermute | solution.py:579
  9.0 1.6 %collective-permute-done.1.refs_6_ = bf16[96,640]{1,0:T(8,128)(2,1)S(1)} collective-permute-done((bf16[96,640]{1,0:T(8,128)(2,1)}, bf16[96,640]{1,0:T(8,128)(2,1)S(1)}, u32[]{:S(2)}, u32[]{:S(2)}) %collective-permute-start.1) | collective-permute-done | bytes 122912 | tf_op jit(solution)/shard_map/ppermute | solution.py:583
  10.6 1.6 %collective-permute-start.2 = (bf16[96,640]{1,0:T(8,128)(2,1)S(1)}, bf16[96,640]{1,0:T(8,128)(2,1)S(1)}, u32[]{:S(2)}, u32[]{:S(2)}) collective-permute-start(bf16[96,640]{1,0:T(8,128)(2,1)S(1)} %collective-permute-done.refs_2_), channel_id=1, source_target_pairs={{0,8},{8,16},{16,24},{24,28},{28,20},{20,12},{12,4},{4,0},{1,9},{9... | collective-permute-start | bytes 368648 | tf_op jit(solution)/shard_map/ppermute | solution.py:579
  12.6 1.5 collective-permute-start.4
  14.1 1.4 copy-done
  17.1 1.5 collective-permute-start.10
  18.6 1.6 %collective-permute-start.5 = (bf16[96,640]{1,0:T(8,128)(2,1)S(1)}, bf16[96,640]{1,0:T(8,128)(2,1)S(1)}, u32[]{:S(2)}, u32[]{:S(2)}) collective-permute-start(bf16[96,640]{1,0:T(8,128)(2,1)S(1)} %collective-permute-done.2.refs_3_), channel_id=1, source_target_pairs={{0,8},{8,16},{16,24},{24,28},{28,20},{20,12},{12,4},{4,0},{1,9},{9... | collective-permute-start | bytes 368648 | tf_op jit(solution)/shard_map/ppermute | solution.py:579
  20.7 1.6 %collective-permute-start.8 = (bf16[96,1152]{1,0:T(8,128)(2,1)S(1)}, bf16[96,1152]{1,0:T(8,128)(2,1)S(1)}, u32[]{:S(2)}, u32[]{:S(2)}) collective-permute-start(bf16[96,1152]{1,0:T(8,128)(2,1)S(1)} %join.1.refs_0_), channel_id=1, source_target_pairs={{0,8},{8,16},{16,24},{24,28},{28,20},{20,12},{12,4},{4,0},{1,9},{9... | collective-permute-start | bytes 663560 | tf_op jit(solution)/shard_map/ppermute | solution.py:579
  22.8 1.0 collective-permute-done.5.refs_4_
  23.7 1.3 collective-permute-done.6.refs_8_
  25.0 1.5 %collective-permute-start.7 = (bf16[96,640]{1,0:T(8,128)(2,1)S(1)}, bf16[96,640]{1,0:T(8,128)(2,1)S(1)}, u32[]{:S(2)}, u32[]{:S(2)}) collective-permute-start(bf16[96,640]{1,0:T(8,128)(2,1)S(1)} %collective-permute-done.5.refs_4_), channel_id=1, source_target_pairs={{0,8},{8,16},{16,24},{24,28},{28,20},{20,12},{12,4},{4,0},{1,9},{9... | collective-permute-start | bytes 368648 | tf_op jit(solution)/shard_map/ppermute | solution.py:579
  26.7 1.6 %collective-permute-done.9.refs_5_ = bf16[96,1152]{1,0:T(8,128)(2,1)S(1)} collective-permute-done((bf16[96,1152]{1,0:T(8,128)(2,1)S(1)}, bf16[96,1152]{1,0:T(8,128)(2,1)S(1)}, u32[]{:S(2)}, u32[]{:S(2)}) %collective-permute-start.9) | collective-permute-done | bytes 221216 | tf_op jit(solution)/shard_map/ppermute | solution.py:583
  28.2 1.7 %collective-permute-done.7.refs_5_ = bf16[96,640]{1,0:T(8,128)(2,1)S(1)} collective-permute-done((bf16[96,640]{1,0:T(8,128)(2,1)S(1)}, bf16[96,640]{1,0:T(8,128)(2,1)S(1)}, u32[]{:S(2)}, u32[]{:S(2)}) %collective-permute-start.7) | collective-permute-done | bytes 122912 | tf_op jit(solution)/shard_map/ppermute | solution.py:579
  29.9 1.6 %collective-permute-start.13 = (bf16[96,1152]{1,0:T(8,128)(2,1)S(1)}, bf16[96,1152]{1,0:T(8,128)(2,1)S(1)}, u32[]{:S(2)}, u32[]{:S(2)}) collective-permute-start(bf16[96,1152]{1,0:T(8,128)(2,1)S(1)} %collective-permute-done.8.refs_1_), channel_id=1, source_target_pairs={{0,8},{8,16},{16,24},{24,28},{28,20},{20,12},{12,4},{4,0},{1,9},{9... | collective-permute-start | bytes 663560 | tf_op jit(solution)/shard_map/ppermute | solution.py:579
  32.0 1.5 %collective-permute-start.15 = (bf16[96,768]{1,0:T(8,128)(2,1)S(1)}, bf16[96,768]{1,0:T(8,128)(2,1)S(1)}, u32[]{:S(2)}, u32[]{:S(2)}) collective-permute-start(bf16[96,768]{1,0:T(8,128)(2,1)S(1)} %copy-done.15), channel_id=1, source_target_pairs={{0,8},{8,16},{16,24},{24,28},{28,20},{20,12},{12,4},{4,0},{1,9},{9... | collective-permute-start | bytes 442376 | tf_op jit(solution)/shard_map/ppermute | solution.py:579
  34.0 2.4 %qkv.1 = (bf16[1024,768]{1,0:T(8,128)(2,1)S(1)}, bf16[1024,576]{1,0:T(8,128)(2,1)S(1)}, bf16[192,1024]{1,0:T(8,128)(2,1)S(1)}, bf16[768,640]{1,0:T(8,128)(2,1)S(1)}, f32[8,768]{1,0:T(8,128)S(1)}) custom-call(f32[1024,768]{1,0:T(8,128)S(1)} %unit.1.refs_0_.refs_2_, bf16[96,640]{1,0:T(8,128)(2,1)S(1)} %copy-done.6, ...), custom_call_target="tpu_custom_call" | custom-call | flops 1 | bytes 1 | tf_op jit(solution)/shard_map/qkv/pallas_call | solution.py:65
  37.2 2.9 %attend0.1 = (bf16[512,192]{1,0:T(8,128)(2,1)S(1)}, f32[8,512]{1,0:T(8,128)S(1)}) custom-call(bf16[1024,576]{1,0:T(8,128)(2,1)S(1)} %get-tuple-element.250.m_ref.refs_1_, bf16[192,1024]{1,0:T(8,128)(2,1)S(1)} %values.1.v_ref.refs_2_), custom_call_target="tpu_custom_call" | custom-call | flops 1 | bytes 1 | tf_op jit(solution)/shard_map/attend0/pallas_call | solution.py:65
  40.9 1.3 collective-permute-done.16.refs_5_
  42.3 1.7 %collective-permute-start.18 = (bf16[96,1152]{1,0:T(8,128)(2,1)S(1)}, bf16[96,1152]{1,0:T(8,128)(2,1)S(1)}, u32[]{:S(2)}, u32[]{:S(2)}) collective-permute-start(bf16[96,1152]{1,0:T(8,128)(2,1)S(1)} %collective-permute-done.13.refs_2_), channel_id=1, source_target_pairs={{0,8},{8,16},{16,24},{24,28},{28,20},{20,12},{12,4},{4,0},{1,9},{9... | collective-permute-start | bytes 663560 | tf_op jit(solution)/shard_map/ppermute | solution.py:579
  44.7 1.5 %collective-permute-start.20 = (bf16[96,768]{1,0:T(8,128)(2,1)S(1)}, bf16[96,768]{1,0:T(8,128)(2,1)S(1)}, u32[]{:S(2)}, u32[]{:S(2)}) collective-permute-start(bf16[96,768]{1,0:T(8,128)(2,1)S(1)} %collective-permute-done.15.refs_1_), channel_id=1, source_target_pairs={{0,8},{8,16},{16,24},{24,28},{28,20},{20,12},{12,4},{4,0},{1,9},{9... | collective-permute-start | bytes 442376 | tf_op jit(solution)/shard_map/ppermute | solution.py:579
  46.8 4.9 %attend1.1 = (bf16[512,192]{1,0:T(8,128)(2,1)S(1)}, f32[8,512]{1,0:T(8,128)S(1)}) custom-call(bf16[1024,576]{1,0:T(8,128)(2,1)S(1)} %get-tuple-element.250.m_ref.refs_1_, bf16[192,1024]{1,0:T(8,128)(2,1)S(1)} %values.1.v_ref.refs_2_), custom_call_target="tpu_custom_call" | custom-call | flops 1 | bytes 1 | tf_op jit(solution)/shard_map/attend1/pallas_call | solution.py:65
  52.2 1.4 collective-permute-done.21.refs_6_
  53.6 1.0 collective-permute-start.25
  55.1 1.0 collective-permute-start.26
  56.1 1.0 collective-permute-start.27
  57.2 5.1 %collective-permute-done.26.refs_3_ = bf16[96,768]{1,0:T(8,128)(2,1)S(1)} collective-permute-done((bf16[96,768]{1,0:T(8,128)(2,1)S(1)}, bf16[96,768]{1,0:T(8,128)(2,1)S(1)}, u32[]{:S(2)}, u32[]{:S(2)}) %collective-permute-start.26) | collective-permute-done | bytes 147488 | tf_op jit(solution)/shard_map/ppermute | solution.py:579
  64.0 1.1 collective-permute-start.32
  65.2 3.4 %mlp0.1 = (f32[512,768]{1,0:T(8,128)S(1)}, f32[512,768]{1,0:T(8,128)S(1)}, bf16[512,768]{1,0:T(8,128)(2,1)S(1)}, bf16[512,768]{1,0:T(8,128)(2,1)S(1)}, f32[512,768]{1,0:T(8,128)S(1)}) custom-call(bf16[1024,768]{1,0:T(8,128)(2,1)S(1)} %copy-done.1, f32[8,768]{1,0:T(8,128)S(1)} %get-tuple-element.265.norm_ref.refs_4_.refs_5_, ...), custom_call_target="tpu_custom_call" | custom-call | flops 1 | bytes 1 | tf_op jit(solution)/shard_map/mlp0/pallas_call | solution.py:65
  68.6 3.4 %mlp1.1 = (f32[512,768]{1,0:T(8,128)S(1)}, f32[512,768]{1,0:T(8,128)S(1)}, bf16[512,768]{1,0:T(8,128)(2,1)S(1)}, bf16[512,768]{1,0:T(8,128)(2,1)S(1)}, f32[512,768]{1,0:T(8,128)S(1)}) custom-call(bf16[1024,768]{1,0:T(8,128)(2,1)S(1)} %copy-done.1, f32[8,768]{1,0:T(8,128)S(1)} %get-tuple-element.265.norm_ref.refs_4_.refs_5_, ...), custom_call_target="tpu_custom_call" | custom-call | flops 1 | bytes 1 | tf_op jit(solution)/shard_map/mlp1/pallas_call | solution.py:65
  72.1 1.6 %mlp_back0.1 = (bf16[512,768]{1,0:T(8,128)(2,1)S(1)}, bf16[128,768]{1,0:T(8,128)(2,1)S(1)}, bf16[128,768]{1,0:T(8,128)(2,1)S(1)}, f32[256,768]{1,0:T(8,128)S(1)}, f32[8,768]{1,0:T(8,128)S(1)}) custom-call(bf16[1024,768]{1,0:T(8,128)(2,1)S(1)} %fetch.1.refs_0_.refs_4_.refs_3_, f32[512,768]{1,0:T(8,128)S(1)} %get-tuple-element.271.refs_1_, ...), custom_call_target="tpu_custom_call" | custom-call | flops 1 | bytes 1 | tf_op jit(solution)/shard_map/mlp_back0/pallas_call | solution.py:65
  74.2 1.5 %mlp_back1.1 = (bf16[512,768]{1,0:T(8,128)(2,1)S(1)}, bf16[128,768]{1,0:T(8,128)(2,1)S(1)}, bf16[128,768]{1,0:T(8,128)(2,1)S(1)}, f32[256,768]{1,0:T(8,128)S(1)}, f32[8,768]{1,0:T(8,128)S(1)}) custom-call(bf16[1024,768]{1,0:T(8,128)(2,1)S(1)} %fetch.1.refs_0_.refs_4_.refs_3_, f32[512,768]{1,0:T(8,128)S(1)} %get-tuple-element.277.refs_1_, ...), custom_call_target="tpu_custom_call" | custom-call | flops 1 | bytes 1 | tf_op jit(solution)/shard_map/mlp_back1/pallas_call | solution.py:65
  76.9 2.7 %mlp_grad.1 = (bf16[768,1536]{1,0:T(8,128)(2,1)S(1)}, bf16[96,1536]{1,0:T(8,128)(2,1)S(1)}, bf16[96,1536]{1,0:T(8,128)(2,1)S(1)}) custom-call(bf16[512,768]{1,0:T(8,128)(2,1)S(1)} %get-tuple-element.286.refs_0_, bf16[512,768]{1,0:T(8,128)(2,1)S(1)} %get-tuple-element.287.refs_1_, bf16[512,768]{1,0:T(8,128)(2,1)S(1)} %get-tuple-element.275.refs_2_, ...), custom_call_target="tpu_custom_call" | custom-call | flops 1 | bytes 1 | tf_op jit(solution)/shard_map/mlp_grad/pallas_call | solution.py:65
  79.6 0.9 collective-permute-start.37
  80.6 1.2 collective-permute-start.38
  81.8 5.4 %collective-permute-done.39.refs_2_ = bf16[256,768]{1,0:T(8,128)(2,1)S(1)} collective-permute-done((bf16[256,768]{1,0:T(8,128)(2,1)S(1)}, bf16[256,768]{1,0:T(8,128)(2,1)S(1)}, u32[]{:S(2)}, u32[]{:S(2)}) %collective-permute-start.39) | collective-permute-done | bytes 393248 | tf_op jit(solution)/shard_map/ppermute | solution.py:571
  89.6 2.9 %attend_back0.1 = (bf16[512,768]{1,0:T(8,128)(2,1)S(1)}, f32[512,192]{1,0:T(8,128)S(1)}, f32[512,192]{1,0:T(8,128)S(1)}, f32[512,192]{1,0:T(8,128)S(1)}) custom-call(s32[12]{0:T(128)S(1)} %copy-done.20, bf16[1024,576]{1,0:T(8,128)(2,1)S(1)} %get-tuple-element.250.m_ref.refs_1_, bf16[192,1024]{1,0:T(8,128)(2,1)S(1)} %values.1.v_ref.refs_2_, ...), custom_call_target="tpu_custom_call" | custom-call | flops 1 | bytes 1 | tf_op jit(solution)/shard_map/attend_back0/pallas_call | solution.py:65
  94.8 1.0 collective-permute-start.45
  95.9 1.1 collective-permute-start.46
  96.9 2.5 %collective-permute-done.42.refs_2_ = bf16[256,768]{1,0:T(8,128)(2,1)S(1)} collective-permute-done((bf16[256,768]{1,0:T(8,128)(2,1)S(1)}, bf16[256,768]{1,0:T(8,128)(2,1)S(1)}, u32[]{:S(2)}, u32[]{:S(2)}) %collective-permute-start.42) | collective-permute-done | bytes 393248 | tf_op jit(solution)/shard_map/ppermute | solution.py:571
  101.8 2.5 %attend_back1.1 = (bf16[512,768]{1,0:T(8,128)(2,1)S(1)}, f32[256,192]{1,0:T(8,128)S(1)}, f32[768,192]{1,0:T(8,128)S(1)}, f32[768,192]{1,0:T(8,128)S(1)}) custom-call(s32[12]{0:T(128)S(1)} %copy-done.20, bf16[1024,576]{1,0:T(8,128)(2,1)S(1)} %get-tuple-element.250.m_ref.refs_1_, bf16[192,1024]{1,0:T(8,128)(2,1)S(1)} %values.1.v_ref.refs_2_, ...), custom_call_target="tpu_custom_call" | custom-call | flops 1 | bytes 1 | tf_op jit(solution)/shard_map/attend_back1/pallas_call | solution.py:65
  104.9 1.1 collective-permute-start.48
  106.0 1.0 collective-permute-start.47
  107.0 3.1 %attend_back2.1 = (bf16[1024,576]{1,0:T(8,128)(2,1)S(1)}, bf16[192,1024]{1,0:T(8,128)(2,1)S(1)}) custom-call(s32[12]{0:T(128)S(1)} %copy-done.20, bf16[1024,576]{1,0:T(8,128)(2,1)S(1)} %get-tuple-element.250.m_ref.refs_1_, bf16[192,1024]{1,0:T(8,128)(2,1)S(1)} %values.1.v_ref.refs_2_, bf16[512,768]{1,0:T(8,128)(2,1)S(1)} %get-tuple-element.311.refs_3_, ...), custom_call_target="tpu_custom_call" | custom-call | flops 1 | bytes 1 | tf_op jit(solution)/shard_map/attend_back2/pallas_call | solution.py:65
  110.1 1.4 input.1
  112.1 2.1 %qkv_grad.1 = (bf16[768,896]{1,0:T(8,128)(2,1)S(1)}, bf16[96,896]{1,0:T(8,128)(2,1)S(1)}, bf16[96,896]{1,0:T(8,128)(2,1)S(1)}) custom-call(bf16[1024,768]{1,0:T(8,128)(2,1)S(1)} %get-tuple-element.228.refs_0_, bf16[1024,576]{1,0:T(8,128)(2,1)S(1)} %get-tuple-element.324.refs_0_.refs_1_, bf16[512,768]{1,0:T(8,128)(2,1)S(1)} %get-tuple-element.325.refs_2_, ...), custom_call_target="tpu_custom_call" | custom-call | flops 1 | bytes 1 | tf_op jit(solution)/shard_map/qkv_grad/pallas_call | solution.py:65
  114.4 1.1 collective-permute-start.52
  116.5 1.2 collective-permute-start.58
  118.6 1.4 collective-permute-start.61
  120.0 1.6 %collective-permute-done.52.refs_1_ = bf16[96,896]{1,0:T(8,128)(2,1)S(1)} collective-permute-done((bf16[96,896]{1,0:T(8,128)(2,1)S(1)}, bf16[96,896]{1,0:T(8,128)(2,1)S(1)}, u32[]{:S(2)}, u32[]{:S(2)}) %collective-permute-start.52) | collective-permute-done | bytes 172064 | tf_op jit(solution)/shard_map/ppermute | solution.py:579
  121.7 1.2 collective-permute-start.56
  124.7 3.2 %collective-permute-done.58.refs_1_ = bf16[96,1536]{1,0:T(8,128)(2,1)S(1)} collective-permute-done((bf16[96,1536]{1,0:T(8,128)(2,1)S(1)}, bf16[96,1536]{1,0:T(8,128)(2,1)S(1)}, u32[]{:S(2)}, u32[]{:S(2)}) %collective-permute-start.58) | collective-permute-done | bytes 294944 | tf_op jit(solution)/shard_map/ppermute | solution.py:579
  127.9 2.7 %collective-permute-done.56.refs_1_ = bf16[96,896]{1,0:T(8,128)(2,1)S(1)} collective-permute-done((bf16[96,896]{1,0:T(8,128)(2,1)S(1)}, bf16[96,896]{1,0:T(8,128)(2,1)S(1)}, u32[]{:S(2)}, u32[]{:S(2)}) %collective-permute-start.56) | collective-permute-done | bytes 172064 | tf_op jit(solution)/shard_map/ppermute | solution.py:579
  131.7 1.2 collective-permute-start.60
  132.9 1.6 %adam_fc.1 = (f32[96,768]{1,0:T(8,128)}, f32[96,768]{1,0:T(8,128)}, f32[96,768]{1,0:T(8,128)}, f32[96,768]{1,0:T(8,128)}, f32[96,768]{1,0:T(8,128)}, /*index=5*/f32[96,768]{1,0:T(8,128)}) custom-call(bf16[768,1536]{1,0:T(8,128)(2,1)S(1)} %get-tuple-element.289.refs_0_, bf16[96,1536]{1,0:T(8,128)(2,1)S(1)} %collective-permute-done.58.refs_1_, ...), custom_call_target="tpu_custom_call" | custom-call | flops 1 | bytes 1 | tf_op jit(solution)/shard_map/adam_fc/pallas_call | solution.py:65
  134.5 1.5 %collective-permute-done.61.refs_2_ = bf16[256,768]{1,0:T(8,128)(2,1)S(1)} collective-permute-done((bf16[256,768]{1,0:T(8,128)(2,1)S(1)}, bf16[256,768]{1,0:T(8,128)(2,1)S(1)}, u32[]{:S(2)}, u32[]{:S(2)}) %collective-permute-start.61) | collective-permute-done | bytes 393248 | tf_op jit(solution)/shard_map/ppermute | solution.py:571
  138.4 1.5 norm_one.1
  139.9 1.6 %first.1 = f32[192,1024]{1,0:T(8,128)} custom-call(s32[12]{0:T(128)S(1)} %copy-done.20, bf16[192,1024]{1,0:T(8,128)(2,1)S(1)} %get-tuple-element.368.refs_1_, bf16[192,1024]{1,0:T(8,128)(2,1)S(1)} %collective-permute-done.64.refs_2_, bf16[192,1024]{1,0:T(8,128)(2,1)S(1)} %collective-permute-done.62.refs_3_, bf16[192,1024]{1,0:T(8,128)(2,1)S(1)} %collective-permute-done.65.refs_4_), custom_call_target="tpu_custom_call" | custom-call | flops 1 | bytes 1 | tf_op jit(solution)/shard_map/first/pallas_call | solution.py:65
  141.5 2.5 %collective-permute-done.63.refs_1_ = bf16[96,896]{1,0:T(8,128)(2,1)S(1)} collective-permute-done((bf16[96,896]{1,0:T(8,128)(2,1)S(1)}, bf16[96,896]{1,0:T(8,128)(2,1)S(1)}, u32[]{:S(2)}, u32[]{:S(2)}) %collective-permute-start.63) | collective-permute-done | bytes 172064 | tf_op jit(solution)/shard_map/ppermute | solution.py:579
  144.1 1.2 collective-permute-done.66.b
  146.2 1.3 adam_qkv.1
  147.5 1.4 collective-permute-done.67.received
  (163 shorter events, 28.5 us)
Async XLA Ops:
  2.4 6.6 %collective-permute-start = (bf16[96,640]{1,0:T(8,128)(2,1)}, bf16[96,640]{1,0:T(8,128)(2,1)S(1)}, u32[]{:S(2)}, u32[]{:S(2)}) collective-permute-start(bf16[96,640]{1,0:T(8,128)(2,1)} %prep_one.1.refs_1_), channel_id=1, source_target_pairs={{0,8},{8,16},{16,24},{24,28},{28,20},{20,12},{12,4},{4,0},{1,9},{9... | collective-permute-start | bytes 368648 | tf_op jit(solution)/shard_map/ppermute | solution.py:579
  5.5 5.1 %collective-permute-start.1 = (bf16[96,640]{1,0:T(8,128)(2,1)}, bf16[96,640]{1,0:T(8,128)(2,1)S(1)}, u32[]{:S(2)}, u32[]{:S(2)}) collective-permute-start(bf16[96,640]{1,0:T(8,128)(2,1)} %prep_one.1.refs_1_), channel_id=1, source_target_pairs={{8,0},{16,8},{24,16},{28,24},{20,28},{12,20},{4,12},{0,4},{9,1},{1... | collective-permute-start | bytes 368648 | tf_op jit(solution)/shard_map/ppermute | solution.py:583
  10.6 6.3 %collective-permute-start.2 = (bf16[96,640]{1,0:T(8,128)(2,1)S(1)}, bf16[96,640]{1,0:T(8,128)(2,1)S(1)}, u32[]{:S(2)}, u32[]{:S(2)}) collective-permute-start(bf16[96,640]{1,0:T(8,128)(2,1)S(1)} %collective-permute-done.refs_2_), channel_id=1, source_target_pairs={{0,8},{8,16},{16,24},{24,28},{28,20},{20,12},{12,4},{4,0},{1,9},{9... | collective-permute-start | bytes 368648 | tf_op jit(solution)/shard_map/ppermute | solution.py:579
  12.2 4.9 %collective-permute-start.3 = (bf16[96,640]{1,0:T(8,128)(2,1)S(1)}, bf16[96,640]{1,0:T(8,128)(2,1)S(1)}, u32[]{:S(2)}, u32[]{:S(2)}) collective-permute-start(bf16[96,640]{1,0:T(8,128)(2,1)S(1)} %collective-permute-done.1.refs_6_), channel_id=1, source_target_pairs={{8,0},{16,8},{24,16},{28,24},{20,28},{12,20},{4,12},{0,4},{9,1},{1... | collective-permute-start | bytes 368648 | tf_op jit(solution)/shard_map/ppermute | solution.py:583
  12.6 4.3 %collective-permute-start.4 = (bf16[96,192]{1,0:T(8,128)(2,1)}, bf16[96,192]{1,0:T(8,128)(2,1)S(1)}, u32[]{:S(2)}, u32[]{:S(2)}) collective-permute-start(bf16[96,192]{1,0:T(8,128)(2,1)} %get-tuple-element.212.own), channel_id=1, source_target_pairs={{0,2},{1,3},{2,0},{3,1},{4,6},{5,7},{6,4},{7,5},{8,10},{9,11},{10,... | collective-permute-start | bytes 110600 | tf_op jit(solution)/shard_map/ppermute | solution.py:571
  17.1 12.8 %collective-permute-start.10 = (bf16[192,1024]{1,0:T(8,128)(2,1)S(1)}, bf16[192,1024]{1,0:T(8,128)(2,1)S(1)}, u32[]{:S(2)}, u32[]{:S(2)}) collective-permute-start(bf16[192,1024]{1,0:T(8,128)(2,1)S(1)} %bitcast.10), channel_id=1, source_target_pairs={{0,2},{1,3},{2,0},{3,1},{4,6},{5,7},{6,4},{7,5},{8,10},{9,11},{10,... | collective-permute-start | bytes 1179656 | tf_op jit(solution)/shard_map/ppermute | solution.py:571
  18.6 5.2 %collective-permute-start.5 = (bf16[96,640]{1,0:T(8,128)(2,1)S(1)}, bf16[96,640]{1,0:T(8,128)(2,1)S(1)}, u32[]{:S(2)}, u32[]{:S(2)}) collective-permute-start(bf16[96,640]{1,0:T(8,128)(2,1)S(1)} %collective-permute-done.2.refs_3_), channel_id=1, source_target_pairs={{0,8},{8,16},{16,24},{24,28},{28,20},{20,12},{12,4},{4,0},{1,9},{9... | collective-permute-start | bytes 368648 | tf_op jit(solution)/shard_map/ppermute | solution.py:579
  20.1 4.9 %collective-permute-start.6 = (bf16[96,640]{1,0:T(8,128)(2,1)S(1)}, bf16[96,640]{1,0:T(8,128)(2,1)S(1)}, u32[]{:S(2)}, u32[]{:S(2)}) collective-permute-start(bf16[96,640]{1,0:T(8,128)(2,1)S(1)} %collective-permute-done.3.refs_7_), channel_id=1, source_target_pairs={{8,0},{16,8},{24,16},{28,24},{20,28},{12,20},{4,12},{0,4},{9,1},{1... | collective-permute-start | bytes 368648 | tf_op jit(solution)/shard_map/ppermute | solution.py:583
  20.7 6.0 %collective-permute-start.8 = (bf16[96,1152]{1,0:T(8,128)(2,1)S(1)}, bf16[96,1152]{1,0:T(8,128)(2,1)S(1)}, u32[]{:S(2)}, u32[]{:S(2)}) collective-permute-start(bf16[96,1152]{1,0:T(8,128)(2,1)S(1)} %join.1.refs_0_), channel_id=1, source_target_pairs={{0,8},{8,16},{16,24},{24,28},{28,20},{20,12},{12,4},{4,0},{1,9},{9... | collective-permute-start | bytes 663560 | tf_op jit(solution)/shard_map/ppermute | solution.py:579
  22.3 5.9 %collective-permute-start.9 = (bf16[96,1152]{1,0:T(8,128)(2,1)S(1)}, bf16[96,1152]{1,0:T(8,128)(2,1)S(1)}, u32[]{:S(2)}, u32[]{:S(2)}) collective-permute-start(bf16[96,1152]{1,0:T(8,128)(2,1)S(1)} %join.1.refs_0_), channel_id=1, source_target_pairs={{8,0},{16,8},{24,16},{28,24},{20,28},{12,20},{4,12},{0,4},{9,1},{1... | collective-permute-start | bytes 663560 | tf_op jit(solution)/shard_map/ppermute | solution.py:583
  23.7 9.8 %collective-permute-start.11 = (bf16[192,1024]{1,0:T(8,128)(2,1)S(1)}, bf16[192,1024]{1,0:T(8,128)(2,1)S(1)}, u32[]{:S(2)}, u32[]{:S(2)}) collective-permute-start(bf16[192,1024]{1,0:T(8,128)(2,1)S(1)} %bitcast.11), channel_id=1, source_target_pairs={{0,1},{1,0},{2,3},{3,2},{4,5},{5,4},{6,7},{7,6},{8,9},{9,8},{10,11... | collective-permute-start | bytes 1179656 | tf_op jit(solution)/shard_map/ppermute | solution.py:567
  25.0 4.9 %collective-permute-start.7 = (bf16[96,640]{1,0:T(8,128)(2,1)S(1)}, bf16[96,640]{1,0:T(8,128)(2,1)S(1)}, u32[]{:S(2)}, u32[]{:S(2)}) collective-permute-start(bf16[96,640]{1,0:T(8,128)(2,1)S(1)} %collective-permute-done.5.refs_4_), channel_id=1, source_target_pairs={{0,8},{8,16},{16,24},{24,28},{28,20},{20,12},{12,4},{4,0},{1,9},{9... | collective-permute-start | bytes 368648 | tf_op jit(solution)/shard_map/ppermute | solution.py:579
  29.9 6.5 %collective-permute-start.12 = (bf16[192,1024]{1,0:T(8,128)(2,1)S(1)}, bf16[192,1024]{1,0:T(8,128)(2,1)S(1)}, u32[]{:S(2)}, u32[]{:S(2)}) collective-permute-start(bf16[192,1024]{1,0:T(8,128)(2,1)S(1)} %collective-permute-done.10.refs_4_), channel_id=1, source_target_pairs={{0,1},{1,0},{2,3},{3,2},{4,5},{5,4},{6,7},{7,6},{8,9},{9,8},{10,11... | collective-permute-start | bytes 1179656 | tf_op jit(solution)/shard_map/ppermute | solution.py:567
  29.9 12.3 %collective-permute-start.13 = (bf16[96,1152]{1,0:T(8,128)(2,1)S(1)}, bf16[96,1152]{1,0:T(8,128)(2,1)S(1)}, u32[]{:S(2)}, u32[]{:S(2)}) collective-permute-start(bf16[96,1152]{1,0:T(8,128)(2,1)S(1)} %collective-permute-done.8.refs_1_), channel_id=1, source_target_pairs={{0,8},{8,16},{16,24},{24,28},{28,20},{20,12},{12,4},{4,0},{1,9},{9... | collective-permute-start | bytes 663560 | tf_op jit(solution)/shard_map/ppermute | solution.py:579
  31.5 10.8 %collective-permute-start.14 = (bf16[96,1152]{1,0:T(8,128)(2,1)S(1)}, bf16[96,1152]{1,0:T(8,128)(2,1)S(1)}, u32[]{:S(2)}, u32[]{:S(2)}) collective-permute-start(bf16[96,1152]{1,0:T(8,128)(2,1)S(1)} %collective-permute-done.9.refs_5_), channel_id=1, source_target_pairs={{8,0},{16,8},{24,16},{28,24},{20,28},{12,20},{4,12},{0,4},{9,1},{1... | collective-permute-start | bytes 663560 | tf_op jit(solution)/shard_map/ppermute | solution.py:583
  32.0 8.9 %collective-permute-start.15 = (bf16[96,768]{1,0:T(8,128)(2,1)S(1)}, bf16[96,768]{1,0:T(8,128)(2,1)S(1)}, u32[]{:S(2)}, u32[]{:S(2)}) collective-permute-start(bf16[96,768]{1,0:T(8,128)(2,1)S(1)} %copy-done.15), channel_id=1, source_target_pairs={{0,8},{8,16},{16,24},{24,28},{28,20},{20,12},{12,4},{4,0},{1,9},{9... | collective-permute-start | bytes 442376 | tf_op jit(solution)/shard_map/ppermute | solution.py:579
  33.5 8.7 %collective-permute-start.16 = (bf16[96,768]{1,0:T(8,128)(2,1)S(1)}, bf16[96,768]{1,0:T(8,128)(2,1)S(1)}, u32[]{:S(2)}, u32[]{:S(2)}) collective-permute-start(bf16[96,768]{1,0:T(8,128)(2,1)S(1)} %copy-done.15), channel_id=1, source_target_pairs={{8,0},{16,8},{24,16},{28,24},{20,28},{12,20},{4,12},{0,4},{9,1},{1... | collective-permute-start | bytes 442376 | tf_op jit(solution)/shard_map/ppermute | solution.py:583
  42.3 11.3 %collective-permute-start.18 = (bf16[96,1152]{1,0:T(8,128)(2,1)S(1)}, bf16[96,1152]{1,0:T(8,128)(2,1)S(1)}, u32[]{:S(2)}, u32[]{:S(2)}) collective-permute-start(bf16[96,1152]{1,0:T(8,128)(2,1)S(1)} %collective-permute-done.13.refs_2_), channel_id=1, source_target_pairs={{0,8},{8,16},{16,24},{24,28},{28,20},{20,12},{12,4},{4,0},{1,9},{9... | collective-permute-start | bytes 663560 | tf_op jit(solution)/shard_map/ppermute | solution.py:579
  44.0 9.6 %collective-permute-start.19 = (bf16[96,1152]{1,0:T(8,128)(2,1)S(1)}, bf16[96,1152]{1,0:T(8,128)(2,1)S(1)}, u32[]{:S(2)}, u32[]{:S(2)}) collective-permute-start(bf16[96,1152]{1,0:T(8,128)(2,1)S(1)} %collective-permute-done.14.refs_6_), channel_id=1, source_target_pairs={{8,0},{16,8},{24,16},{28,24},{20,28},{12,20},{4,12},{0,4},{9,1},{1... | collective-permute-start | bytes 663560 | tf_op jit(solution)/shard_map/ppermute | solution.py:583
  44.3 9.3 %collective-permute-start.22 = (bf16[512,192]{1,0:T(8,128)(2,1)S(1)}, bf16[512,192]{1,0:T(8,128)(2,1)S(1)}, u32[]{:S(2)}, u32[]{:S(2)}) collective-permute-start(bf16[512,192]{1,0:T(8,128)(2,1)S(1)} %get-tuple-element.241.c0.refs_9_.refs_4_), channel_id=1, source_target_pairs={{0,2},{1,3},{2,0},{3,1},{4,6},{5,7},{6,4},{7,5},{8,10},{9,11},{10,... | collective-permute-start | bytes 589832 | tf_op jit(solution)/shard_map/ppermute | solution.py:571
  44.7 7.5 %collective-permute-start.20 = (bf16[96,768]{1,0:T(8,128)(2,1)S(1)}, bf16[96,768]{1,0:T(8,128)(2,1)S(1)}, u32[]{:S(2)}, u32[]{:S(2)}) collective-permute-start(bf16[96,768]{1,0:T(8,128)(2,1)S(1)} %collective-permute-done.15.refs_1_), channel_id=1, source_target_pairs={{0,8},{8,16},{16,24},{24,28},{28,20},{20,12},{12,4},{4,0},{1,9},{9... | collective-permute-start | bytes 442376 | tf_op jit(solution)/shard_map/ppermute | solution.py:579
  46.2 7.3 %collective-permute-start.21 = (bf16[96,768]{1,0:T(8,128)(2,1)S(1)}, bf16[96,768]{1,0:T(8,128)(2,1)S(1)}, u32[]{:S(2)}, u32[]{:S(2)}) collective-permute-start(bf16[96,768]{1,0:T(8,128)(2,1)S(1)} %collective-permute-done.16.refs_5_), channel_id=1, source_target_pairs={{8,0},{16,8},{24,16},{28,24},{20,28},{12,20},{4,12},{0,4},{9,1},{1... | collective-permute-start | bytes 442376 | tf_op jit(solution)/shard_map/ppermute | solution.py:583
  53.6 8.9 %collective-permute-start.25 = (bf16[96,1152]{1,0:T(8,128)(2,1)S(1)}, bf16[96,1152]{1,0:T(8,128)(2,1)S(1)}, u32[]{:S(2)}, u32[]{:S(2)}) collective-permute-start(bf16[96,1152]{1,0:T(8,128)(2,1)S(1)} %collective-permute-done.18.refs_3_), channel_id=1, source_target_pairs={{0,8},{8,16},{16,24},{24,28},{28,20},{20,12},{12,4},{4,0},{1,9},{9... | collective-permute-start | bytes 663560 | tf_op jit(solution)/shard_map/ppermute | solution.py:579
  54.6 7.8 %collective-permute-start.24 = (bf16[512,192]{1,0:T(8,128)(2,1)S(1)}, bf16[512,192]{1,0:T(8,128)(2,1)S(1)}, u32[]{:S(2)}, u32[]{:S(2)}) collective-permute-start(bf16[512,192]{1,0:T(8,128)(2,1)S(1)} %get-tuple-element.253.c0.refs_9_.refs_6_.refs_5_), channel_id=1, source_target_pairs={{0,2},{1,3},{2,0},{3,1},{4,6},{5,7},{6,4},{7,5},{8,10},{9,11},{10,... | collective-permute-start | bytes 589832 | tf_op jit(solution)/shard_map/ppermute | solution.py:571
  55.1 7.1 %collective-permute-start.26 = (bf16[96,768]{1,0:T(8,128)(2,1)S(1)}, bf16[96,768]{1,0:T(8,128)(2,1)S(1)}, u32[]{:S(2)}, u32[]{:S(2)}) collective-permute-start(bf16[96,768]{1,0:T(8,128)(2,1)S(1)} %collective-permute-done.20.refs_2_), channel_id=1, source_target_pairs={{0,8},{8,16},{16,24},{24,28},{28,20},{20,12},{12,4},{4,0},{1,9},{9... | collective-permute-start | bytes 442376 | tf_op jit(solution)/shard_map/ppermute | solution.py:579
  56.1 6.3 %collective-permute-start.27 = (bf16[96,768]{1,0:T(8,128)(2,1)S(1)}, bf16[96,768]{1,0:T(8,128)(2,1)S(1)}, u32[]{:S(2)}, u32[]{:S(2)}) collective-permute-start(bf16[96,768]{1,0:T(8,128)(2,1)S(1)} %collective-permute-done.21.refs_6_), channel_id=1, source_target_pairs={{8,0},{16,8},{24,16},{28,24},{20,28},{12,20},{4,12},{0,4},{9,1},{1... | collective-permute-start | bytes 442376 | tf_op jit(solution)/shard_map/ppermute | solution.py:583
  57.2 6.8 %collective-permute-start.17 = (bf16[512,192]{1,0:T(8,128)(2,1)S(1)}, bf16[512,192]{1,0:T(8,128)(2,1)S(1)}, u32[]{:S(2)}, u32[]{:S(2)}) collective-permute-start(bf16[512,192]{1,0:T(8,128)(2,1)S(1)} %get-tuple-element.241.c0.refs_9_.refs_4_), channel_id=1, source_target_pairs={{0,1},{1,0},{2,3},{3,2},{4,5},{5,4},{6,7},{7,6},{8,9},{9,8},{10,11... | collective-permute-start | bytes 589832 | tf_op jit(solution)/shard_map/ppermute | solution.py:567
  62.3 1.7 %collective-permute-start.23 = (bf16[512,192]{1,0:T(8,128)(2,1)S(1)}, bf16[512,192]{1,0:T(8,128)(2,1)S(1)}, u32[]{:S(2)}, u32[]{:S(2)}) collective-permute-start(bf16[512,192]{1,0:T(8,128)(2,1)S(1)} %collective-permute-done.22.c2), channel_id=1, source_target_pairs={{0,1},{1,0},{2,3},{3,2},{4,5},{5,4},{6,7},{7,6},{8,9},{9,8},{10,11... | collective-permute-start | bytes 589832 | tf_op jit(solution)/shard_map/ppermute | solution.py:567
  62.9 2.3 %collective-permute-start.29 = (bf16[192,768]{1,0:T(8,128)(2,1)S(1)}, bf16[192,768]{1,0:T(8,128)(2,1)S(1)}, u32[]{:S(2)}, u32[]{:S(2)}) collective-permute-start(bf16[192,768]{1,0:T(8,128)(2,1)S(1)} %get-tuple-element.262.w2), channel_id=1, source_target_pairs={{0,1},{1,0},{2,3},{3,2},{4,5},{5,4},{6,7},{7,6},{8,9},{9,8},{10,11... | collective-permute-start | bytes 884744 | tf_op jit(solution)/shard_map/ppermute | solution.py:567
  63.4 1.7 %collective-permute-start.28 = (bf16[192,768]{1,0:T(8,128)(2,1)S(1)}, bf16[192,768]{1,0:T(8,128)(2,1)S(1)}, u32[]{:S(2)}, u32[]{:S(2)}) collective-permute-start(bf16[192,768]{1,0:T(8,128)(2,1)S(1)} %get-tuple-element.261.w0.refs_7_.refs_4_), channel_id=1, source_target_pairs={{0,1},{1,0},{2,3},{3,2},{4,5},{5,4},{6,7},{7,6},{8,9},{9,8},{10,11... | collective-permute-start | bytes 884744 | tf_op jit(solution)/shard_map/ppermute | solution.py:567
  63.5 5.1 %collective-permute-start.30 = (bf16[512,192]{1,0:T(8,128)(2,1)S(1)}, bf16[512,192]{1,0:T(8,128)(2,1)S(1)}, u32[]{:S(2)}, u32[]{:S(2)}) collective-permute-start(bf16[512,192]{1,0:T(8,128)(2,1)S(1)} %get-tuple-element.253.c0.refs_9_.refs_6_.refs_5_), channel_id=1, source_target_pairs={{0,1},{1,0},{2,3},{3,2},{4,5},{5,4},{6,7},{7,6},{8,9},{9,8},{10,11... | collective-permute-start | bytes 589832 | tf_op jit(solution)/shard_map/ppermute | solution.py:567
  63.9 4.6 %collective-permute-start.31 = (bf16[512,192]{1,0:T(8,128)(2,1)S(1)}, bf16[512,192]{1,0:T(8,128)(2,1)S(1)}, u32[]{:S(2)}, u32[]{:S(2)}) collective-permute-start(bf16[512,192]{1,0:T(8,128)(2,1)S(1)} %collective-permute-done.24.c2), channel_id=1, source_target_pairs={{0,1},{1,0},{2,3},{3,2},{4,5},{5,4},{6,7},{7,6},{8,9},{9,8},{10,11... | collective-permute-start | bytes 589832 | tf_op jit(solution)/shard_map/ppermute | solution.py:567
  64.0 7.9 %collective-permute-start.32 = (bf16[96,768]{1,0:T(8,128)(2,1)S(1)}, bf16[96,768]{1,0:T(8,128)(2,1)S(1)}, u32[]{:S(2)}, u32[]{:S(2)}) collective-permute-start(bf16[96,768]{1,0:T(8,128)(2,1)S(1)} %collective-permute-done.26.refs_3_), channel_id=1, source_target_pairs={{0,8},{8,16},{16,24},{24,28},{28,20},{20,12},{12,4},{4,0},{1,9},{9... | collective-permute-start | bytes 442376 | tf_op jit(solution)/shard_map/ppermute | solution.py:579
  73.6 2.1 %collective-permute-start.33 = (bf16[128,768]{1,0:T(8,128)(2,1)S(1)}, bf16[128,768]{1,0:T(8,128)(2,1)S(1)}, u32[]{:S(2)}, u32[]{:S(2)}) collective-permute-start(bf16[128,768]{1,0:T(8,128)(2,1)S(1)} %get-tuple-element.284), channel_id=1, source_target_pairs={{0,1},{1,0},{2,3},{3,2},{4,5},{5,4},{6,7},{7,6},{8,9},{9,8},{10,11... | collective-permute-start | bytes 589832 | tf_op jit(solution)/shard_map/ppermute | solution.py:567
  74.0 1.8 %collective-permute-start.34 = (bf16[128,768]{1,0:T(8,128)(2,1)S(1)}, bf16[128,768]{1,0:T(8,128)(2,1)S(1)}, u32[]{:S(2)}, u32[]{:S(2)}) collective-permute-start(bf16[128,768]{1,0:T(8,128)(2,1)S(1)} %get-tuple-element.285), channel_id=1, source_target_pairs={{0,1},{1,0},{2,3},{3,2},{4,5},{5,4},{6,7},{7,6},{8,9},{9,8},{10,11... | collective-permute-start | bytes 589832 | tf_op jit(solution)/shard_map/ppermute | solution.py:567
  75.9 11.3 %collective-permute-start.39 = (bf16[256,768]{1,0:T(8,128)(2,1)S(1)}, bf16[256,768]{1,0:T(8,128)(2,1)S(1)}, u32[]{:S(2)}, u32[]{:S(2)}) collective-permute-start(bf16[256,768]{1,0:T(8,128)(2,1)S(1)} %add0.1.refs_1_), channel_id=1, source_target_pairs={{0,2},{1,3},{2,0},{3,1},{4,6},{5,7},{6,4},{7,5},{8,10},{9,11},{10,... | collective-permute-start | bytes 1179656 | tf_op jit(solution)/shard_map/ppermute | solution.py:571
  76.4 5.3 %collective-permute-start.35 = (bf16[128,768]{1,0:T(8,128)(2,1)S(1)}, bf16[128,768]{1,0:T(8,128)(2,1)S(1)}, u32[]{:S(2)}, u32[]{:S(2)}) collective-permute-start(bf16[128,768]{1,0:T(8,128)(2,1)S(1)} %get-tuple-element.291), channel_id=1, source_target_pairs={{0,1},{1,0},{2,3},{3,2},{4,5},{5,4},{6,7},{7,6},{8,9},{9,8},{10,11... | collective-permute-start | bytes 589832 | tf_op jit(solution)/shard_map/ppermute | solution.py:567
  76.4 5.3 %collective-permute-start.36 = (bf16[128,768]{1,0:T(8,128)(2,1)S(1)}, bf16[128,768]{1,0:T(8,128)(2,1)S(1)}, u32[]{:S(2)}, u32[]{:S(2)}) collective-permute-start(bf16[128,768]{1,0:T(8,128)(2,1)S(1)} %get-tuple-element.292), channel_id=1, source_target_pairs={{0,1},{1,0},{2,3},{3,2},{4,5},{5,4},{6,7},{7,6},{8,9},{9,8},{10,11... | collective-permute-start | bytes 589832 | tf_op jit(solution)/shard_map/ppermute | solution.py:567
  79.6 12.8 %collective-permute-start.37 = (bf16[96,1536]{1,0:T(8,128)(2,1)S(1)}, bf16[96,1536]{1,0:T(8,128)(2,1)S(1)}, u32[]{:S(2)}, u32[]{:S(2)}) collective-permute-start(bf16[96,1536]{1,0:T(8,128)(2,1)S(1)} %get-tuple-element.293), channel_id=1, source_target_pairs={{0,8},{8,16},{16,24},{24,28},{28,20},{20,12},{12,4},{4,0},{1,9},{9... | collective-permute-start | bytes 884744 | tf_op jit(solution)/shard_map/ppermute | solution.py:579
  80.6 11.9 %collective-permute-start.38 = (bf16[96,1536]{1,0:T(8,128)(2,1)S(1)}, bf16[96,1536]{1,0:T(8,128)(2,1)S(1)}, u32[]{:S(2)}, u32[]{:S(2)}) collective-permute-start(bf16[96,1536]{1,0:T(8,128)(2,1)S(1)} %get-tuple-element.294), channel_id=1, source_target_pairs={{8,0},{16,8},{24,16},{28,24},{20,28},{12,20},{4,12},{0,4},{9,1},{1... | collective-permute-start | bytes 884744 | tf_op jit(solution)/shard_map/ppermute | solution.py:583
  87.9 1.7 %collective-permute-start.41 = (bf16[128,768]{1,0:T(8,128)(2,1)S(1)}, bf16[128,768]{1,0:T(8,128)(2,1)S(1)}, u32[]{:S(2)}, u32[]{:S(2)}) collective-permute-start(bf16[128,768]{1,0:T(8,128)(2,1)S(1)} %get-tuple-element.297.refs_4_), channel_id=1, source_target_pairs={{0,1},{1,0},{2,3},{3,2},{4,5},{5,4},{6,7},{7,6},{8,9},{9,8},{10,11... | collective-permute-start | bytes 589832 | tf_op jit(solution)/shard_map/ppermute | solution.py:567
  88.4 11.1 %collective-permute-start.42 = (bf16[256,768]{1,0:T(8,128)(2,1)S(1)}, bf16[256,768]{1,0:T(8,128)(2,1)S(1)}, u32[]{:S(2)}, u32[]{:S(2)}) collective-permute-start(bf16[256,768]{1,0:T(8,128)(2,1)S(1)} %add1.1.refs_1_), channel_id=1, source_target_pairs={{0,2},{1,3},{2,0},{3,1},{4,6},{5,7},{6,4},{7,5},{8,10},{9,11},{10,... | collective-permute-start | bytes 1179656 | tf_op jit(solution)/shard_map/ppermute | solution.py:571
  94.1 6.0 %collective-permute-start.50 = (bf16[256,768]{1,0:T(8,128)(2,1)S(1)}, bf16[256,768]{1,0:T(8,128)(2,1)S(1)}, u32[]{:S(2)}, u32[]{:S(2)}) collective-permute-start(bf16[256,768]{1,0:T(8,128)(2,1)S(1)} %get-tuple-element.304), channel_id=1, source_target_pairs={{0,1},{1,0},{2,3},{3,2},{4,5},{5,4},{6,7},{7,6},{8,9},{9,8},{10,11... | collective-permute-start | bytes 1179656 | tf_op jit(solution)/shard_map/ppermute | solution.py:567
  94.4 6.2 %collective-permute-start.49 = (bf16[256,768]{1,0:T(8,128)(2,1)S(1)}, bf16[256,768]{1,0:T(8,128)(2,1)S(1)}, u32[]{:S(2)}, u32[]{:S(2)}) collective-permute-start(bf16[256,768]{1,0:T(8,128)(2,1)S(1)} %get-tuple-element.302), channel_id=1, source_target_pairs={{0,1},{1,0},{2,3},{3,2},{4,5},{5,4},{6,7},{7,6},{8,9},{9,8},{10,11... | collective-permute-start | bytes 1179656 | tf_op jit(solution)/shard_map/ppermute | solution.py:567
  94.8 9.5 %collective-permute-start.45 = (bf16[96,1536]{1,0:T(8,128)(2,1)S(1)}, bf16[96,1536]{1,0:T(8,128)(2,1)S(1)}, u32[]{:S(2)}, u32[]{:S(2)}) collective-permute-start(bf16[96,1536]{1,0:T(8,128)(2,1)S(1)} %get-tuple-element.315), channel_id=1, source_target_pairs={{0,8},{8,16},{16,24},{24,28},{28,20},{20,12},{12,4},{4,0},{1,9},{9... | collective-permute-start | bytes 884744 | tf_op jit(solution)/shard_map/ppermute | solution.py:579
  95.9 8.9 %collective-permute-start.46 = (bf16[96,1536]{1,0:T(8,128)(2,1)S(1)}, bf16[96,1536]{1,0:T(8,128)(2,1)S(1)}, u32[]{:S(2)}, u32[]{:S(2)}) collective-permute-start(bf16[96,1536]{1,0:T(8,128)(2,1)S(1)} %get-tuple-element.316), channel_id=1, source_target_pairs={{8,0},{16,8},{24,16},{28,24},{20,28},{12,20},{4,12},{0,4},{9,1},{1... | collective-permute-start | bytes 884744 | tf_op jit(solution)/shard_map/ppermute | solution.py:583
  100.8 13.5 %collective-permute-start.51 = (bf16[256,768]{1,0:T(8,128)(2,1)S(1)}, bf16[256,768]{1,0:T(8,128)(2,1)S(1)}, u32[]{:S(2)}, u32[]{:S(2)}) collective-permute-start(bf16[256,768]{1,0:T(8,128)(2,1)S(1)} %get-tuple-element.338), channel_id=1, source_target_pairs={{0,2},{1,3},{2,0},{3,1},{4,6},{5,7},{6,4},{7,5},{8,10},{9,11},{10,... | collective-permute-start | bytes 1179656 | tf_op jit(solution)/shard_map/ppermute | solution.py:571
  104.9 9.3 %collective-permute-start.48 = (bf16[96,1536]{1,0:T(8,128)(2,1)S(1)}, bf16[96,1536]{1,0:T(8,128)(2,1)S(1)}, u32[]{:S(2)}, u32[]{:S(2)}) collective-permute-start(bf16[96,1536]{1,0:T(8,128)(2,1)S(1)} %get-tuple-element.331), channel_id=1, source_target_pairs={{8,0},{16,8},{24,16},{28,24},{20,28},{12,20},{4,12},{0,4},{9,1},{1... | collective-permute-start | bytes 884744 | tf_op jit(solution)/shard_map/ppermute | solution.py:583
  106.0 8.4 %collective-permute-start.47 = (bf16[96,1536]{1,0:T(8,128)(2,1)S(1)}, bf16[96,1536]{1,0:T(8,128)(2,1)S(1)}, u32[]{:S(2)}, u32[]{:S(2)}) collective-permute-start(bf16[96,1536]{1,0:T(8,128)(2,1)S(1)} %get-tuple-element.320), channel_id=1, source_target_pairs={{0,8},{8,16},{16,24},{24,28},{28,20},{20,12},{12,4},{4,0},{1,9},{9... | collective-permute-start | bytes 884744 | tf_op jit(solution)/shard_map/ppermute | solution.py:579
  111.5 6.1 %collective-permute-start.54 = (bf16[256,768]{1,0:T(8,128)(2,1)S(1)}, bf16[256,768]{1,0:T(8,128)(2,1)S(1)}, u32[]{:S(2)}, u32[]{:S(2)}) collective-permute-start(bf16[256,768]{1,0:T(8,128)(2,1)S(1)} %get-tuple-element.342), channel_id=1, source_target_pairs={{0,1},{1,0},{2,3},{3,2},{4,5},{5,4},{6,7},{7,6},{8,9},{9,8},{10,11... | collective-permute-start | bytes 1179656 | tf_op jit(solution)/shard_map/ppermute | solution.py:567
  111.6 6.8 %collective-permute-start.55 = (bf16[256,768]{1,0:T(8,128)(2,1)S(1)}, bf16[256,768]{1,0:T(8,128)(2,1)S(1)}, u32[]{:S(2)}, u32[]{:S(2)}) collective-permute-start(bf16[256,768]{1,0:T(8,128)(2,1)S(1)} %get-tuple-element.343), channel_id=1, source_target_pairs={{0,1},{1,0},{2,3},{3,2},{4,5},{5,4},{6,7},{7,6},{8,9},{9,8},{10,11... | collective-permute-start | bytes 1179656 | tf_op jit(solution)/shard_map/ppermute | solution.py:567
  114.4 7.2 %collective-permute-start.52 = (bf16[96,896]{1,0:T(8,128)(2,1)S(1)}, bf16[96,896]{1,0:T(8,128)(2,1)S(1)}, u32[]{:S(2)}, u32[]{:S(2)}) collective-permute-start(bf16[96,896]{1,0:T(8,128)(2,1)S(1)} %get-tuple-element.339), channel_id=1, source_target_pairs={{0,8},{8,16},{16,24},{24,28},{28,20},{20,12},{12,4},{4,0},{1,9},{9... | collective-permute-start | bytes 516104 | tf_op jit(solution)/shard_map/ppermute | solution.py:579
  115.5 6.1 %collective-permute-start.53 = (bf16[96,896]{1,0:T(8,128)(2,1)S(1)}, bf16[96,896]{1,0:T(8,128)(2,1)S(1)}, u32[]{:S(2)}, u32[]{:S(2)}) collective-permute-start(bf16[96,896]{1,0:T(8,128)(2,1)S(1)} %get-tuple-element.340), channel_id=1, source_target_pairs={{8,0},{16,8},{24,16},{28,24},{20,28},{12,20},{4,12},{0,4},{9,1},{1... | collective-permute-start | bytes 516104 | tf_op jit(solution)/shard_map/ppermute | solution.py:583
  116.5 11.4 %collective-permute-start.58 = (bf16[96,1536]{1,0:T(8,128)(2,1)S(1)}, bf16[96,1536]{1,0:T(8,128)(2,1)S(1)}, u32[]{:S(2)}, u32[]{:S(2)}) collective-permute-start(bf16[96,1536]{1,0:T(8,128)(2,1)S(1)} %mlp_hop1.1), channel_id=1, source_target_pairs={{0,8},{8,16},{16,24},{24,28},{28,20},{20,12},{12,4},{4,0},{1,9},{9... | collective-permute-start | bytes 884744 | tf_op jit(solution)/shard_map/ppermute | solution.py:579
  117.7 16.8 %collective-permute-start.62 = (bf16[192,1024]{1,0:T(8,128)(2,1)S(1)}, bf16[192,1024]{1,0:T(8,128)(2,1)S(1)}, u32[]{:S(2)}, u32[]{:S(2)}) collective-permute-start(bf16[192,1024]{1,0:T(8,128)(2,1)S(1)} %get-tuple-element.368.refs_1_), channel_id=1, source_target_pairs={{0,2},{1,3},{2,0},{3,1},{4,6},{5,7},{6,4},{7,5},{8,10},{9,11},{10,... | collective-permute-start | bytes 1179656 | tf_op jit(solution)/shard_map/ppermute | solution.py:571
  118.6 17.4 %collective-permute-start.61 = (bf16[256,768]{1,0:T(8,128)(2,1)S(1)}, bf16[256,768]{1,0:T(8,128)(2,1)S(1)}, u32[]{:S(2)}, u32[]{:S(2)}) collective-permute-start(bf16[256,768]{1,0:T(8,128)(2,1)S(1)} %get-tuple-element.344), channel_id=1, source_target_pairs={{0,2},{1,3},{2,0},{3,1},{4,6},{5,7},{6,4},{7,5},{8,10},{9,11},{10,... | collective-permute-start | bytes 1179656 | tf_op jit(solution)/shard_map/ppermute | solution.py:571
  121.7 8.9 %collective-permute-start.56 = (bf16[96,896]{1,0:T(8,128)(2,1)S(1)}, bf16[96,896]{1,0:T(8,128)(2,1)S(1)}, u32[]{:S(2)}, u32[]{:S(2)}) collective-permute-start(bf16[96,896]{1,0:T(8,128)(2,1)S(1)} %get-tuple-element.347), channel_id=1, source_target_pairs={{0,8},{8,16},{16,24},{24,28},{28,20},{20,12},{12,4},{4,0},{1,9},{9... | collective-permute-start | bytes 516104 | tf_op jit(solution)/shard_map/ppermute | solution.py:579
  123.0 7.7 %collective-permute-start.57 = (bf16[96,896]{1,0:T(8,128)(2,1)S(1)}, bf16[96,896]{1,0:T(8,128)(2,1)S(1)}, u32[]{:S(2)}, u32[]{:S(2)}) collective-permute-start(bf16[96,896]{1,0:T(8,128)(2,1)S(1)} %get-tuple-element.348), channel_id=1, source_target_pairs={{8,0},{16,8},{24,16},{28,24},{20,28},{12,20},{4,12},{0,4},{9,1},{1... | collective-permute-start | bytes 516104 | tf_op jit(solution)/shard_map/ppermute | solution.py:583
  130.8 5.5 %collective-permute-start.59 = (bf16[96,896]{1,0:T(8,128)(2,1)S(1)}, bf16[96,896]{1,0:T(8,128)(2,1)S(1)}, u32[]{:S(2)}, u32[]{:S(2)}) collective-permute-start(bf16[96,896]{1,0:T(8,128)(2,1)S(1)} %get-tuple-element.355), channel_id=1, source_target_pairs={{0,8},{8,16},{16,24},{24,28},{28,20},{20,12},{12,4},{4,0},{1,9},{9... | collective-permute-start | bytes 516104 | tf_op jit(solution)/shard_map/ppermute | solution.py:579
  131.7 5.4 %collective-permute-start.60 = (bf16[96,896]{1,0:T(8,128)(2,1)S(1)}, bf16[96,896]{1,0:T(8,128)(2,1)S(1)}, u32[]{:S(2)}, u32[]{:S(2)}) collective-permute-start(bf16[96,896]{1,0:T(8,128)(2,1)S(1)} %get-tuple-element.356), channel_id=1, source_target_pairs={{8,0},{16,8},{24,16},{28,24},{20,28},{12,20},{4,12},{0,4},{9,1},{1... | collective-permute-start | bytes 516104 | tf_op jit(solution)/shard_map/ppermute | solution.py:583
  137.1 2.8 %collective-permute-start.64 = (bf16[192,1024]{1,0:T(8,128)(2,1)S(1)}, bf16[192,1024]{1,0:T(8,128)(2,1)S(1)}, u32[]{:S(2)}, u32[]{:S(2)}) collective-permute-start(bf16[192,1024]{1,0:T(8,128)(2,1)S(1)} %get-tuple-element.368.refs_1_), channel_id=1, source_target_pairs={{0,1},{1,0},{2,3},{3,2},{4,5},{5,4},{6,7},{7,6},{8,9},{9,8},{10,11... | collective-permute-start | bytes 1179656 | tf_op jit(solution)/shard_map/ppermute | solution.py:567
  137.1 2.8 %collective-permute-start.65 = (bf16[192,1024]{1,0:T(8,128)(2,1)S(1)}, bf16[192,1024]{1,0:T(8,128)(2,1)S(1)}, u32[]{:S(2)}, u32[]{:S(2)}) collective-permute-start(bf16[192,1024]{1,0:T(8,128)(2,1)S(1)} %collective-permute-done.62.refs_3_), channel_id=1, source_target_pairs={{0,1},{1,0},{2,3},{3,2},{4,5},{5,4},{6,7},{7,6},{8,9},{9,8},{10,11... | collective-permute-start | bytes 1179656 | tf_op jit(solution)/shard_map/ppermute | solution.py:567
  137.7 6.3 %collective-permute-start.63 = (bf16[96,896]{1,0:T(8,128)(2,1)S(1)}, bf16[96,896]{1,0:T(8,128)(2,1)S(1)}, u32[]{:S(2)}, u32[]{:S(2)}) collective-permute-start(bf16[96,896]{1,0:T(8,128)(2,1)S(1)} %qkv_hop1.1), channel_id=1, source_target_pairs={{0,8},{8,16},{16,24},{24,28},{28,20},{20,12},{12,4},{4,0},{1,9},{9... | collective-permute-start | bytes 516104 | tf_op jit(solution)/shard_map/ppermute | solution.py:579
  145.3 3.6 %collective-permute-start.67 = (f32[8,128]{1,0:T(8,128)S(1)}, f32[8,128]{1,0:T(8,128)S(1)}, u32[]{:S(2)}, u32[]{:S(2)}) collective-permute-start(f32[8,128]{1,0:T(8,128)S(1)} %sum.1.sums), channel_id=1, source_target_pairs={{0,2},{1,3},{2,0},{3,1},{4,6},{5,7},{6,4},{7,5},{8,10},{9,11},{10,... | collective-permute-start | bytes 12296 | tf_op jit(solution)/shard_map/ppermute | solution.py:571
  (28 other events, 190.9 us)
where the time goes:
time: 150 us
  Pallas kernels  52.4 us (35%)
  starting transfers between devices  50.9 us (34%)
  waiting for transfers between devices  43.6 us (29%)
  local copies, waits for them, and re-layouts  1.51 us (1%)
    pallas_call x43, Pallas kernels, call(): pl.pallas_call(kernel, in_specs=[smem] * len(scalars) + [given] * len(ins...  52.4 us
    ppermute x20, starting transfers between devices, ahead(): return lax.ppermute(value, 'dp', FORWARD)  27 us
    ppermute x20, waiting for transfers between devices, ahead(): return lax.ppermute(value, 'dp', FORWARD)  21.2 us
    ppermute x10, waiting for transfers between devices, swap_x(): return lax.ppermute(value, 'mp', [(i, i ^ 2) for i in range(4)])  11.4 us
    ppermute x15, starting transfers between devices, behind(): return lax.ppermute(value, 'dp', BACKWARD)  10.4 us
    ppermute x15, waiting for transfers between devices, behind(): return lax.ppermute(value, 'dp', BACKWARD)  8.52 us
    ppermute x10, starting transfers between devices, swap_x(): return lax.ppermute(value, 'mp', [(i, i ^ 2) for i in range(4)])  8.39 us
    ppermute x23, starting transfers between devices, swap_core(): return lax.ppermute(value, 'mp', [(i, i ^ 1) for i in range(4)])  5.1 us
  transfers between devices with their start and end apart: 68, of which 31 were waited for; matrix products, arithmetic and copies ran while one was open for 0% of the time, Pallas kernels for 32%

commit v1 on v0

--- a/solution.py
+++ b/solution.py
@@ -911,6 +911,9 @@
             vmem=24,
         )
 
+    ysend_a, ykeep_a = mlp_out(0, mine_b)
+    ysend_b, ykeep_b = mlp_out(1, mine_b)
+    across_a, ysend_a, ysend_b = fence(across_a, ysend_a, ysend_b)
     dr_a, *ab_a = norm_two(0, after(mine_a, mine_b), across_a)
     partner = [swap_core(v) for v in ab_a]
     ab_one, dq_a, dk, dv = attend_back(
@@ -918,8 +921,7 @@
     )
     mlp_sum.a, mlp_sum.b, dq_a = fence(mlp_sum.a, mlp_sum.b, dq_a)
     mlp_sum.step()
-    ysend_a, ykeep_a = mlp_out(0, dq_a)
-    ysend_b, ykeep_b = mlp_out(1, ysend_a)
+    dq_a, ysend_a, ysend_b = fence(dq_a, ysend_a, ysend_b)
     yreceived_a, yreceived_b = swap_core(ysend_a), swap_core(ysend_b)
     rows_mine, rows_sent = call(
         output_rows_kernel,

time: 150 us -> 150 us (level)
  transfers between devices with their start and end apart: 68 -> 68, of which waited for: 31 -> 30; matrix products, arithmetic and copies ran while one was open for 0% -> 0% of each run, Pallas kernels for 32% -> 32%
where the time goes in v1:
time: 150 us; the launch traced here: 149 us
  Pallas kernels  52.6 us (35%)
  starting transfers between devices  51.4 us (34%)
  waiting for transfers between devices  42.8 us (29%)
  local copies, waits for them, and re-layouts  1.51 us (1%)
    pallas_call x43, Pallas kernels, call(): pl.pallas_call(kernel, in_specs=[smem] * len(scalars) + [given] * len(ins...  52.6 us
    ppermute x20, starting transfers between devices, ahead(): return lax.ppermute(value, 'dp', FORWARD)  27.5 us
    ppermute x20, waiting for transfers between devices, ahead(): return lax.ppermute(value, 'dp', FORWARD)  20.8 us
    ppermute x10, waiting for transfers between devices, swap_x(): return lax.ppermute(value, 'mp', [(i, i ^ 2) for i in range(4)])  11.2 us
    ppermute x15, starting transfers between devices, behind(): return lax.ppermute(value, 'dp', BACKWARD)  10.1 us
    ppermute x10, starting transfers between devices, swap_x(): return lax.ppermute(value, 'mp', [(i, i ^ 2) for i in range(4)])  8.64 us
    ppermute x15, waiting for transfers between devices, behind(): return lax.ppermute(value, 'dp', BACKWARD)  8.3 us
    ppermute x23, starting transfers between devices, swap_core(): return lax.ppermute(value, 'mp', [(i, i ^ 1) for i in range(4)])  5.1 us
  transfers between devices with their start and end apart: 68, of which 30 were waited for; matrix products, arithmetic and copies ran while one was open for 0% of the time, Pallas kernels for 32%

profile of v1, /device:TPU:0, one launch (start us, length us, event | category | flops | bytes accessed | tf_op | source)
XLA Modules:
  0.0 149.4 jit_solution(4596018730899000363)
XLA Ops:
  0.7 1.8 %prep_one.1.refs_1_ = bf16[96,640]{1,0:T(8,128)(2,1)} custom-call(f32[96,576]{1,0:T(8,128)} %refs_3_.3, f32[4,96]{1,0:T(4,128)} %w.1), custom_call_target="tpu_custom_call" | custom-call | flops 1 | bytes 1 | tf_op jit(solution)/shard_map/prep_one/pallas_call | solution.py:65
  2.4 3.1 %collective-permute-start = (bf16[96,640]{1,0:T(8,128)(2,1)}, bf16[96,640]{1,0:T(8,128)(2,1)S(1)}, u32[]{:S(2)}, u32[]{:S(2)}) collective-permute-start(bf16[96,640]{1,0:T(8,128)(2,1)} %prep_one.1.refs_1_), channel_id=1, source_target_pairs={{0,8},{8,16},{16,24},{24,28},{28,20},{20,12},{12,4},{4,0},{1,9},{9... | collective-permute-start | bytes 368648 | tf_op jit(solution)/shard_map/ppermute | solution.py:579
  5.5 1.9 %prep_two.1 = (bf16[96,192]{1,0:T(8,128)(2,1)}, bf16[96,768]{1,0:T(8,128)(2,1)}, bf16[96,768]{1,0:T(8,128)(2,1)}) custom-call(f32[192,96]{1,0:T(8,128)} %refs_6_.1, f32[96,768]{1,0:T(8,128)} %refs_3_.2, f32[96,768]{1,0:T(8,128)} %bitcast.8), custom_call_target="tpu_custom_call" | custom-call | flops 1 | bytes 1 | tf_op jit(solution)/shard_map/prep_two/pallas_call | solution.py:65
  7.4 1.6 %collective-permute-done.refs_2_ = bf16[96,640]{1,0:T(8,128)(2,1)S(1)} collective-permute-done((bf16[96,640]{1,0:T(8,128)(2,1)}, bf16[96,640]{1,0:T(8,128)(2,1)S(1)}, u32[]{:S(2)}, u32[]{:S(2)}) %collective-permute-start) | collective-permute-done | bytes 122912 | tf_op jit(solution)/shard_map/ppermute | solution.py:579
  9.0 1.6 %collective-permute-done.1.refs_6_ = bf16[96,640]{1,0:T(8,128)(2,1)S(1)} collective-permute-done((bf16[96,640]{1,0:T(8,128)(2,1)}, bf16[96,640]{1,0:T(8,128)(2,1)S(1)}, u32[]{:S(2)}, u32[]{:S(2)}) %collective-permute-start.1) | collective-permute-done | bytes 122912 | tf_op jit(solution)/shard_map/ppermute | solution.py:583
  10.6 1.6 %collective-permute-start.2 = (bf16[96,640]{1,0:T(8,128)(2,1)S(1)}, bf16[96,640]{1,0:T(8,128)(2,1)S(1)}, u32[]{:S(2)}, u32[]{:S(2)}) collective-permute-start(bf16[96,640]{1,0:T(8,128)(2,1)S(1)} %collective-permute-done.refs_2_), channel_id=1, source_target_pairs={{0,8},{8,16},{16,24},{24,28},{28,20},{20,12},{12,4},{4,0},{1,9},{9... | collective-permute-start | bytes 368648 | tf_op jit(solution)/shard_map/ppermute | solution.py:579
  12.6 1.5 collective-permute-start.4
  14.1 1.4 copy-done
  17.1 1.5 collective-permute-start.10
  18.6 1.6 %collective-permute-start.5 = (bf16[96,640]{1,0:T(8,128)(2,1)S(1)}, bf16[96,640]{1,0:T(8,128)(2,1)S(1)}, u32[]{:S(2)}, u32[]{:S(2)}) collective-permute-start(bf16[96,640]{1,0:T(8,128)(2,1)S(1)} %collective-permute-done.2.refs_3_), channel_id=1, source_target_pairs={{0,8},{8,16},{16,24},{24,28},{28,20},{20,12},{12,4},{4,0},{1,9},{9... | collective-permute-start | bytes 368648 | tf_op jit(solution)/shard_map/ppermute | solution.py:579
  20.7 1.6 %collective-permute-start.8 = (bf16[96,1152]{1,0:T(8,128)(2,1)S(1)}, bf16[96,1152]{1,0:T(8,128)(2,1)S(1)}, u32[]{:S(2)}, u32[]{:S(2)}) collective-permute-start(bf16[96,1152]{1,0:T(8,128)(2,1)S(1)} %join.1.refs_0_), channel_id=1, source_target_pairs={{0,8},{8,16},{16,24},{24,28},{28,20},{20,12},{12,4},{4,0},{1,9},{9... | collective-permute-start | bytes 663560 | tf_op jit(solution)/shard_map/ppermute | solution.py:579
  23.7 1.3 collective-permute-done.6.refs_8_
  25.0 1.5 %collective-permute-start.7 = (bf16[96,640]{1,0:T(8,128)(2,1)S(1)}, bf16[96,640]{1,0:T(8,128)(2,1)S(1)}, u32[]{:S(2)}, u32[]{:S(2)}) collective-permute-start(bf16[96,640]{1,0:T(8,128)(2,1)S(1)} %collective-permute-done.5.refs_4_), channel_id=1, source_target_pairs={{0,8},{8,16},{16,24},{24,28},{28,20},{20,12},{12,4},{4,0},{1,9},{9... | collective-permute-start | bytes 368648 | tf_op jit(solution)/shard_map/ppermute | solution.py:579
  26.7 1.6 %collective-permute-done.9.refs_5_ = bf16[96,1152]{1,0:T(8,128)(2,1)S(1)} collective-permute-done((bf16[96,1152]{1,0:T(8,128)(2,1)S(1)}, bf16[96,1152]{1,0:T(8,128)(2,1)S(1)}, u32[]{:S(2)}, u32[]{:S(2)}) %collective-permute-start.9) | collective-permute-done | bytes 221216 | tf_op jit(solution)/shard_map/ppermute | solution.py:583
  28.2 1.7 %collective-permute-done.7.refs_5_ = bf16[96,640]{1,0:T(8,128)(2,1)S(1)} collective-permute-done((bf16[96,640]{1,0:T(8,128)(2,1)S(1)}, bf16[96,640]{1,0:T(8,128)(2,1)S(1)}, u32[]{:S(2)}, u32[]{:S(2)}) %collective-permute-start.7) | collective-permute-done | bytes 122912 | tf_op jit(solution)/shard_map/ppermute | solution.py:579
  29.9 1.6 %collective-permute-start.13 = (bf16[96,1152]{1,0:T(8,128)(2,1)S(1)}, bf16[96,1152]{1,0:T(8,128)(2,1)S(1)}, u32[]{:S(2)}, u32[]{:S(2)}) collective-permute-start(bf16[96,1152]{1,0:T(8,128)(2,1)S(1)} %collective-permute-done.8.refs_1_), channel_id=1, source_target_pairs={{0,8},{8,16},{16,24},{24,28},{28,20},{20,12},{12,4},{4,0},{1,9},{9... | collective-permute-start | bytes 663560 | tf_op jit(solution)/shard_map/ppermute | solution.py:579
  32.0 1.5 %collective-permute-start.15 = (bf16[96,768]{1,0:T(8,128)(2,1)S(1)}, bf16[96,768]{1,0:T(8,128)(2,1)S(1)}, u32[]{:S(2)}, u32[]{:S(2)}) collective-permute-start(bf16[96,768]{1,0:T(8,128)(2,1)S(1)} %copy-done.15), channel_id=1, source_target_pairs={{0,8},{8,16},{16,24},{24,28},{28,20},{20,12},{12,4},{4,0},{1,9},{9... | collective-permute-start | bytes 442376 | tf_op jit(solution)/shard_map/ppermute | solution.py:579
  34.0 2.4 %qkv.1 = (bf16[1024,768]{1,0:T(8,128)(2,1)S(1)}, bf16[1024,576]{1,0:T(8,128)(2,1)S(1)}, bf16[192,1024]{1,0:T(8,128)(2,1)S(1)}, bf16[768,640]{1,0:T(8,128)(2,1)S(1)}, f32[8,768]{1,0:T(8,128)S(1)}) custom-call(f32[1024,768]{1,0:T(8,128)S(1)} %unit.1.refs_0_.refs_2_, bf16[96,640]{1,0:T(8,128)(2,1)S(1)} %copy-done.6, ...), custom_call_target="tpu_custom_call" | custom-call | flops 1 | bytes 1 | tf_op jit(solution)/shard_map/qkv/pallas_call | solution.py:65
  37.2 2.9 %attend0.1 = (bf16[512,192]{1,0:T(8,128)(2,1)S(1)}, f32[8,512]{1,0:T(8,128)S(1)}) custom-call(bf16[1024,576]{1,0:T(8,128)(2,1)S(1)} %get-tuple-element.256.m_ref.refs_1_, bf16[192,1024]{1,0:T(8,128)(2,1)S(1)} %values.1.v_ref.refs_2_), custom_call_target="tpu_custom_call" | custom-call | flops 1 | bytes 1 | tf_op jit(solution)/shard_map/attend0/pallas_call | solution.py:65
  40.9 1.3 collective-permute-done.16.refs_5_
  42.3 1.7 %collective-permute-start.18 = (bf16[96,1152]{1,0:T(8,128)(2,1)S(1)}, bf16[96,1152]{1,0:T(8,128)(2,1)S(1)}, u32[]{:S(2)}, u32[]{:S(2)}) collective-permute-start(bf16[96,1152]{1,0:T(8,128)(2,1)S(1)} %collective-permute-done.13.refs_2_), channel_id=1, source_target_pairs={{0,8},{8,16},{16,24},{24,28},{28,20},{20,12},{12,4},{4,0},{1,9},{9... | collective-permute-start | bytes 663560 | tf_op jit(solution)/shard_map/ppermute | solution.py:579
  44.7 1.5 %collective-permute-start.20 = (bf16[96,768]{1,0:T(8,128)(2,1)S(1)}, bf16[96,768]{1,0:T(8,128)(2,1)S(1)}, u32[]{:S(2)}, u32[]{:S(2)}) collective-permute-start(bf16[96,768]{1,0:T(8,128)(2,1)S(1)} %collective-permute-done.15.refs_1_), channel_id=1, source_target_pairs={{0,8},{8,16},{16,24},{24,28},{28,20},{20,12},{12,4},{4,0},{1,9},{9... | collective-permute-start | bytes 442376 | tf_op jit(solution)/shard_map/ppermute | solution.py:579
  46.8 4.9 %attend1.1 = (bf16[512,192]{1,0:T(8,128)(2,1)S(1)}, f32[8,512]{1,0:T(8,128)S(1)}) custom-call(bf16[1024,576]{1,0:T(8,128)(2,1)S(1)} %get-tuple-element.256.m_ref.refs_1_, bf16[192,1024]{1,0:T(8,128)(2,1)S(1)} %values.1.v_ref.refs_2_), custom_call_target="tpu_custom_call" | custom-call | flops 1 | bytes 1 | tf_op jit(solution)/shard_map/attend1/pallas_call | solution.py:65
  52.2 1.4 collective-permute-done.21.refs_6_
  53.6 1.0 collective-permute-start.25
  55.1 1.0 collective-permute-start.26
  56.1 1.0 collective-permute-start.27
  57.2 5.1 %collective-permute-done.26.refs_3_ = bf16[96,768]{1,0:T(8,128)(2,1)S(1)} collective-permute-done((bf16[96,768]{1,0:T(8,128)(2,1)S(1)}, bf16[96,768]{1,0:T(8,128)(2,1)S(1)}, u32[]{:S(2)}, u32[]{:S(2)}) %collective-permute-start.26) | collective-permute-done | bytes 147488 | tf_op jit(solution)/shard_map/ppermute | solution.py:579
  64.0 1.1 collective-permute-start.32
  65.2 3.4 %mlp0.1 = (f32[512,768]{1,0:T(8,128)S(1)}, f32[512,768]{1,0:T(8,128)S(1)}, bf16[512,768]{1,0:T(8,128)(2,1)S(1)}, bf16[512,768]{1,0:T(8,128)(2,1)S(1)}, f32[512,768]{1,0:T(8,128)S(1)}) custom-call(bf16[1024,768]{1,0:T(8,128)(2,1)S(1)} %copy-done.1, f32[8,768]{1,0:T(8,128)S(1)} %get-tuple-element.271.norm_ref.refs_4_.refs_5_, ...), custom_call_target="tpu_custom_call" | custom-call | flops 1 | bytes 1 | tf_op jit(solution)/shard_map/mlp0/pallas_call | solution.py:65
  68.6 3.4 %mlp1.1 = (f32[512,768]{1,0:T(8,128)S(1)}, f32[512,768]{1,0:T(8,128)S(1)}, bf16[512,768]{1,0:T(8,128)(2,1)S(1)}, bf16[512,768]{1,0:T(8,128)(2,1)S(1)}, f32[512,768]{1,0:T(8,128)S(1)}) custom-call(bf16[1024,768]{1,0:T(8,128)(2,1)S(1)} %copy-done.1, f32[8,768]{1,0:T(8,128)S(1)} %get-tuple-element.271.norm_ref.refs_4_.refs_5_, ...), custom_call_target="tpu_custom_call" | custom-call | flops 1 | bytes 1 | tf_op jit(solution)/shard_map/mlp1/pallas_call | solution.py:65
  72.1 1.6 %mlp_back0.1 = (bf16[512,768]{1,0:T(8,128)(2,1)S(1)}, bf16[128,768]{1,0:T(8,128)(2,1)S(1)}, bf16[128,768]{1,0:T(8,128)(2,1)S(1)}, f32[256,768]{1,0:T(8,128)S(1)}, f32[8,768]{1,0:T(8,128)S(1)}) custom-call(bf16[1024,768]{1,0:T(8,128)(2,1)S(1)} %fetch.1.refs_0_.refs_4_.refs_3_, f32[512,768]{1,0:T(8,128)S(1)} %get-tuple-element.277.refs_1_, ...), custom_call_target="tpu_custom_call" | custom-call | flops 1 | bytes 1 | tf_op jit(solution)/shard_map/mlp_back0/pallas_call | solution.py:65
  74.2 1.6 %mlp_back1.1 = (bf16[512,768]{1,0:T(8,128)(2,1)S(1)}, bf16[128,768]{1,0:T(8,128)(2,1)S(1)}, bf16[128,768]{1,0:T(8,128)(2,1)S(1)}, f32[256,768]{1,0:T(8,128)S(1)}, f32[8,768]{1,0:T(8,128)S(1)}) custom-call(bf16[1024,768]{1,0:T(8,128)(2,1)S(1)} %fetch.1.refs_0_.refs_4_.refs_3_, f32[512,768]{1,0:T(8,128)S(1)} %get-tuple-element.283.refs_1_, ...), custom_call_target="tpu_custom_call" | custom-call | flops 1 | bytes 1 | tf_op jit(solution)/shard_map/mlp_back1/pallas_call | solution.py:65
  77.0 2.7 %mlp_grad.1 = (bf16[768,1536]{1,0:T(8,128)(2,1)S(1)}, bf16[96,1536]{1,0:T(8,128)(2,1)S(1)}, bf16[96,1536]{1,0:T(8,128)(2,1)S(1)}) custom-call(bf16[512,768]{1,0:T(8,128)(2,1)S(1)} %get-tuple-element.292.refs_0_, bf16[512,768]{1,0:T(8,128)(2,1)S(1)} %get-tuple-element.293.refs_1_, bf16[512,768]{1,0:T(8,128)(2,1)S(1)} %get-tuple-element.281.refs_2_, ...), custom_call_target="tpu_custom_call" | custom-call | flops 1 | bytes 1 | tf_op jit(solution)/shard_map/mlp_grad/pallas_call | solution.py:65
  80.6 1.2 collective-permute-start.38
  83.5 3.8 %collective-permute-done.39.refs_2_ = bf16[256,768]{1,0:T(8,128)(2,1)S(1)} collective-permute-done((bf16[256,768]{1,0:T(8,128)(2,1)S(1)}, bf16[256,768]{1,0:T(8,128)(2,1)S(1)}, u32[]{:S(2)}, u32[]{:S(2)}) %collective-permute-start.39) | collective-permute-done | bytes 393248 | tf_op jit(solution)/shard_map/ppermute | solution.py:571
  89.6 2.9 %attend_back0.1 = (bf16[512,768]{1,0:T(8,128)(2,1)S(1)}, f32[512,192]{1,0:T(8,128)S(1)}, f32[512,192]{1,0:T(8,128)S(1)}, f32[512,192]{1,0:T(8,128)S(1)}) custom-call(s32[12]{0:T(128)S(1)} %copy-done.20, bf16[1024,576]{1,0:T(8,128)(2,1)S(1)} %get-tuple-element.256.m_ref.refs_1_, bf16[192,1024]{1,0:T(8,128)(2,1)S(1)} %values.1.v_ref.refs_2_, ...), custom_call_target="tpu_custom_call" | custom-call | flops 1 | bytes 1 | tf_op jit(solution)/shard_map/attend_back0/pallas_call | solution.py:65
  93.3 1.0 collective-permute-start.45
  94.3 1.1 collective-permute-start.46
  95.4 4.2 %collective-permute-done.42.refs_2_ = bf16[256,768]{1,0:T(8,128)(2,1)S(1)} collective-permute-done((bf16[256,768]{1,0:T(8,128)(2,1)S(1)}, bf16[256,768]{1,0:T(8,128)(2,1)S(1)}, u32[]{:S(2)}, u32[]{:S(2)}) %collective-permute-start.42) | collective-permute-done | bytes 393248 | tf_op jit(solution)/shard_map/ppermute | solution.py:571
  101.9 2.5 %attend_back1.1 = (bf16[512,768]{1,0:T(8,128)(2,1)S(1)}, f32[256,192]{1,0:T(8,128)S(1)}, f32[768,192]{1,0:T(8,128)S(1)}, f32[768,192]{1,0:T(8,128)S(1)}) custom-call(s32[12]{0:T(128)S(1)} %copy-done.20, bf16[1024,576]{1,0:T(8,128)(2,1)S(1)} %get-tuple-element.256.m_ref.refs_1_, bf16[192,1024]{1,0:T(8,128)(2,1)S(1)} %values.1.v_ref.refs_2_, ...), custom_call_target="tpu_custom_call" | custom-call | flops 1 | bytes 1 | tf_op jit(solution)/shard_map/attend_back1/pallas_call | solution.py:65
  105.6 1.2 collective-permute-start.47
  106.7 3.1 %attend_back2.1 = (bf16[1024,576]{1,0:T(8,128)(2,1)S(1)}, bf16[192,1024]{1,0:T(8,128)(2,1)S(1)}) custom-call(s32[12]{0:T(128)S(1)} %copy-done.20, bf16[1024,576]{1,0:T(8,128)(2,1)S(1)} %get-tuple-element.256.m_ref.refs_1_, bf16[192,1024]{1,0:T(8,128)(2,1)S(1)} %values.1.v_ref.refs_2_, bf16[512,768]{1,0:T(8,128)(2,1)S(1)} %get-tuple-element.321.refs_3_, ...), custom_call_target="tpu_custom_call" | custom-call | flops 1 | bytes 1 | tf_op jit(solution)/shard_map/attend_back2/pallas_call | solution.py:65
  109.8 1.5 %input.1 = (bf16[256,768]{1,0:T(8,128)(2,1)S(1)}, bf16[256,768]{1,0:T(8,128)(2,1)S(1)}, f32[512,768]{1,0:T(8,128)S(1)}, f32[8,768]{1,0:T(8,128)S(1)}) custom-call(bf16[1024,576]{1,0:T(8,128)(2,1)S(1)} %get-tuple-element.335.refs_0_.refs_1_, bf16[768,640]{1,0:T(8,128)(2,1)S(1)} %get-tuple-element.337.refs_1_, f32[1024,768]{1,0:T(8,128)S(1)} %unit.1.refs_0_.refs_2_, ...), custom_call_target="tpu_custom_call" | custom-call | flops 1 | bytes 1 | tf_op jit(solution)/shard_map/input/pallas_call | solution.py:65
  111.9 2.0 %qkv_grad.1 = (bf16[768,896]{1,0:T(8,128)(2,1)S(1)}, bf16[96,896]{1,0:T(8,128)(2,1)S(1)}, bf16[96,896]{1,0:T(8,128)(2,1)S(1)}) custom-call(bf16[1024,768]{1,0:T(8,128)(2,1)S(1)} %get-tuple-element.234.refs_0_, bf16[1024,576]{1,0:T(8,128)(2,1)S(1)} %get-tuple-element.335.refs_0_.refs_1_, bf16[512,768]{1,0:T(8,128)(2,1)S(1)} %get-tuple-element.336.refs_2_, ...), custom_call_target="tpu_custom_call" | custom-call | flops 1 | bytes 1 | tf_op jit(solution)/shard_map/qkv_grad/pallas_call | solution.py:65
  114.4 1.2 collective-permute-start.52
  116.5 1.2 collective-permute-start.58
  118.7 1.4 collective-permute-start.61
  120.1 1.6 %collective-permute-done.52.refs_1_ = bf16[96,896]{1,0:T(8,128)(2,1)S(1)} collective-permute-done((bf16[96,896]{1,0:T(8,128)(2,1)S(1)}, bf16[96,896]{1,0:T(8,128)(2,1)S(1)}, u32[]{:S(2)}, u32[]{:S(2)}) %collective-permute-start.52) | collective-permute-done | bytes 172064 | tf_op jit(solution)/shard_map/ppermute | solution.py:579
  121.8 1.2 collective-permute-start.56
  124.8 3.2 %collective-permute-done.58.refs_1_ = bf16[96,1536]{1,0:T(8,128)(2,1)S(1)} collective-permute-done((bf16[96,1536]{1,0:T(8,128)(2,1)S(1)}, bf16[96,1536]{1,0:T(8,128)(2,1)S(1)}, u32[]{:S(2)}, u32[]{:S(2)}) %collective-permute-start.58) | collective-permute-done | bytes 294944 | tf_op jit(solution)/shard_map/ppermute | solution.py:579
  128.0 2.4 %collective-permute-done.56.refs_1_ = bf16[96,896]{1,0:T(8,128)(2,1)S(1)} collective-permute-done((bf16[96,896]{1,0:T(8,128)(2,1)S(1)}, bf16[96,896]{1,0:T(8,128)(2,1)S(1)}, u32[]{:S(2)}, u32[]{:S(2)}) %collective-permute-start.56) | collective-permute-done | bytes 172064 | tf_op jit(solution)/shard_map/ppermute | solution.py:579
  130.5 1.0 collective-permute-start.59
  131.6 1.0 collective-permute-start.60
  132.6 1.6 %adam_fc.1 = (f32[96,768]{1,0:T(8,128)}, f32[96,768]{1,0:T(8,128)}, f32[96,768]{1,0:T(8,128)}, f32[96,768]{1,0:T(8,128)}, f32[96,768]{1,0:T(8,128)}, /*index=5*/f32[96,768]{1,0:T(8,128)}) custom-call(bf16[768,1536]{1,0:T(8,128)(2,1)S(1)} %get-tuple-element.295.refs_0_, bf16[96,1536]{1,0:T(8,128)(2,1)S(1)} %collective-permute-done.58.refs_1_, ...), custom_call_target="tpu_custom_call" | custom-call | flops 1 | bytes 1 | tf_op jit(solution)/shard_map/adam_fc/pallas_call | solution.py:65
  134.3 1.6 %collective-permute-done.61.refs_2_ = bf16[256,768]{1,0:T(8,128)(2,1)S(1)} collective-permute-done((bf16[256,768]{1,0:T(8,128)(2,1)S(1)}, bf16[256,768]{1,0:T(8,128)(2,1)S(1)}, u32[]{:S(2)}, u32[]{:S(2)}) %collective-permute-start.61) | collective-permute-done | bytes 393248 | tf_op jit(solution)/shard_map/ppermute | solution.py:571
  136.0 1.0 collective-permute-done.60.refs_2_
  138.5 1.5 norm_one.1
  140.0 1.6 %first.1 = f32[192,1024]{1,0:T(8,128)} custom-call(s32[12]{0:T(128)S(1)} %copy-done.20, bf16[192,1024]{1,0:T(8,128)(2,1)S(1)} %get-tuple-element.380.refs_1_, bf16[192,1024]{1,0:T(8,128)(2,1)S(1)} %collective-permute-done.64.refs_2_, bf16[192,1024]{1,0:T(8,128)(2,1)S(1)} %collective-permute-done.62.refs_3_, bf16[192,1024]{1,0:T(8,128)(2,1)S(1)} %collective-permute-done.65.refs_4_), custom_call_target="tpu_custom_call" | custom-call | flops 1 | bytes 1 | tf_op jit(solution)/shard_map/first/pallas_call | solution.py:65
  141.6 2.3 %collective-permute-done.63.refs_1_ = bf16[96,896]{1,0:T(8,128)(2,1)S(1)} collective-permute-done((bf16[96,896]{1,0:T(8,128)(2,1)S(1)}, bf16[96,896]{1,0:T(8,128)(2,1)S(1)}, u32[]{:S(2)}, u32[]{:S(2)}) %collective-permute-start.63) | collective-permute-done | bytes 172064 | tf_op jit(solution)/shard_map/ppermute | solution.py:579
  144.0 1.2 collective-permute-done.66.b
  145.2 1.1 collective-permute-start.67
  146.4 1.3 adam_qkv.1
  147.6 1.2 collective-permute-done.67.received
  (163 shorter events, 28.8 us)
Async XLA Ops:
  2.4 6.6 %collective-permute-start = (bf16[96,640]{1,0:T(8,128)(2,1)}, bf16[96,640]{1,0:T(8,128)(2,1)S(1)}, u32[]{:S(2)}, u32[]{:S(2)}) collective-permute-start(bf16[96,640]{1,0:T(8,128)(2,1)} %prep_one.1.refs_1_), channel_id=1, source_target_pairs={{0,8},{8,16},{16,24},{24,28},{28,20},{20,12},{12,4},{4,0},{1,9},{9... | collective-permute-start | bytes 368648 | tf_op jit(solution)/shard_map/ppermute | solution.py:579
  5.5 5.1 %collective-permute-start.1 = (bf16[96,640]{1,0:T(8,128)(2,1)}, bf16[96,640]{1,0:T(8,128)(2,1)S(1)}, u32[]{:S(2)}, u32[]{:S(2)}) collective-permute-start(bf16[96,640]{1,0:T(8,128)(2,1)} %prep_one.1.refs_1_), channel_id=1, source_target_pairs={{8,0},{16,8},{24,16},{28,24},{20,28},{12,20},{4,12},{0,4},{9,1},{1... | collective-permute-start | bytes 368648 | tf_op jit(solution)/shard_map/ppermute | solution.py:583
  10.6 6.3 %collective-permute-start.2 = (bf16[96,640]{1,0:T(8,128)(2,1)S(1)}, bf16[96,640]{1,0:T(8,128)(2,1)S(1)}, u32[]{:S(2)}, u32[]{:S(2)}) collective-permute-start(bf16[96,640]{1,0:T(8,128)(2,1)S(1)} %collective-permute-done.refs_2_), channel_id=1, source_target_pairs={{0,8},{8,16},{16,24},{24,28},{28,20},{20,12},{12,4},{4,0},{1,9},{9... | collective-permute-start | bytes 368648 | tf_op jit(solution)/shard_map/ppermute | solution.py:579
  12.2 4.9 %collective-permute-start.3 = (bf16[96,640]{1,0:T(8,128)(2,1)S(1)}, bf16[96,640]{1,0:T(8,128)(2,1)S(1)}, u32[]{:S(2)}, u32[]{:S(2)}) collective-permute-start(bf16[96,640]{1,0:T(8,128)(2,1)S(1)} %collective-permute-done.1.refs_6_), channel_id=1, source_target_pairs={{8,0},{16,8},{24,16},{28,24},{20,28},{12,20},{4,12},{0,4},{9,1},{1... | collective-permute-start | bytes 368648 | tf_op jit(solution)/shard_map/ppermute | solution.py:583
  12.6 4.3 %collective-permute-start.4 = (bf16[96,192]{1,0:T(8,128)(2,1)}, bf16[96,192]{1,0:T(8,128)(2,1)S(1)}, u32[]{:S(2)}, u32[]{:S(2)}) collective-permute-start(bf16[96,192]{1,0:T(8,128)(2,1)} %get-tuple-element.218.own), channel_id=1, source_target_pairs={{0,2},{1,3},{2,0},{3,1},{4,6},{5,7},{6,4},{7,5},{8,10},{9,11},{10,... | collective-permute-start | bytes 110600 | tf_op jit(solution)/shard_map/ppermute | solution.py:571
  17.1 12.8 %collective-permute-start.10 = (bf16[192,1024]{1,0:T(8,128)(2,1)S(1)}, bf16[192,1024]{1,0:T(8,128)(2,1)S(1)}, u32[]{:S(2)}, u32[]{:S(2)}) collective-permute-start(bf16[192,1024]{1,0:T(8,128)(2,1)S(1)} %bitcast.10), channel_id=1, source_target_pairs={{0,2},{1,3},{2,0},{3,1},{4,6},{5,7},{6,4},{7,5},{8,10},{9,11},{10,... | collective-permute-start | bytes 1179656 | tf_op jit(solution)/shard_map/ppermute | solution.py:571
  18.6 5.2 %collective-permute-start.5 = (bf16[96,640]{1,0:T(8,128)(2,1)S(1)}, bf16[96,640]{1,0:T(8,128)(2,1)S(1)}, u32[]{:S(2)}, u32[]{:S(2)}) collective-permute-start(bf16[96,640]{1,0:T(8,128)(2,1)S(1)} %collective-permute-done.2.refs_3_), channel_id=1, source_target_pairs={{0,8},{8,16},{16,24},{24,28},{28,20},{20,12},{12,4},{4,0},{1,9},{9... | collective-permute-start | bytes 368648 | tf_op jit(solution)/shard_map/ppermute | solution.py:579
  20.1 4.9 %collective-permute-start.6 = (bf16[96,640]{1,0:T(8,128)(2,1)S(1)}, bf16[96,640]{1,0:T(8,128)(2,1)S(1)}, u32[]{:S(2)}, u32[]{:S(2)}) collective-permute-start(bf16[96,640]{1,0:T(8,128)(2,1)S(1)} %collective-permute-done.3.refs_7_), channel_id=1, source_target_pairs={{8,0},{16,8},{24,16},{28,24},{20,28},{12,20},{4,12},{0,4},{9,1},{1... | collective-permute-start | bytes 368648 | tf_op jit(solution)/shard_map/ppermute | solution.py:583
  20.7 6.0 %collective-permute-start.8 = (bf16[96,1152]{1,0:T(8,128)(2,1)S(1)}, bf16[96,1152]{1,0:T(8,128)(2,1)S(1)}, u32[]{:S(2)}, u32[]{:S(2)}) collective-permute-start(bf16[96,1152]{1,0:T(8,128)(2,1)S(1)} %join.1.refs_0_), channel_id=1, source_target_pairs={{0,8},{8,16},{16,24},{24,28},{28,20},{20,12},{12,4},{4,0},{1,9},{9... | collective-permute-start | bytes 663560 | tf_op jit(solution)/shard_map/ppermute | solution.py:579
  22.3 5.9 %collective-permute-start.9 = (bf16[96,1152]{1,0:T(8,128)(2,1)S(1)}, bf16[96,1152]{1,0:T(8,128)(2,1)S(1)}, u32[]{:S(2)}, u32[]{:S(2)}) collective-permute-start(bf16[96,1152]{1,0:T(8,128)(2,1)S(1)} %join.1.refs_0_), channel_id=1, source_target_pairs={{8,0},{16,8},{24,16},{28,24},{20,28},{12,20},{4,12},{0,4},{9,1},{1... | collective-permute-start | bytes 663560 | tf_op jit(solution)/shard_map/ppermute | solution.py:583
  23.7 9.8 %collective-permute-start.11 = (bf16[192,1024]{1,0:T(8,128)(2,1)S(1)}, bf16[192,1024]{1,0:T(8,128)(2,1)S(1)}, u32[]{:S(2)}, u32[]{:S(2)}) collective-permute-start(bf16[192,1024]{1,0:T(8,128)(2,1)S(1)} %bitcast.11), channel_id=1, source_target_pairs={{0,1},{1,0},{2,3},{3,2},{4,5},{5,4},{6,7},{7,6},{8,9},{9,8},{10,11... | collective-permute-start | bytes 1179656 | tf_op jit(solution)/shard_map/ppermute | solution.py:567
  25.0 4.9 %collective-permute-start.7 = (bf16[96,640]{1,0:T(8,128)(2,1)S(1)}, bf16[96,640]{1,0:T(8,128)(2,1)S(1)}, u32[]{:S(2)}, u32[]{:S(2)}) collective-permute-start(bf16[96,640]{1,0:T(8,128)(2,1)S(1)} %collective-permute-done.5.refs_4_), channel_id=1, source_target_pairs={{0,8},{8,16},{16,24},{24,28},{28,20},{20,12},{12,4},{4,0},{1,9},{9... | collective-permute-start | bytes 368648 | tf_op jit(solution)/shard_map/ppermute | solution.py:579
  29.9 6.5 %collective-permute-start.12 = (bf16[192,1024]{1,0:T(8,128)(2,1)S(1)}, bf16[192,1024]{1,0:T(8,128)(2,1)S(1)}, u32[]{:S(2)}, u32[]{:S(2)}) collective-permute-start(bf16[192,1024]{1,0:T(8,128)(2,1)S(1)} %collective-permute-done.10.refs_4_), channel_id=1, source_target_pairs={{0,1},{1,0},{2,3},{3,2},{4,5},{5,4},{6,7},{7,6},{8,9},{9,8},{10,11... | collective-permute-start | bytes 1179656 | tf_op jit(solution)/shard_map/ppermute | solution.py:567
  29.9 12.3 %collective-permute-start.13 = (bf16[96,1152]{1,0:T(8,128)(2,1)S(1)}, bf16[96,1152]{1,0:T(8,128)(2,1)S(1)}, u32[]{:S(2)}, u32[]{:S(2)}) collective-permute-start(bf16[96,1152]{1,0:T(8,128)(2,1)S(1)} %collective-permute-done.8.refs_1_), channel_id=1, source_target_pairs={{0,8},{8,16},{16,24},{24,28},{28,20},{20,12},{12,4},{4,0},{1,9},{9... | collective-permute-start | bytes 663560 | tf_op jit(solution)/shard_map/ppermute | solution.py:579
  31.5 10.8 %collective-permute-start.14 = (bf16[96,1152]{1,0:T(8,128)(2,1)S(1)}, bf16[96,1152]{1,0:T(8,128)(2,1)S(1)}, u32[]{:S(2)}, u32[]{:S(2)}) collective-permute-start(bf16[96,1152]{1,0:T(8,128)(2,1)S(1)} %collective-permute-done.9.refs_5_), channel_id=1, source_target_pairs={{8,0},{16,8},{24,16},{28,24},{20,28},{12,20},{4,12},{0,4},{9,1},{1... | collective-permute-start | bytes 663560 | tf_op jit(solution)/shard_map/ppermute | solution.py:583
  32.0 8.9 %collective-permute-start.15 = (bf16[96,768]{1,0:T(8,128)(2,1)S(1)}, bf16[96,768]{1,0:T(8,128)(2,1)S(1)}, u32[]{:S(2)}, u32[]{:S(2)}) collective-permute-start(bf16[96,768]{1,0:T(8,128)(2,1)S(1)} %copy-done.15), channel_id=1, source_target_pairs={{0,8},{8,16},{16,24},{24,28},{28,20},{20,12},{12,4},{4,0},{1,9},{9... | collective-permute-start | bytes 442376 | tf_op jit(solution)/shard_map/ppermute | solution.py:579
  33.5 8.7 %collective-permute-start.16 = (bf16[96,768]{1,0:T(8,128)(2,1)S(1)}, bf16[96,768]{1,0:T(8,128)(2,1)S(1)}, u32[]{:S(2)}, u32[]{:S(2)}) collective-permute-start(bf16[96,768]{1,0:T(8,128)(2,1)S(1)} %copy-done.15), channel_id=1, source_target_pairs={{8,0},{16,8},{24,16},{28,24},{20,28},{12,20},{4,12},{0,4},{9,1},{1... | collective-permute-start | bytes 442376 | tf_op jit(solution)/shard_map/ppermute | solution.py:583
  42.3 11.3 %collective-permute-start.18 = (bf16[96,1152]{1,0:T(8,128)(2,1)S(1)}, bf16[96,1152]{1,0:T(8,128)(2,1)S(1)}, u32[]{:S(2)}, u32[]{:S(2)}) collective-permute-start(bf16[96,1152]{1,0:T(8,128)(2,1)S(1)} %collective-permute-done.13.refs_2_), channel_id=1, source_target_pairs={{0,8},{8,16},{16,24},{24,28},{28,20},{20,12},{12,4},{4,0},{1,9},{9... | collective-permute-start | bytes 663560 | tf_op jit(solution)/shard_map/ppermute | solution.py:579
  44.0 9.6 %collective-permute-start.19 = (bf16[96,1152]{1,0:T(8,128)(2,1)S(1)}, bf16[96,1152]{1,0:T(8,128)(2,1)S(1)}, u32[]{:S(2)}, u32[]{:S(2)}) collective-permute-start(bf16[96,1152]{1,0:T(8,128)(2,1)S(1)} %collective-permute-done.14.refs_6_), channel_id=1, source_target_pairs={{8,0},{16,8},{24,16},{28,24},{20,28},{12,20},{4,12},{0,4},{9,1},{1... | collective-permute-start | bytes 663560 | tf_op jit(solution)/shard_map/ppermute | solution.py:583
  44.3 9.3 %collective-permute-start.22 = (bf16[512,192]{1,0:T(8,128)(2,1)S(1)}, bf16[512,192]{1,0:T(8,128)(2,1)S(1)}, u32[]{:S(2)}, u32[]{:S(2)}) collective-permute-start(bf16[512,192]{1,0:T(8,128)(2,1)S(1)} %get-tuple-element.247.c0.refs_9_.refs_4_), channel_id=1, source_target_pairs={{0,2},{1,3},{2,0},{3,1},{4,6},{5,7},{6,4},{7,5},{8,10},{9,11},{10,... | collective-permute-start | bytes 589832 | tf_op jit(solution)/shard_map/ppermute | solution.py:571
  44.7 7.5 %collective-permute-start.20 = (bf16[96,768]{1,0:T(8,128)(2,1)S(1)}, bf16[96,768]{1,0:T(8,128)(2,1)S(1)}, u32[]{:S(2)}, u32[]{:S(2)}) collective-permute-start(bf16[96,768]{1,0:T(8,128)(2,1)S(1)} %collective-permute-done.15.refs_1_), channel_id=1, source_target_pairs={{0,8},{8,16},{16,24},{24,28},{28,20},{20,12},{12,4},{4,0},{1,9},{9... | collective-permute-start | bytes 442376 | tf_op jit(solution)/shard_map/ppermute | solution.py:579
  46.2 7.3 %collective-permute-start.21 = (bf16[96,768]{1,0:T(8,128)(2,1)S(1)}, bf16[96,768]{1,0:T(8,128)(2,1)S(1)}, u32[]{:S(2)}, u32[]{:S(2)}) collective-permute-start(bf16[96,768]{1,0:T(8,128)(2,1)S(1)} %collective-permute-done.16.refs_5_), channel_id=1, source_target_pairs={{8,0},{16,8},{24,16},{28,24},{20,28},{12,20},{4,12},{0,4},{9,1},{1... | collective-permute-start | bytes 442376 | tf_op jit(solution)/shard_map/ppermute | solution.py:583
  53.6 8.9 %collective-permute-start.25 = (bf16[96,1152]{1,0:T(8,128)(2,1)S(1)}, bf16[96,1152]{1,0:T(8,128)(2,1)S(1)}, u32[]{:S(2)}, u32[]{:S(2)}) collective-permute-start(bf16[96,1152]{1,0:T(8,128)(2,1)S(1)} %collective-permute-done.18.refs_3_), channel_id=1, source_target_pairs={{0,8},{8,16},{16,24},{24,28},{28,20},{20,12},{12,4},{4,0},{1,9},{9... | collective-permute-start | bytes 663560 | tf_op jit(solution)/shard_map/ppermute | solution.py:579
  54.6 7.8 %collective-permute-start.24 = (bf16[512,192]{1,0:T(8,128)(2,1)S(1)}, bf16[512,192]{1,0:T(8,128)(2,1)S(1)}, u32[]{:S(2)}, u32[]{:S(2)}) collective-permute-start(bf16[512,192]{1,0:T(8,128)(2,1)S(1)} %get-tuple-element.259.c0.refs_9_.refs_6_.refs_5_), channel_id=1, source_target_pairs={{0,2},{1,3},{2,0},{3,1},{4,6},{5,7},{6,4},{7,5},{8,10},{9,11},{10,... | collective-permute-start | bytes 589832 | tf_op jit(solution)/shard_map/ppermute | solution.py:571
  55.1 7.1 %collective-permute-start.26 = (bf16[96,768]{1,0:T(8,128)(2,1)S(1)}, bf16[96,768]{1,0:T(8,128)(2,1)S(1)}, u32[]{:S(2)}, u32[]{:S(2)}) collective-permute-start(bf16[96,768]{1,0:T(8,128)(2,1)S(1)} %collective-permute-done.20.refs_2_), channel_id=1, source_target_pairs={{0,8},{8,16},{16,24},{24,28},{28,20},{20,12},{12,4},{4,0},{1,9},{9... | collective-permute-start | bytes 442376 | tf_op jit(solution)/shard_map/ppermute | solution.py:579
  56.1 6.3 %collective-permute-start.27 = (bf16[96,768]{1,0:T(8,128)(2,1)S(1)}, bf16[96,768]{1,0:T(8,128)(2,1)S(1)}, u32[]{:S(2)}, u32[]{:S(2)}) collective-permute-start(bf16[96,768]{1,0:T(8,128)(2,1)S(1)} %collective-permute-done.21.refs_6_), channel_id=1, source_target_pairs={{8,0},{16,8},{24,16},{28,24},{20,28},{12,20},{4,12},{0,4},{9,1},{1... | collective-permute-start | bytes 442376 | tf_op jit(solution)/shard_map/ppermute | solution.py:583
  57.2 6.8 %collective-permute-start.17 = (bf16[512,192]{1,0:T(8,128)(2,1)S(1)}, bf16[512,192]{1,0:T(8,128)(2,1)S(1)}, u32[]{:S(2)}, u32[]{:S(2)}) collective-permute-start(bf16[512,192]{1,0:T(8,128)(2,1)S(1)} %get-tuple-element.247.c0.refs_9_.refs_4_), channel_id=1, source_target_pairs={{0,1},{1,0},{2,3},{3,2},{4,5},{5,4},{6,7},{7,6},{8,9},{9,8},{10,11... | collective-permute-start | bytes 589832 | tf_op jit(solution)/shard_map/ppermute | solution.py:567
  62.3 1.7 %collective-permute-start.23 = (bf16[512,192]{1,0:T(8,128)(2,1)S(1)}, bf16[512,192]{1,0:T(8,128)(2,1)S(1)}, u32[]{:S(2)}, u32[]{:S(2)}) collective-permute-start(bf16[512,192]{1,0:T(8,128)(2,1)S(1)} %collective-permute-done.22.c2), channel_id=1, source_target_pairs={{0,1},{1,0},{2,3},{3,2},{4,5},{5,4},{6,7},{7,6},{8,9},{9,8},{10,11... | collective-permute-start | bytes 589832 | tf_op jit(solution)/shard_map/ppermute | solution.py:567
  62.9 2.3 %collective-permute-start.29 = (bf16[192,768]{1,0:T(8,128)(2,1)S(1)}, bf16[192,768]{1,0:T(8,128)(2,1)S(1)}, u32[]{:S(2)}, u32[]{:S(2)}) collective-permute-start(bf16[192,768]{1,0:T(8,128)(2,1)S(1)} %get-tuple-element.268.w2), channel_id=1, source_target_pairs={{0,1},{1,0},{2,3},{3,2},{4,5},{5,4},{6,7},{7,6},{8,9},{9,8},{10,11... | collective-permute-start | bytes 884744 | tf_op jit(solution)/shard_map/ppermute | solution.py:567
  63.4 1.7 %collective-permute-start.28 = (bf16[192,768]{1,0:T(8,128)(2,1)S(1)}, bf16[192,768]{1,0:T(8,128)(2,1)S(1)}, u32[]{:S(2)}, u32[]{:S(2)}) collective-permute-start(bf16[192,768]{1,0:T(8,128)(2,1)S(1)} %get-tuple-element.267.w0.refs_7_.refs_4_), channel_id=1, source_target_pairs={{0,1},{1,0},{2,3},{3,2},{4,5},{5,4},{6,7},{7,6},{8,9},{9,8},{10,11... | collective-permute-start | bytes 884744 | tf_op jit(solution)/shard_map/ppermute | solution.py:567
  63.5 5.1 %collective-permute-start.30 = (bf16[512,192]{1,0:T(8,128)(2,1)S(1)}, bf16[512,192]{1,0:T(8,128)(2,1)S(1)}, u32[]{:S(2)}, u32[]{:S(2)}) collective-permute-start(bf16[512,192]{1,0:T(8,128)(2,1)S(1)} %get-tuple-element.259.c0.refs_9_.refs_6_.refs_5_), channel_id=1, source_target_pairs={{0,1},{1,0},{2,3},{3,2},{4,5},{5,4},{6,7},{7,6},{8,9},{9,8},{10,11... | collective-permute-start | bytes 589832 | tf_op jit(solution)/shard_map/ppermute | solution.py:567
  63.9 4.6 %collective-permute-start.31 = (bf16[512,192]{1,0:T(8,128)(2,1)S(1)}, bf16[512,192]{1,0:T(8,128)(2,1)S(1)}, u32[]{:S(2)}, u32[]{:S(2)}) collective-permute-start(bf16[512,192]{1,0:T(8,128)(2,1)S(1)} %collective-permute-done.24.c2), channel_id=1, source_target_pairs={{0,1},{1,0},{2,3},{3,2},{4,5},{5,4},{6,7},{7,6},{8,9},{9,8},{10,11... | collective-permute-start | bytes 589832 | tf_op jit(solution)/shard_map/ppermute | solution.py:567
  64.0 7.9 %collective-permute-start.32 = (bf16[96,768]{1,0:T(8,128)(2,1)S(1)}, bf16[96,768]{1,0:T(8,128)(2,1)S(1)}, u32[]{:S(2)}, u32[]{:S(2)}) collective-permute-start(bf16[96,768]{1,0:T(8,128)(2,1)S(1)} %collective-permute-done.26.refs_3_), channel_id=1, source_target_pairs={{0,8},{8,16},{16,24},{24,28},{28,20},{20,12},{12,4},{4,0},{1,9},{9... | collective-permute-start | bytes 442376 | tf_op jit(solution)/shard_map/ppermute | solution.py:579
  73.7 2.2 %collective-permute-start.33 = (bf16[128,768]{1,0:T(8,128)(2,1)S(1)}, bf16[128,768]{1,0:T(8,128)(2,1)S(1)}, u32[]{:S(2)}, u32[]{:S(2)}) collective-permute-start(bf16[128,768]{1,0:T(8,128)(2,1)S(1)} %get-tuple-element.290), channel_id=1, source_target_pairs={{0,1},{1,0},{2,3},{3,2},{4,5},{5,4},{6,7},{7,6},{8,9},{9,8},{10,11... | collective-permute-start | bytes 589832 | tf_op jit(solution)/shard_map/ppermute | solution.py:567
  74.0 1.9 %collective-permute-start.34 = (bf16[128,768]{1,0:T(8,128)(2,1)S(1)}, bf16[128,768]{1,0:T(8,128)(2,1)S(1)}, u32[]{:S(2)}, u32[]{:S(2)}) collective-permute-start(bf16[128,768]{1,0:T(8,128)(2,1)S(1)} %get-tuple-element.291), channel_id=1, source_target_pairs={{0,1},{1,0},{2,3},{3,2},{4,5},{5,4},{6,7},{7,6},{8,9},{9,8},{10,11... | collective-permute-start | bytes 589832 | tf_op jit(solution)/shard_map/ppermute | solution.py:567
  75.9 11.4 %collective-permute-start.39 = (bf16[256,768]{1,0:T(8,128)(2,1)S(1)}, bf16[256,768]{1,0:T(8,128)(2,1)S(1)}, u32[]{:S(2)}, u32[]{:S(2)}) collective-permute-start(bf16[256,768]{1,0:T(8,128)(2,1)S(1)} %add0.1.refs_1_), channel_id=1, source_target_pairs={{0,2},{1,3},{2,0},{3,1},{4,6},{5,7},{6,4},{7,5},{8,10},{9,11},{10,... | collective-permute-start | bytes 1179656 | tf_op jit(solution)/shard_map/ppermute | solution.py:571
  76.5 5.3 %collective-permute-start.35 = (bf16[128,768]{1,0:T(8,128)(2,1)S(1)}, bf16[128,768]{1,0:T(8,128)(2,1)S(1)}, u32[]{:S(2)}, u32[]{:S(2)}) collective-permute-start(bf16[128,768]{1,0:T(8,128)(2,1)S(1)} %get-tuple-element.297), channel_id=1, source_target_pairs={{0,1},{1,0},{2,3},{3,2},{4,5},{5,4},{6,7},{7,6},{8,9},{9,8},{10,11... | collective-permute-start | bytes 589832 | tf_op jit(solution)/shard_map/ppermute | solution.py:567
  76.5 5.3 %collective-permute-start.36 = (bf16[128,768]{1,0:T(8,128)(2,1)S(1)}, bf16[128,768]{1,0:T(8,128)(2,1)S(1)}, u32[]{:S(2)}, u32[]{:S(2)}) collective-permute-start(bf16[128,768]{1,0:T(8,128)(2,1)S(1)} %get-tuple-element.298), channel_id=1, source_target_pairs={{0,1},{1,0},{2,3},{3,2},{4,5},{5,4},{6,7},{7,6},{8,9},{9,8},{10,11... | collective-permute-start | bytes 589832 | tf_op jit(solution)/shard_map/ppermute | solution.py:567
  79.7 12.8 %collective-permute-start.37 = (bf16[96,1536]{1,0:T(8,128)(2,1)S(1)}, bf16[96,1536]{1,0:T(8,128)(2,1)S(1)}, u32[]{:S(2)}, u32[]{:S(2)}) collective-permute-start(bf16[96,1536]{1,0:T(8,128)(2,1)S(1)} %get-tuple-element.299), channel_id=1, source_target_pairs={{0,8},{8,16},{16,24},{24,28},{28,20},{20,12},{12,4},{4,0},{1,9},{9... | collective-permute-start | bytes 884744 | tf_op jit(solution)/shard_map/ppermute | solution.py:579
  80.6 11.9 %collective-permute-start.38 = (bf16[96,1536]{1,0:T(8,128)(2,1)S(1)}, bf16[96,1536]{1,0:T(8,128)(2,1)S(1)}, u32[]{:S(2)}, u32[]{:S(2)}) collective-permute-start(bf16[96,1536]{1,0:T(8,128)(2,1)S(1)} %get-tuple-element.300), channel_id=1, source_target_pairs={{8,0},{16,8},{24,16},{28,24},{20,28},{12,20},{4,12},{0,4},{9,1},{1... | collective-permute-start | bytes 884744 | tf_op jit(solution)/shard_map/ppermute | solution.py:583
  87.9 1.7 %collective-permute-start.41 = (bf16[128,768]{1,0:T(8,128)(2,1)S(1)}, bf16[128,768]{1,0:T(8,128)(2,1)S(1)}, u32[]{:S(2)}, u32[]{:S(2)}) collective-permute-start(bf16[128,768]{1,0:T(8,128)(2,1)S(1)} %get-tuple-element.308.refs_4_), channel_id=1, source_target_pairs={{0,1},{1,0},{2,3},{3,2},{4,5},{5,4},{6,7},{7,6},{8,9},{9,8},{10,11... | collective-permute-start | bytes 589832 | tf_op jit(solution)/shard_map/ppermute | solution.py:567
  88.4 11.1 %collective-permute-start.42 = (bf16[256,768]{1,0:T(8,128)(2,1)S(1)}, bf16[256,768]{1,0:T(8,128)(2,1)S(1)}, u32[]{:S(2)}, u32[]{:S(2)}) collective-permute-start(bf16[256,768]{1,0:T(8,128)(2,1)S(1)} %add1.1.refs_1_), channel_id=1, source_target_pairs={{0,2},{1,3},{2,0},{3,1},{4,6},{5,7},{6,4},{7,5},{8,10},{9,11},{10,... | collective-permute-start | bytes 1179656 | tf_op jit(solution)/shard_map/ppermute | solution.py:571
  92.5 7.6 %collective-permute-start.49 = (bf16[256,768]{1,0:T(8,128)(2,1)S(1)}, bf16[256,768]{1,0:T(8,128)(2,1)S(1)}, u32[]{:S(2)}, u32[]{:S(2)}) collective-permute-start(bf16[256,768]{1,0:T(8,128)(2,1)S(1)} %get-tuple-element.347), channel_id=1, source_target_pairs={{0,1},{1,0},{2,3},{3,2},{4,5},{5,4},{6,7},{7,6},{8,9},{9,8},{10,11... | collective-permute-start | bytes 1179656 | tf_op jit(solution)/shard_map/ppermute | solution.py:567
  92.8 7.9 %collective-permute-start.50 = (bf16[256,768]{1,0:T(8,128)(2,1)S(1)}, bf16[256,768]{1,0:T(8,128)(2,1)S(1)}, u32[]{:S(2)}, u32[]{:S(2)}) collective-permute-start(bf16[256,768]{1,0:T(8,128)(2,1)S(1)} %get-tuple-element.314), channel_id=1, source_target_pairs={{0,1},{1,0},{2,3},{3,2},{4,5},{5,4},{6,7},{7,6},{8,9},{9,8},{10,11... | collective-permute-start | bytes 1179656 | tf_op jit(solution)/shard_map/ppermute | solution.py:567
  93.3 11.2 %collective-permute-start.45 = (bf16[96,1536]{1,0:T(8,128)(2,1)S(1)}, bf16[96,1536]{1,0:T(8,128)(2,1)S(1)}, u32[]{:S(2)}, u32[]{:S(2)}) collective-permute-start(bf16[96,1536]{1,0:T(8,128)(2,1)S(1)} %get-tuple-element.325), channel_id=1, source_target_pairs={{0,8},{8,16},{16,24},{24,28},{28,20},{20,12},{12,4},{4,0},{1,9},{9... | collective-permute-start | bytes 884744 | tf_op jit(solution)/shard_map/ppermute | solution.py:579
  94.3 10.2 %collective-permute-start.46 = (bf16[96,1536]{1,0:T(8,128)(2,1)S(1)}, bf16[96,1536]{1,0:T(8,128)(2,1)S(1)}, u32[]{:S(2)}, u32[]{:S(2)}) collective-permute-start(bf16[96,1536]{1,0:T(8,128)(2,1)S(1)} %get-tuple-element.326), channel_id=1, source_target_pairs={{8,0},{16,8},{24,16},{28,24},{20,28},{12,20},{4,12},{0,4},{9,1},{1... | collective-permute-start | bytes 884744 | tf_op jit(solution)/shard_map/ppermute | solution.py:583
  100.9 13.5 %collective-permute-start.51 = (bf16[256,768]{1,0:T(8,128)(2,1)S(1)}, bf16[256,768]{1,0:T(8,128)(2,1)S(1)}, u32[]{:S(2)}, u32[]{:S(2)}) collective-permute-start(bf16[256,768]{1,0:T(8,128)(2,1)S(1)} %get-tuple-element.350), channel_id=1, source_target_pairs={{0,2},{1,3},{2,0},{3,1},{4,6},{5,7},{6,4},{7,5},{8,10},{9,11},{10,... | collective-permute-start | bytes 1179656 | tf_op jit(solution)/shard_map/ppermute | solution.py:571
  104.6 9.3 %collective-permute-start.48 = (bf16[96,1536]{1,0:T(8,128)(2,1)S(1)}, bf16[96,1536]{1,0:T(8,128)(2,1)S(1)}, u32[]{:S(2)}, u32[]{:S(2)}) collective-permute-start(bf16[96,1536]{1,0:T(8,128)(2,1)S(1)} %get-tuple-element.342), channel_id=1, source_target_pairs={{8,0},{16,8},{24,16},{28,24},{20,28},{12,20},{4,12},{0,4},{9,1},{1... | collective-permute-start | bytes 884744 | tf_op jit(solution)/shard_map/ppermute | solution.py:583
  105.6 8.9 %collective-permute-start.47 = (bf16[96,1536]{1,0:T(8,128)(2,1)S(1)}, bf16[96,1536]{1,0:T(8,128)(2,1)S(1)}, u32[]{:S(2)}, u32[]{:S(2)}) collective-permute-start(bf16[96,1536]{1,0:T(8,128)(2,1)S(1)} %get-tuple-element.330), channel_id=1, source_target_pairs={{0,8},{8,16},{16,24},{24,28},{28,20},{20,12},{12,4},{4,0},{1,9},{9... | collective-permute-start | bytes 884744 | tf_op jit(solution)/shard_map/ppermute | solution.py:579
  111.3 6.4 %collective-permute-start.54 = (bf16[256,768]{1,0:T(8,128)(2,1)S(1)}, bf16[256,768]{1,0:T(8,128)(2,1)S(1)}, u32[]{:S(2)}, u32[]{:S(2)}) collective-permute-start(bf16[256,768]{1,0:T(8,128)(2,1)S(1)} %get-tuple-element.354), channel_id=1, source_target_pairs={{0,1},{1,0},{2,3},{3,2},{4,5},{5,4},{6,7},{7,6},{8,9},{9,8},{10,11... | collective-permute-start | bytes 1179656 | tf_op jit(solution)/shard_map/ppermute | solution.py:567
  111.4 7.1 %collective-permute-start.55 = (bf16[256,768]{1,0:T(8,128)(2,1)S(1)}, bf16[256,768]{1,0:T(8,128)(2,1)S(1)}, u32[]{:S(2)}, u32[]{:S(2)}) collective-permute-start(bf16[256,768]{1,0:T(8,128)(2,1)S(1)} %get-tuple-element.355), channel_id=1, source_target_pairs={{0,1},{1,0},{2,3},{3,2},{4,5},{5,4},{6,7},{7,6},{8,9},{9,8},{10,11... | collective-permute-start | bytes 1179656 | tf_op jit(solution)/shard_map/ppermute | solution.py:567
  114.4 7.3 %collective-permute-start.52 = (bf16[96,896]{1,0:T(8,128)(2,1)S(1)}, bf16[96,896]{1,0:T(8,128)(2,1)S(1)}, u32[]{:S(2)}, u32[]{:S(2)}) collective-permute-start(bf16[96,896]{1,0:T(8,128)(2,1)S(1)} %get-tuple-element.351), channel_id=1, source_target_pairs={{0,8},{8,16},{16,24},{24,28},{28,20},{20,12},{12,4},{4,0},{1,9},{9... | collective-permute-start | bytes 516104 | tf_op jit(solution)/shard_map/ppermute | solution.py:579
  115.6 6.1 %collective-permute-start.53 = (bf16[96,896]{1,0:T(8,128)(2,1)S(1)}, bf16[96,896]{1,0:T(8,128)(2,1)S(1)}, u32[]{:S(2)}, u32[]{:S(2)}) collective-permute-start(bf16[96,896]{1,0:T(8,128)(2,1)S(1)} %get-tuple-element.352), channel_id=1, source_target_pairs={{8,0},{16,8},{24,16},{28,24},{20,28},{12,20},{4,12},{0,4},{9,1},{1... | collective-permute-start | bytes 516104 | tf_op jit(solution)/shard_map/ppermute | solution.py:583
  116.5 11.5 %collective-permute-start.58 = (bf16[96,1536]{1,0:T(8,128)(2,1)S(1)}, bf16[96,1536]{1,0:T(8,128)(2,1)S(1)}, u32[]{:S(2)}, u32[]{:S(2)}) collective-permute-start(bf16[96,1536]{1,0:T(8,128)(2,1)S(1)} %mlp_hop1.1), channel_id=1, source_target_pairs={{0,8},{8,16},{16,24},{24,28},{28,20},{20,12},{12,4},{4,0},{1,9},{9... | collective-permute-start | bytes 884744 | tf_op jit(solution)/shard_map/ppermute | solution.py:579
  117.8 16.5 %collective-permute-start.62 = (bf16[192,1024]{1,0:T(8,128)(2,1)S(1)}, bf16[192,1024]{1,0:T(8,128)(2,1)S(1)}, u32[]{:S(2)}, u32[]{:S(2)}) collective-permute-start(bf16[192,1024]{1,0:T(8,128)(2,1)S(1)} %get-tuple-element.380.refs_1_), channel_id=1, source_target_pairs={{0,2},{1,3},{2,0},{3,1},{4,6},{5,7},{6,4},{7,5},{8,10},{9,11},{10,... | collective-permute-start | bytes 1179656 | tf_op jit(solution)/shard_map/ppermute | solution.py:571
  118.7 17.2 %collective-permute-start.61 = (bf16[256,768]{1,0:T(8,128)(2,1)S(1)}, bf16[256,768]{1,0:T(8,128)(2,1)S(1)}, u32[]{:S(2)}, u32[]{:S(2)}) collective-permute-start(bf16[256,768]{1,0:T(8,128)(2,1)S(1)} %get-tuple-element.356), channel_id=1, source_target_pairs={{0,2},{1,3},{2,0},{3,1},{4,6},{5,7},{6,4},{7,5},{8,10},{9,11},{10,... | collective-permute-start | bytes 1179656 | tf_op jit(solution)/shard_map/ppermute | solution.py:571
  121.8 8.6 %collective-permute-start.56 = (bf16[96,896]{1,0:T(8,128)(2,1)S(1)}, bf16[96,896]{1,0:T(8,128)(2,1)S(1)}, u32[]{:S(2)}, u32[]{:S(2)}) collective-permute-start(bf16[96,896]{1,0:T(8,128)(2,1)S(1)} %get-tuple-element.359), channel_id=1, source_target_pairs={{0,8},{8,16},{16,24},{24,28},{28,20},{20,12},{12,4},{4,0},{1,9},{9... | collective-permute-start | bytes 516104 | tf_op jit(solution)/shard_map/ppermute | solution.py:579
  123.1 7.4 %collective-permute-start.57 = (bf16[96,896]{1,0:T(8,128)(2,1)S(1)}, bf16[96,896]{1,0:T(8,128)(2,1)S(1)}, u32[]{:S(2)}, u32[]{:S(2)}) collective-permute-start(bf16[96,896]{1,0:T(8,128)(2,1)S(1)} %get-tuple-element.360), channel_id=1, source_target_pairs={{8,0},{16,8},{24,16},{28,24},{20,28},{12,20},{4,12},{0,4},{9,1},{1... | collective-permute-start | bytes 516104 | tf_op jit(solution)/shard_map/ppermute | solution.py:583
  130.5 5.5 %collective-permute-start.59 = (bf16[96,896]{1,0:T(8,128)(2,1)S(1)}, bf16[96,896]{1,0:T(8,128)(2,1)S(1)}, u32[]{:S(2)}, u32[]{:S(2)}) collective-permute-start(bf16[96,896]{1,0:T(8,128)(2,1)S(1)} %get-tuple-element.367), channel_id=1, source_target_pairs={{0,8},{8,16},{16,24},{24,28},{28,20},{20,12},{12,4},{4,0},{1,9},{9... | collective-permute-start | bytes 516104 | tf_op jit(solution)/shard_map/ppermute | solution.py:579
  131.6 5.4 %collective-permute-start.60 = (bf16[96,896]{1,0:T(8,128)(2,1)S(1)}, bf16[96,896]{1,0:T(8,128)(2,1)S(1)}, u32[]{:S(2)}, u32[]{:S(2)}) collective-permute-start(bf16[96,896]{1,0:T(8,128)(2,1)S(1)} %get-tuple-element.368), channel_id=1, source_target_pairs={{8,0},{16,8},{24,16},{28,24},{20,28},{12,20},{4,12},{0,4},{9,1},{1... | collective-permute-start | bytes 516104 | tf_op jit(solution)/shard_map/ppermute | solution.py:583
  137.0 3.0 %collective-permute-start.64 = (bf16[192,1024]{1,0:T(8,128)(2,1)S(1)}, bf16[192,1024]{1,0:T(8,128)(2,1)S(1)}, u32[]{:S(2)}, u32[]{:S(2)}) collective-permute-start(bf16[192,1024]{1,0:T(8,128)(2,1)S(1)} %get-tuple-element.380.refs_1_), channel_id=1, source_target_pairs={{0,1},{1,0},{2,3},{3,2},{4,5},{5,4},{6,7},{7,6},{8,9},{9,8},{10,11... | collective-permute-start | bytes 1179656 | tf_op jit(solution)/shard_map/ppermute | solution.py:567
  137.0 3.0 %collective-permute-start.65 = (bf16[192,1024]{1,0:T(8,128)(2,1)S(1)}, bf16[192,1024]{1,0:T(8,128)(2,1)S(1)}, u32[]{:S(2)}, u32[]{:S(2)}) collective-permute-start(bf16[192,1024]{1,0:T(8,128)(2,1)S(1)} %collective-permute-done.62.refs_3_), channel_id=1, source_target_pairs={{0,1},{1,0},{2,3},{3,2},{4,5},{5,4},{6,7},{7,6},{8,9},{9,8},{10,11... | collective-permute-start | bytes 1179656 | tf_op jit(solution)/shard_map/ppermute | solution.py:567
  137.6 6.3 %collective-permute-start.63 = (bf16[96,896]{1,0:T(8,128)(2,1)S(1)}, bf16[96,896]{1,0:T(8,128)(2,1)S(1)}, u32[]{:S(2)}, u32[]{:S(2)}) collective-permute-start(bf16[96,896]{1,0:T(8,128)(2,1)S(1)} %qkv_hop1.1), channel_id=1, source_target_pairs={{0,8},{8,16},{16,24},{24,28},{28,20},{20,12},{12,4},{4,0},{1,9},{9... | collective-permute-start | bytes 516104 | tf_op jit(solution)/shard_map/ppermute | solution.py:579
  145.2 3.6 %collective-permute-start.67 = (f32[8,128]{1,0:T(8,128)S(1)}, f32[8,128]{1,0:T(8,128)S(1)}, u32[]{:S(2)}, u32[]{:S(2)}) collective-permute-start(f32[8,128]{1,0:T(8,128)S(1)} %sum.1.sums), channel_id=1, source_target_pairs={{0,2},{1,3},{2,0},{3,1},{4,6},{5,7},{6,4},{7,5},{8,10},{9,11},{10,... | collective-permute-start | bytes 12296 | tf_op jit(solution)/shard_map/ppermute | solution.py:571
  (28 other events, 189.1 us)

commit v2 on v1

--- a/solution.py
+++ b/solution.py
@@ -335,37 +335,33 @@
     )
 
 
-def norm_two_kernel(part, info, r_ref, own, received, e_ref, norm_ref, dr_ref, top, bottom):
+def norm_two_kernel(part, info, r_ref, own, received, e_ref, norm_ref, dr_ref, ab_ref):
     unit, scale = norm_stats(r_ref[block(info[0]), :])
     grad = own[...].astype(f32) + received[...].astype(f32)
     e = e_ref[block(2 * part + info[0]), :].astype(f32)
     dr = e + norm_back(unit, scale, norm_ref[2:3], grad)
     dr_ref[...] = dr
-    top[...] = dr[: RB // 2].astype(bf16)
-    bottom[...] = dr[RB // 2 :].astype(bf16)
+    ab_ref[...] = dr.astype(bf16)
 
 
 def attend_back_kernel(heads, base, blocks, stage, info, src, m_ref, v_ref, *refs):
     if stage < 2:
-        halves, refs = refs[:4], refs[4:]
+        ab_in, refs = refs[0], refs[1:]
     else:
         ab_in, refs = refs[0], refs[1:]
     wp, lse_ref, c_ref, *refs = refs
     if stage:
         dk_in, dv_in, *refs = refs
     if stage == 0:
-        ab_ref, dq_ref, dk_ref, dv_ref = refs
+        dq_ref, dk_ref, dv_ref = refs
     elif stage == 1:
-        ab_ref, dq_ref, dk_ref, dv_ref = refs
+        dq_ref, dk_ref, dv_ref = refs
     else:
         dq_first, dq_second, dm_ref, dvr_ref = refs
     keep = masked_tile()
     core = info[0]
     if stage < 2:
-        for k in range(2):
-            ab_ref[block(2 * core + k, RB // 2), :] = halves[k][...]
-            ab_ref[block(2 * (1 - core) + k, RB // 2), :] = halves[2 + k][...]
-        source, skip = ab_ref, 0
+        source, skip = ab_in, 0
     else:
         source, skip = ab_in, ab_in.shape[0] - blocks * RB
     top = base + blocks * RB
@@ -571,6 +567,10 @@
     return lax.ppermute(value, "mp", [(i, i ^ 2) for i in range(4)])
 
 
+def both_cores(value):
+    return lax.all_gather(value, "mp", axis_index_groups=[[0, 1], [2, 3]], axis=0, tiled=True)
+
+
 FORWARD = [(RING[i], RING[(i + 1) % 8]) for i in range(8)]
 BACKWARD = [(b, a) for a, b in FORWARD]
 
@@ -898,7 +898,7 @@
             f"norm_two{part}",
             (info,),
             [resid[part], mine, across, grad_out, norms],
-            [((RB, width), f32)] + [((RB // 2, width), bf16)] * 2,
+            [((RB, width), f32), ((RB, width), bf16)],
         )
 
     def attend_back(stage, base, blocks, given, part, before, outs):
@@ -914,10 +914,10 @@
     ysend_a, ykeep_a = mlp_out(0, mine_b)
     ysend_b, ykeep_b = mlp_out(1, mine_b)
     across_a, ysend_a, ysend_b = fence(across_a, ysend_a, ysend_b)
-    dr_a, *ab_a = norm_two(0, after(mine_a, mine_b), across_a)
-    partner = [swap_core(v) for v in ab_a]
-    ab_one, dq_a, dk, dv = attend_back(
-        0, 0, 2, [*ab_a, *partner], 0, [], [((half, width), bf16)] + [((half, cw), f32)] * 3
+    dr_a, ab_a = norm_two(0, after(mine_a, mine_b), across_a)
+    ab_one = both_cores(ab_a)
+    dq_a, dk, dv = attend_back(
+        0, 0, 2, [ab_one], 0, [], [((half, cw), f32)] * 3
     )
     mlp_sum.a, mlp_sum.b, dq_a = fence(mlp_sum.a, mlp_sum.b, dq_a)
     mlp_sum.step()
@@ -930,12 +930,12 @@
         [ykeep_a, ykeep_b, yreceived_a, yreceived_b],
         [((RB, width), f32), ((RB, width), bf16)],
     )
-    dr_b, *ab_b = norm_two(1, after(mine_b, ysend_b), across_b)
-    partner = [swap_core(v) for v in ab_b]
+    dr_b, ab_b = norm_two(1, after(mine_b, ysend_b), across_b)
+    ab_two = both_cores(ab_b)
     rows_received = swap_x(after(rows_sent, dr_b))
     top = half + RB
-    ab_two, dq_b, dk, dv = attend_back(
-        1, half, 1, [*ab_b, *partner], 1, [dk, dv], [((half, width), bf16), ((RB, cw), f32)] + [((top, cw), f32)] * 2
+    dq_b, dk, dv = attend_back(
+        1, half, 1, [ab_two], 1, [dk, dv], [((RB, cw), f32)] + [((top, cw), f32)] * 2
     )
     mlp_sum.a, mlp_sum.b, dq_b = fence(mlp_sum.a, mlp_sum.b, dq_b)
     mlp_sum.step()

time: 150 us -> 149 us (level)
  blocking collectives: 0 us -> 4.95 us
  waiting for transfers between devices: 42.8 us -> 38.5 us
    all_gather x0 -> x2, blocking collectives: none -> 4.95 us  [both_cores(): lax.all_gather(value, 'mp', axis_index_groups=[[0, 1], [2, 3]], axis=0, t...]
    ppermute x10, waiting for transfers between devices: 11.2 us -> 6.92 us  [swap_x(): return lax.ppermute(value, 'mp', [(i, i ^ 2) for i in range(4)])]
    ppermute x23 -> x19, starting transfers between devices: 5.1 us -> 3.97 us  [swap_core(): return lax.ppermute(value, 'mp', [(i, i ^ 1) for i in range(4)])]
  transfers between devices with their start and end apart: 68 -> 64, of which waited for: 30 -> 26; matrix products, arithmetic and copies ran while one was open for 0% -> 0% of each run, Pallas kernels for 32% -> 32%
where the time goes in v2:
time: 149 us
  Pallas kernels  52.6 us (35%)
  starting transfers between devices  50.5 us (34%)
  waiting for transfers between devices  38.5 us (26%)
  blocking collectives  4.95 us (3%)
  local copies, waits for them, and re-layouts  1.51 us (1%)
    pallas_call x43, Pallas kernels, call(): pl.pallas_call(kernel, in_specs=[smem] * len(scalars) + [given] * len(ins...  52.6 us
    ppermute x20, starting transfers between devices, ahead(): return lax.ppermute(value, 'dp', FORWARD)  26.1 us
    ppermute x20, waiting for transfers between devices, ahead(): return lax.ppermute(value, 'dp', FORWARD)  21.7 us
    ppermute x15, starting transfers between devices, behind(): return lax.ppermute(value, 'dp', BACKWARD)  11.3 us
    ppermute x10, starting transfers between devices, swap_x(): return lax.ppermute(value, 'mp', [(i, i ^ 2) for i in range(4)])  9.16 us
    ppermute x15, waiting for transfers between devices, behind(): return lax.ppermute(value, 'dp', BACKWARD)  8.65 us
    ppermute x10, waiting for transfers between devices, swap_x(): return lax.ppermute(value, 'mp', [(i, i ^ 2) for i in range(4)])  6.92 us
    all_gather x2, blocking collectives, both_cores(): lax.all_gather(value, 'mp', axis_index_groups=[[0, 1], [2, 3]], axis=0, t...  4.95 us
  transfers between devices with their start and end apart: 64, of which 26 were waited for; matrix products, arithmetic and copies ran while one was open for 0% of the time, Pallas kernels for 32%

profile of v2, /device:TPU:0, one launch (start us, length us, event | category | flops | bytes accessed | tf_op | source)
XLA Modules:
  0.0 149.3 jit_solution(13946927438346709958)
XLA Ops:
  0.7 1.8 %prep_one.1.refs_1_ = bf16[96,640]{1,0:T(8,128)(2,1)} custom-call(f32[96,576]{1,0:T(8,128)} %refs_3_.3, f32[4,96]{1,0:T(4,128)} %w.1), custom_call_target="tpu_custom_call" | custom-call | flops 1 | bytes 1 | tf_op jit(solution)/shard_map/prep_one/pallas_call | solution.py:65
  2.4 3.1 %collective-permute-start = (bf16[96,640]{1,0:T(8,128)(2,1)}, bf16[96,640]{1,0:T(8,128)(2,1)S(1)}, u32[]{:S(2)}, u32[]{:S(2)}) collective-permute-start(bf16[96,640]{1,0:T(8,128)(2,1)} %prep_one.1.refs_1_), channel_id=1, source_target_pairs={{0,8},{8,16},{16,24},{24,28},{28,20},{20,12},{12,4},{4,0},{1,9},{9... | collective-permute-start | bytes 368648 | tf_op jit(solution)/shard_map/ppermute | solution.py:579
  5.5 1.9 %prep_two.1 = (bf16[96,192]{1,0:T(8,128)(2,1)}, bf16[96,768]{1,0:T(8,128)(2,1)}, bf16[96,768]{1,0:T(8,128)(2,1)}) custom-call(f32[192,96]{1,0:T(8,128)} %refs_6_.1, f32[96,768]{1,0:T(8,128)} %refs_3_.2, f32[96,768]{1,0:T(8,128)} %bitcast.8), custom_call_target="tpu_custom_call" | custom-call | flops 1 | bytes 1 | tf_op jit(solution)/shard_map/prep_two/pallas_call | solution.py:65
  7.4 1.6 %collective-permute-done.refs_2_ = bf16[96,640]{1,0:T(8,128)(2,1)S(1)} collective-permute-done((bf16[96,640]{1,0:T(8,128)(2,1)}, bf16[96,640]{1,0:T(8,128)(2,1)S(1)}, u32[]{:S(2)}, u32[]{:S(2)}) %collective-permute-start) | collective-permute-done | bytes 122912 | tf_op jit(solution)/shard_map/ppermute | solution.py:579
  9.0 1.6 %collective-permute-done.1.refs_6_ = bf16[96,640]{1,0:T(8,128)(2,1)S(1)} collective-permute-done((bf16[96,640]{1,0:T(8,128)(2,1)}, bf16[96,640]{1,0:T(8,128)(2,1)S(1)}, u32[]{:S(2)}, u32[]{:S(2)}) %collective-permute-start.1) | collective-permute-done | bytes 122912 | tf_op jit(solution)/shard_map/ppermute | solution.py:583
  10.6 1.6 %collective-permute-start.2 = (bf16[96,640]{1,0:T(8,128)(2,1)S(1)}, bf16[96,640]{1,0:T(8,128)(2,1)S(1)}, u32[]{:S(2)}, u32[]{:S(2)}) collective-permute-start(bf16[96,640]{1,0:T(8,128)(2,1)S(1)} %collective-permute-done.refs_2_), channel_id=1, source_target_pairs={{0,8},{8,16},{16,24},{24,28},{28,20},{20,12},{12,4},{4,0},{1,9},{9... | collective-permute-start | bytes 368648 | tf_op jit(solution)/shard_map/ppermute | solution.py:579
  12.6 1.5 collective-permute-start.4
  14.1 1.4 copy-done
  17.1 1.5 collective-permute-start.10
  18.6 1.6 %collective-permute-start.5 = (bf16[96,640]{1,0:T(8,128)(2,1)S(1)}, bf16[96,640]{1,0:T(8,128)(2,1)S(1)}, u32[]{:S(2)}, u32[]{:S(2)}) collective-permute-start(bf16[96,640]{1,0:T(8,128)(2,1)S(1)} %collective-permute-done.2.refs_3_), channel_id=1, source_target_pairs={{0,8},{8,16},{16,24},{24,28},{28,20},{20,12},{12,4},{4,0},{1,9},{9... | collective-permute-start | bytes 368648 | tf_op jit(solution)/shard_map/ppermute | solution.py:579
  20.7 1.6 %collective-permute-start.8 = (bf16[96,1152]{1,0:T(8,128)(2,1)S(1)}, bf16[96,1152]{1,0:T(8,128)(2,1)S(1)}, u32[]{:S(2)}, u32[]{:S(2)}) collective-permute-start(bf16[96,1152]{1,0:T(8,128)(2,1)S(1)} %join.1.refs_0_), channel_id=1, source_target_pairs={{0,8},{8,16},{16,24},{24,28},{28,20},{20,12},{12,4},{4,0},{1,9},{9... | collective-permute-start | bytes 663560 | tf_op jit(solution)/shard_map/ppermute | solution.py:579
  22.8 1.0 collective-permute-done.5.refs_4_
  23.7 1.3 collective-permute-done.6.refs_8_
  25.0 1.5 %collective-permute-start.7 = (bf16[96,640]{1,0:T(8,128)(2,1)S(1)}, bf16[96,640]{1,0:T(8,128)(2,1)S(1)}, u32[]{:S(2)}, u32[]{:S(2)}) collective-permute-start(bf16[96,640]{1,0:T(8,128)(2,1)S(1)} %collective-permute-done.5.refs_4_), channel_id=1, source_target_pairs={{0,8},{8,16},{16,24},{24,28},{28,20},{20,12},{12,4},{4,0},{1,9},{9... | collective-permute-start | bytes 368648 | tf_op jit(solution)/shard_map/ppermute | solution.py:579
  26.7 1.6 %collective-permute-done.9.refs_5_ = bf16[96,1152]{1,0:T(8,128)(2,1)S(1)} collective-permute-done((bf16[96,1152]{1,0:T(8,128)(2,1)S(1)}, bf16[96,1152]{1,0:T(8,128)(2,1)S(1)}, u32[]{:S(2)}, u32[]{:S(2)}) %collective-permute-start.9) | collective-permute-done | bytes 221216 | tf_op jit(solution)/shard_map/ppermute | solution.py:583
  28.2 1.7 %collective-permute-done.7.refs_5_ = bf16[96,640]{1,0:T(8,128)(2,1)S(1)} collective-permute-done((bf16[96,640]{1,0:T(8,128)(2,1)S(1)}, bf16[96,640]{1,0:T(8,128)(2,1)S(1)}, u32[]{:S(2)}, u32[]{:S(2)}) %collective-permute-start.7) | collective-permute-done | bytes 122912 | tf_op jit(solution)/shard_map/ppermute | solution.py:579
  29.9 1.6 %collective-permute-start.13 = (bf16[96,1152]{1,0:T(8,128)(2,1)S(1)}, bf16[96,1152]{1,0:T(8,128)(2,1)S(1)}, u32[]{:S(2)}, u32[]{:S(2)}) collective-permute-start(bf16[96,1152]{1,0:T(8,128)(2,1)S(1)} %collective-permute-done.8.refs_1_), channel_id=1, source_target_pairs={{0,8},{8,16},{16,24},{24,28},{28,20},{20,12},{12,4},{4,0},{1,9},{9... | collective-permute-start | bytes 663560 | tf_op jit(solution)/shard_map/ppermute | solution.py:579
  32.0 1.5 %collective-permute-start.15 = (bf16[96,768]{1,0:T(8,128)(2,1)S(1)}, bf16[96,768]{1,0:T(8,128)(2,1)S(1)}, u32[]{:S(2)}, u32[]{:S(2)}) collective-permute-start(bf16[96,768]{1,0:T(8,128)(2,1)S(1)} %copy-done.15), channel_id=1, source_target_pairs={{0,8},{8,16},{16,24},{24,28},{28,20},{20,12},{12,4},{4,0},{1,9},{9... | collective-permute-start | bytes 442376 | tf_op jit(solution)/shard_map/ppermute | solution.py:579
  34.0 2.4 %qkv.1 = (bf16[1024,768]{1,0:T(8,128)(2,1)S(1)}, bf16[1024,576]{1,0:T(8,128)(2,1)S(1)}, bf16[192,1024]{1,0:T(8,128)(2,1)S(1)}, bf16[768,640]{1,0:T(8,128)(2,1)S(1)}, f32[8,768]{1,0:T(8,128)S(1)}) custom-call(f32[1024,768]{1,0:T(8,128)S(1)} %unit.1.refs_0_.refs_2_, bf16[96,640]{1,0:T(8,128)(2,1)S(1)} %copy-done.6, ...), custom_call_target="tpu_custom_call" | custom-call | flops 1 | bytes 1 | tf_op jit(solution)/shard_map/qkv/pallas_call | solution.py:65
  37.2 2.9 %attend0.1 = (bf16[512,192]{1,0:T(8,128)(2,1)S(1)}, f32[8,512]{1,0:T(8,128)S(1)}) custom-call(bf16[1024,576]{1,0:T(8,128)(2,1)S(1)} %get-tuple-element.252.m_ref.refs_1_, bf16[192,1024]{1,0:T(8,128)(2,1)S(1)} %values.1.v_ref.refs_2_), custom_call_target="tpu_custom_call" | custom-call | flops 1 | bytes 1 | tf_op jit(solution)/shard_map/attend0/pallas_call | solution.py:65
  40.9 1.3 collective-permute-done.16.refs_5_
  42.3 1.7 %collective-permute-start.18 = (bf16[96,1152]{1,0:T(8,128)(2,1)S(1)}, bf16[96,1152]{1,0:T(8,128)(2,1)S(1)}, u32[]{:S(2)}, u32[]{:S(2)}) collective-permute-start(bf16[96,1152]{1,0:T(8,128)(2,1)S(1)} %collective-permute-done.13.refs_2_), channel_id=1, source_target_pairs={{0,8},{8,16},{16,24},{24,28},{28,20},{20,12},{12,4},{4,0},{1,9},{9... | collective-permute-start | bytes 663560 | tf_op jit(solution)/shard_map/ppermute | solution.py:579
  44.7 1.5 %collective-permute-start.20 = (bf16[96,768]{1,0:T(8,128)(2,1)S(1)}, bf16[96,768]{1,0:T(8,128)(2,1)S(1)}, u32[]{:S(2)}, u32[]{:S(2)}) collective-permute-start(bf16[96,768]{1,0:T(8,128)(2,1)S(1)} %collective-permute-done.15.refs_1_), channel_id=1, source_target_pairs={{0,8},{8,16},{16,24},{24,28},{28,20},{20,12},{12,4},{4,0},{1,9},{9... | collective-permute-start | bytes 442376 | tf_op jit(solution)/shard_map/ppermute | solution.py:579
  46.8 4.9 %attend1.1 = (bf16[512,192]{1,0:T(8,128)(2,1)S(1)}, f32[8,512]{1,0:T(8,128)S(1)}) custom-call(bf16[1024,576]{1,0:T(8,128)(2,1)S(1)} %get-tuple-element.252.m_ref.refs_1_, bf16[192,1024]{1,0:T(8,128)(2,1)S(1)} %values.1.v_ref.refs_2_), custom_call_target="tpu_custom_call" | custom-call | flops 1 | bytes 1 | tf_op jit(solution)/shard_map/attend1/pallas_call | solution.py:65
  52.2 1.4 collective-permute-done.21.refs_6_
  53.6 1.0 collective-permute-start.25
  55.1 1.0 collective-permute-start.26
  56.1 1.0 collective-permute-start.27
  57.2 5.1 %collective-permute-done.26.refs_3_ = bf16[96,768]{1,0:T(8,128)(2,1)S(1)} collective-permute-done((bf16[96,768]{1,0:T(8,128)(2,1)S(1)}, bf16[96,768]{1,0:T(8,128)(2,1)S(1)}, u32[]{:S(2)}, u32[]{:S(2)}) %collective-permute-start.26) | collective-permute-done | bytes 147488 | tf_op jit(solution)/shard_map/ppermute | solution.py:579
  64.0 1.1 collective-permute-start.32
  65.2 3.4 %mlp0.1 = (f32[512,768]{1,0:T(8,128)S(1)}, f32[512,768]{1,0:T(8,128)S(1)}, bf16[512,768]{1,0:T(8,128)(2,1)S(1)}, bf16[512,768]{1,0:T(8,128)(2,1)S(1)}, f32[512,768]{1,0:T(8,128)S(1)}) custom-call(bf16[1024,768]{1,0:T(8,128)(2,1)S(1)} %copy-done.1, f32[8,768]{1,0:T(8,128)S(1)} %get-tuple-element.267.norm_ref.refs_4_.refs_5_, ...), custom_call_target="tpu_custom_call" | custom-call | flops 1 | bytes 1 | tf_op jit(solution)/shard_map/mlp0/pallas_call | solution.py:65
  68.6 3.4 %mlp1.1 = (f32[512,768]{1,0:T(8,128)S(1)}, f32[512,768]{1,0:T(8,128)S(1)}, bf16[512,768]{1,0:T(8,128)(2,1)S(1)}, bf16[512,768]{1,0:T(8,128)(2,1)S(1)}, f32[512,768]{1,0:T(8,128)S(1)}) custom-call(bf16[1024,768]{1,0:T(8,128)(2,1)S(1)} %copy-done.1, f32[8,768]{1,0:T(8,128)S(1)} %get-tuple-element.267.norm_ref.refs_4_.refs_5_, ...), custom_call_target="tpu_custom_call" | custom-call | flops 1 | bytes 1 | tf_op jit(solution)/shard_map/mlp1/pallas_call | solution.py:65
  72.2 1.6 %mlp_back0.1 = (bf16[512,768]{1,0:T(8,128)(2,1)S(1)}, bf16[128,768]{1,0:T(8,128)(2,1)S(1)}, bf16[128,768]{1,0:T(8,128)(2,1)S(1)}, f32[256,768]{1,0:T(8,128)S(1)}, f32[8,768]{1,0:T(8,128)S(1)}) custom-call(bf16[1024,768]{1,0:T(8,128)(2,1)S(1)} %fetch.1.refs_0_.refs_4_.refs_3_, f32[512,768]{1,0:T(8,128)S(1)} %get-tuple-element.273.refs_1_, ...), custom_call_target="tpu_custom_call" | custom-call | flops 1 | bytes 1 | tf_op jit(solution)/shard_map/mlp_back0/pallas_call | solution.py:65
  74.3 1.6 %mlp_back1.1 = (bf16[512,768]{1,0:T(8,128)(2,1)S(1)}, bf16[128,768]{1,0:T(8,128)(2,1)S(1)}, bf16[128,768]{1,0:T(8,128)(2,1)S(1)}, f32[256,768]{1,0:T(8,128)S(1)}, f32[8,768]{1,0:T(8,128)S(1)}) custom-call(bf16[1024,768]{1,0:T(8,128)(2,1)S(1)} %fetch.1.refs_0_.refs_4_.refs_3_, f32[512,768]{1,0:T(8,128)S(1)} %get-tuple-element.279.refs_1_, ...), custom_call_target="tpu_custom_call" | custom-call | flops 1 | bytes 1 | tf_op jit(solution)/shard_map/mlp_back1/pallas_call | solution.py:65
  77.1 2.7 %mlp_grad.1 = (bf16[768,1536]{1,0:T(8,128)(2,1)S(1)}, bf16[96,1536]{1,0:T(8,128)(2,1)S(1)}, bf16[96,1536]{1,0:T(8,128)(2,1)S(1)}) custom-call(bf16[512,768]{1,0:T(8,128)(2,1)S(1)} %get-tuple-element.288.refs_0_, bf16[512,768]{1,0:T(8,128)(2,1)S(1)} %get-tuple-element.289.refs_1_, bf16[512,768]{1,0:T(8,128)(2,1)S(1)} %get-tuple-element.277.refs_2_, ...), custom_call_target="tpu_custom_call" | custom-call | flops 1 | bytes 1 | tf_op jit(solution)/shard_map/mlp_grad/pallas_call | solution.py:65
  80.7 1.2 collective-permute-start.38
  82.0 1.6 %collective-permute-start.40 = (bf16[256,768]{1,0:T(8,128)(2,1)S(1)}, bf16[256,768]{1,0:T(8,128)(2,1)S(1)}, u32[]{:S(2)}, u32[]{:S(2)}) collective-permute-start(bf16[256,768]{1,0:T(8,128)(2,1)S(1)} %add1.1.refs_1_), channel_id=1, source_target_pairs={{0,2},{1,3},{2,0},{3,1},{4,6},{5,7},{6,4},{7,5},{8,10},{9,11},{10,... | collective-permute-start | bytes 1179656 | tf_op jit(solution)/shard_map/ppermute | solution.py:567
  85.2 2.8 %collective-permute-done.39.refs_2_ = bf16[256,768]{1,0:T(8,128)(2,1)S(1)} collective-permute-done((bf16[256,768]{1,0:T(8,128)(2,1)S(1)}, bf16[256,768]{1,0:T(8,128)(2,1)S(1)}, u32[]{:S(2)}, u32[]{:S(2)}) %collective-permute-start.39) | collective-permute-done | bytes 393248 | tf_op jit(solution)/shard_map/ppermute | solution.py:567
  88.6 2.6 %all_gather.6.refs_3_.refs_2_ = bf16[512,768]{1,0:T(8,128)(2,1)S(1)} all-gather(bf16[256,768]{1,0:T(8,128)(2,1)S(1)} %get-tuple-element.303), channel_id=1, replica_groups={{0,1},{2,3},{4,5},{6,7},{8,9},{10,11},{12,13},{14,15},{16,17},{18,19},{..., dimensions={0}, use_global_device_ids=true | all-gather | bytes 1179648 | tf_op jit(solution)/shard_map/all_gather | solution.py:571
  91.2 2.9 %attend_back0.1 = (f32[512,192]{1,0:T(8,128)S(1)}, f32[512,192]{1,0:T(8,128)S(1)}, f32[512,192]{1,0:T(8,128)S(1)}) custom-call(s32[12]{0:T(128)S(1)} %copy-done.20, bf16[1024,576]{1,0:T(8,128)(2,1)S(1)} %get-tuple-element.252.m_ref.refs_1_, bf16[192,1024]{1,0:T(8,128)(2,1)S(1)} %values.1.v_ref.refs_2_, bf16[512,768]{1,0:T(8,128)(2,1)S(1)} %all_gather.6.refs_3_.refs_2_, ...), custom_call_target="tpu_custom_call" | custom-call | flops 1 | bytes 1 | tf_op jit(solution)/shard_map/attend_back0/pallas_call | solution.py:65
  94.8 0.9 collective-permute-start.41
  95.7 1.2 collective-permute-start.42
  98.3 2.4 %all_gather.7.refs_3_ = bf16[512,768]{1,0:T(8,128)(2,1)S(1)} all-gather(bf16[256,768]{1,0:T(8,128)(2,1)S(1)} %get-tuple-element.311), channel_id=1, replica_groups={{0,1},{2,3},{4,5},{6,7},{8,9},{10,11},{12,13},{14,15},{16,17},{18,19},{..., dimensions={0}, use_global_device_ids=true | all-gather | bytes 1179648 | tf_op jit(solution)/shard_map/all_gather | solution.py:571
  100.6 2.5 %attend_back1.1 = (f32[256,192]{1,0:T(8,128)S(1)}, f32[768,192]{1,0:T(8,128)S(1)}, f32[768,192]{1,0:T(8,128)S(1)}) custom-call(s32[12]{0:T(128)S(1)} %copy-done.20, bf16[1024,576]{1,0:T(8,128)(2,1)S(1)} %get-tuple-element.252.m_ref.refs_1_, bf16[192,1024]{1,0:T(8,128)(2,1)S(1)} %values.1.v_ref.refs_2_, bf16[512,768]{1,0:T(8,128)(2,1)S(1)} %all_gather.7.refs_3_, ...), custom_call_target="tpu_custom_call" | custom-call | flops 1 | bytes 1 | tf_op jit(solution)/shard_map/attend_back1/pallas_call | solution.py:65
  104.7 1.2 collective-permute-start.44
  106.7 3.1 %attend_back2.1 = (bf16[1024,576]{1,0:T(8,128)(2,1)S(1)}, bf16[192,1024]{1,0:T(8,128)(2,1)S(1)}) custom-call(s32[12]{0:T(128)S(1)} %copy-done.20, bf16[1024,576]{1,0:T(8,128)(2,1)S(1)} %get-tuple-element.252.m_ref.refs_1_, bf16[192,1024]{1,0:T(8,128)(2,1)S(1)} %values.1.v_ref.refs_2_, bf16[512,768]{1,0:T(8,128)(2,1)S(1)} %all_gather.7.refs_3_, ...), custom_call_target="tpu_custom_call" | custom-call | flops 1 | bytes 1 | tf_op jit(solution)/shard_map/attend_back2/pallas_call | solution.py:65
  109.9 1.4 input.1
  111.9 2.1 %qkv_grad.1 = (bf16[768,896]{1,0:T(8,128)(2,1)S(1)}, bf16[96,896]{1,0:T(8,128)(2,1)S(1)}, bf16[96,896]{1,0:T(8,128)(2,1)S(1)}) custom-call(bf16[1024,768]{1,0:T(8,128)(2,1)S(1)} %get-tuple-element.230.refs_0_, bf16[1024,576]{1,0:T(8,128)(2,1)S(1)} %get-tuple-element.328.refs_0_.refs_1_, bf16[512,768]{1,0:T(8,128)(2,1)S(1)} %all_gather.6.refs_3_.refs_2_, ...), custom_call_target="tpu_custom_call" | custom-call | flops 1 | bytes 1 | tf_op jit(solution)/shard_map/qkv_grad/pallas_call | solution.py:65
  114.9 1.2 collective-permute-start.49
  116.2 1.2 collective-permute-start.54
  118.5 1.2 collective-permute-start.57
  119.6 1.6 %collective-permute-done.48.refs_1_ = bf16[96,896]{1,0:T(8,128)(2,1)S(1)} collective-permute-done((bf16[96,896]{1,0:T(8,128)(2,1)S(1)}, bf16[96,896]{1,0:T(8,128)(2,1)S(1)}, u32[]{:S(2)}, u32[]{:S(2)}) %collective-permute-start.48) | collective-permute-done | bytes 172064 | tf_op jit(solution)/shard_map/ppermute | solution.py:579
  122.3 1.2 collective-permute-start.53
  124.4 3.2 %collective-permute-done.54.refs_1_ = bf16[96,1536]{1,0:T(8,128)(2,1)S(1)} collective-permute-done((bf16[96,1536]{1,0:T(8,128)(2,1)S(1)}, bf16[96,1536]{1,0:T(8,128)(2,1)S(1)}, u32[]{:S(2)}, u32[]{:S(2)}) %collective-permute-start.54) | collective-permute-done | bytes 294944 | tf_op jit(solution)/shard_map/ppermute | solution.py:579
  127.6 2.8 %collective-permute-done.52.refs_1_ = bf16[96,896]{1,0:T(8,128)(2,1)S(1)} collective-permute-done((bf16[96,896]{1,0:T(8,128)(2,1)S(1)}, bf16[96,896]{1,0:T(8,128)(2,1)S(1)}, u32[]{:S(2)}, u32[]{:S(2)}) %collective-permute-start.52) | collective-permute-done | bytes 172064 | tf_op jit(solution)/shard_map/ppermute | solution.py:579
  131.4 1.2 collective-permute-start.56
  132.6 1.6 %adam_fc.1 = (f32[96,768]{1,0:T(8,128)}, f32[96,768]{1,0:T(8,128)}, f32[96,768]{1,0:T(8,128)}, f32[96,768]{1,0:T(8,128)}, f32[96,768]{1,0:T(8,128)}, /*index=5*/f32[96,768]{1,0:T(8,128)}) custom-call(bf16[768,1536]{1,0:T(8,128)(2,1)S(1)} %get-tuple-element.291.refs_0_, bf16[96,1536]{1,0:T(8,128)(2,1)S(1)} %collective-permute-done.54.refs_1_, ...), custom_call_target="tpu_custom_call" | custom-call | flops 1 | bytes 1 | tf_op jit(solution)/shard_map/adam_fc/pallas_call | solution.py:65
  134.2 1.8 %collective-permute-done.57.refs_2_ = bf16[256,768]{1,0:T(8,128)(2,1)S(1)} collective-permute-done((bf16[256,768]{1,0:T(8,128)(2,1)S(1)}, bf16[256,768]{1,0:T(8,128)(2,1)S(1)}, u32[]{:S(2)}, u32[]{:S(2)}) %collective-permute-start.57) | collective-permute-done | bytes 393248 | tf_op jit(solution)/shard_map/ppermute | solution.py:567
  138.1 1.5 norm_one.1
  139.6 1.6 %first.1 = f32[192,1024]{1,0:T(8,128)} custom-call(s32[12]{0:T(128)S(1)} %copy-done.20, bf16[192,1024]{1,0:T(8,128)(2,1)S(1)} %get-tuple-element.372.refs_1_, bf16[192,1024]{1,0:T(8,128)(2,1)S(1)} %collective-permute-done.60.refs_2_, bf16[192,1024]{1,0:T(8,128)(2,1)S(1)} %collective-permute-done.58.refs_3_, bf16[192,1024]{1,0:T(8,128)(2,1)S(1)} %collective-permute-done.61.refs_4_), custom_call_target="tpu_custom_call" | custom-call | flops 1 | bytes 1 | tf_op jit(solution)/shard_map/first/pallas_call | solution.py:65
  141.3 2.5 %collective-permute-done.59.refs_1_ = bf16[96,896]{1,0:T(8,128)(2,1)S(1)} collective-permute-done((bf16[96,896]{1,0:T(8,128)(2,1)S(1)}, bf16[96,896]{1,0:T(8,128)(2,1)S(1)}, u32[]{:S(2)}, u32[]{:S(2)}) %collective-permute-start.59) | collective-permute-done | bytes 172064 | tf_op jit(solution)/shard_map/ppermute | solution.py:579
  143.9 1.2 collective-permute-done.62.b
  145.5 1.3 adam_qkv.1
  146.8 1.9 %collective-permute-done.63.received = f32[8,128]{1,0:T(8,128)S(1)} collective-permute-done((f32[8,128]{1,0:T(8,128)S(1)}, f32[8,128]{1,0:T(8,128)S(1)}, u32[]{:S(2)}, u32[]{:S(2)}) %collective-permute-start.63) | collective-permute-done | bytes 4128 | tf_op jit(solution)/shard_map/ppermute | solution.py:567
  (157 shorter events, 28.0 us)
Async XLA Ops:
  2.4 6.6 %collective-permute-start = (bf16[96,640]{1,0:T(8,128)(2,1)}, bf16[96,640]{1,0:T(8,128)(2,1)S(1)}, u32[]{:S(2)}, u32[]{:S(2)}) collective-permute-start(bf16[96,640]{1,0:T(8,128)(2,1)} %prep_one.1.refs_1_), channel_id=1, source_target_pairs={{0,8},{8,16},{16,24},{24,28},{28,20},{20,12},{12,4},{4,0},{1,9},{9... | collective-permute-start | bytes 368648 | tf_op jit(solution)/shard_map/ppermute | solution.py:579
  5.5 5.1 %collective-permute-start.1 = (bf16[96,640]{1,0:T(8,128)(2,1)}, bf16[96,640]{1,0:T(8,128)(2,1)S(1)}, u32[]{:S(2)}, u32[]{:S(2)}) collective-permute-start(bf16[96,640]{1,0:T(8,128)(2,1)} %prep_one.1.refs_1_), channel_id=1, source_target_pairs={{8,0},{16,8},{24,16},{28,24},{20,28},{12,20},{4,12},{0,4},{9,1},{1... | collective-permute-start | bytes 368648 | tf_op jit(solution)/shard_map/ppermute | solution.py:583
  10.6 6.3 %collective-permute-start.2 = (bf16[96,640]{1,0:T(8,128)(2,1)S(1)}, bf16[96,640]{1,0:T(8,128)(2,1)S(1)}, u32[]{:S(2)}, u32[]{:S(2)}) collective-permute-start(bf16[96,640]{1,0:T(8,128)(2,1)S(1)} %collective-permute-done.refs_2_), channel_id=1, source_target_pairs={{0,8},{8,16},{16,24},{24,28},{28,20},{20,12},{12,4},{4,0},{1,9},{9... | collective-permute-start | bytes 368648 | tf_op jit(solution)/shard_map/ppermute | solution.py:579
  12.2 4.9 %collective-permute-start.3 = (bf16[96,640]{1,0:T(8,128)(2,1)S(1)}, bf16[96,640]{1,0:T(8,128)(2,1)S(1)}, u32[]{:S(2)}, u32[]{:S(2)}) collective-permute-start(bf16[96,640]{1,0:T(8,128)(2,1)S(1)} %collective-permute-done.1.refs_6_), channel_id=1, source_target_pairs={{8,0},{16,8},{24,16},{28,24},{20,28},{12,20},{4,12},{0,4},{9,1},{1... | collective-permute-start | bytes 368648 | tf_op jit(solution)/shard_map/ppermute | solution.py:583
  12.6 4.3 %collective-permute-start.4 = (bf16[96,192]{1,0:T(8,128)(2,1)}, bf16[96,192]{1,0:T(8,128)(2,1)S(1)}, u32[]{:S(2)}, u32[]{:S(2)}) collective-permute-start(bf16[96,192]{1,0:T(8,128)(2,1)} %get-tuple-element.214.own), channel_id=1, source_target_pairs={{0,2},{1,3},{2,0},{3,1},{4,6},{5,7},{6,4},{7,5},{8,10},{9,11},{10,... | collective-permute-start | bytes 110600 | tf_op jit(solution)/shard_map/ppermute | solution.py:567
  17.1 12.8 %collective-permute-start.10 = (bf16[192,1024]{1,0:T(8,128)(2,1)S(1)}, bf16[192,1024]{1,0:T(8,128)(2,1)S(1)}, u32[]{:S(2)}, u32[]{:S(2)}) collective-permute-start(bf16[192,1024]{1,0:T(8,128)(2,1)S(1)} %bitcast.10), channel_id=1, source_target_pairs={{0,2},{1,3},{2,0},{3,1},{4,6},{5,7},{6,4},{7,5},{8,10},{9,11},{10,... | collective-permute-start | bytes 1179656 | tf_op jit(solution)/shard_map/ppermute | solution.py:567
  18.6 5.2 %collective-permute-start.5 = (bf16[96,640]{1,0:T(8,128)(2,1)S(1)}, bf16[96,640]{1,0:T(8,128)(2,1)S(1)}, u32[]{:S(2)}, u32[]{:S(2)}) collective-permute-start(bf16[96,640]{1,0:T(8,128)(2,1)S(1)} %collective-permute-done.2.refs_3_), channel_id=1, source_target_pairs={{0,8},{8,16},{16,24},{24,28},{28,20},{20,12},{12,4},{4,0},{1,9},{9... | collective-permute-start | bytes 368648 | tf_op jit(solution)/shard_map/ppermute | solution.py:579
  20.1 4.9 %collective-permute-start.6 = (bf16[96,640]{1,0:T(8,128)(2,1)S(1)}, bf16[96,640]{1,0:T(8,128)(2,1)S(1)}, u32[]{:S(2)}, u32[]{:S(2)}) collective-permute-start(bf16[96,640]{1,0:T(8,128)(2,1)S(1)} %collective-permute-done.3.refs_7_), channel_id=1, source_target_pairs={{8,0},{16,8},{24,16},{28,24},{20,28},{12,20},{4,12},{0,4},{9,1},{1... | collective-permute-start | bytes 368648 | tf_op jit(solution)/shard_map/ppermute | solution.py:583
  20.7 6.0 %collective-permute-start.8 = (bf16[96,1152]{1,0:T(8,128)(2,1)S(1)}, bf16[96,1152]{1,0:T(8,128)(2,1)S(1)}, u32[]{:S(2)}, u32[]{:S(2)}) collective-permute-start(bf16[96,1152]{1,0:T(8,128)(2,1)S(1)} %join.1.refs_0_), channel_id=1, source_target_pairs={{0,8},{8,16},{16,24},{24,28},{28,20},{20,12},{12,4},{4,0},{1,9},{9... | collective-permute-start | bytes 663560 | tf_op jit(solution)/shard_map/ppermute | solution.py:579
  22.3 5.9 %collective-permute-start.9 = (bf16[96,1152]{1,0:T(8,128)(2,1)S(1)}, bf16[96,1152]{1,0:T(8,128)(2,1)S(1)}, u32[]{:S(2)}, u32[]{:S(2)}) collective-permute-start(bf16[96,1152]{1,0:T(8,128)(2,1)S(1)} %join.1.refs_0_), channel_id=1, source_target_pairs={{8,0},{16,8},{24,16},{28,24},{20,28},{12,20},{4,12},{0,4},{9,1},{1... | collective-permute-start | bytes 663560 | tf_op jit(solution)/shard_map/ppermute | solution.py:583
  23.7 9.8 %collective-permute-start.11 = (bf16[192,1024]{1,0:T(8,128)(2,1)S(1)}, bf16[192,1024]{1,0:T(8,128)(2,1)S(1)}, u32[]{:S(2)}, u32[]{:S(2)}) collective-permute-start(bf16[192,1024]{1,0:T(8,128)(2,1)S(1)} %bitcast.11), channel_id=1, source_target_pairs={{0,1},{1,0},{2,3},{3,2},{4,5},{5,4},{6,7},{7,6},{8,9},{9,8},{10,11... | collective-permute-start | bytes 1179656 | tf_op jit(solution)/shard_map/ppermute | solution.py:563
  25.0 4.9 %collective-permute-start.7 = (bf16[96,640]{1,0:T(8,128)(2,1)S(1)}, bf16[96,640]{1,0:T(8,128)(2,1)S(1)}, u32[]{:S(2)}, u32[]{:S(2)}) collective-permute-start(bf16[96,640]{1,0:T(8,128)(2,1)S(1)} %collective-permute-done.5.refs_4_), channel_id=1, source_target_pairs={{0,8},{8,16},{16,24},{24,28},{28,20},{20,12},{12,4},{4,0},{1,9},{9... | collective-permute-start | bytes 368648 | tf_op jit(solution)/shard_map/ppermute | solution.py:579
  29.9 6.5 %collective-permute-start.12 = (bf16[192,1024]{1,0:T(8,128)(2,1)S(1)}, bf16[192,1024]{1,0:T(8,128)(2,1)S(1)}, u32[]{:S(2)}, u32[]{:S(2)}) collective-permute-start(bf16[192,1024]{1,0:T(8,128)(2,1)S(1)} %collective-permute-done.10.refs_4_), channel_id=1, source_target_pairs={{0,1},{1,0},{2,3},{3,2},{4,5},{5,4},{6,7},{7,6},{8,9},{9,8},{10,11... | collective-permute-start | bytes 1179656 | tf_op jit(solution)/shard_map/ppermute | solution.py:563
  29.9 12.3 %collective-permute-start.13 = (bf16[96,1152]{1,0:T(8,128)(2,1)S(1)}, bf16[96,1152]{1,0:T(8,128)(2,1)S(1)}, u32[]{:S(2)}, u32[]{:S(2)}) collective-permute-start(bf16[96,1152]{1,0:T(8,128)(2,1)S(1)} %collective-permute-done.8.refs_1_), channel_id=1, source_target_pairs={{0,8},{8,16},{16,24},{24,28},{28,20},{20,12},{12,4},{4,0},{1,9},{9... | collective-permute-start | bytes 663560 | tf_op jit(solution)/shard_map/ppermute | solution.py:579
  31.5 10.8 %collective-permute-start.14 = (bf16[96,1152]{1,0:T(8,128)(2,1)S(1)}, bf16[96,1152]{1,0:T(8,128)(2,1)S(1)}, u32[]{:S(2)}, u32[]{:S(2)}) collective-permute-start(bf16[96,1152]{1,0:T(8,128)(2,1)S(1)} %collective-permute-done.9.refs_5_), channel_id=1, source_target_pairs={{8,0},{16,8},{24,16},{28,24},{20,28},{12,20},{4,12},{0,4},{9,1},{1... | collective-permute-start | bytes 663560 | tf_op jit(solution)/shard_map/ppermute | solution.py:583
  32.0 8.9 %collective-permute-start.15 = (bf16[96,768]{1,0:T(8,128)(2,1)S(1)}, bf16[96,768]{1,0:T(8,128)(2,1)S(1)}, u32[]{:S(2)}, u32[]{:S(2)}) collective-permute-start(bf16[96,768]{1,0:T(8,128)(2,1)S(1)} %copy-done.15), channel_id=1, source_target_pairs={{0,8},{8,16},{16,24},{24,28},{28,20},{20,12},{12,4},{4,0},{1,9},{9... | collective-permute-start | bytes 442376 | tf_op jit(solution)/shard_map/ppermute | solution.py:579
  33.5 8.7 %collective-permute-start.16 = (bf16[96,768]{1,0:T(8,128)(2,1)S(1)}, bf16[96,768]{1,0:T(8,128)(2,1)S(1)}, u32[]{:S(2)}, u32[]{:S(2)}) collective-permute-start(bf16[96,768]{1,0:T(8,128)(2,1)S(1)} %copy-done.15), channel_id=1, source_target_pairs={{8,0},{16,8},{24,16},{28,24},{20,28},{12,20},{4,12},{0,4},{9,1},{1... | collective-permute-start | bytes 442376 | tf_op jit(solution)/shard_map/ppermute | solution.py:583
  42.3 11.3 %collective-permute-start.18 = (bf16[96,1152]{1,0:T(8,128)(2,1)S(1)}, bf16[96,1152]{1,0:T(8,128)(2,1)S(1)}, u32[]{:S(2)}, u32[]{:S(2)}) collective-permute-start(bf16[96,1152]{1,0:T(8,128)(2,1)S(1)} %collective-permute-done.13.refs_2_), channel_id=1, source_target_pairs={{0,8},{8,16},{16,24},{24,28},{28,20},{20,12},{12,4},{4,0},{1,9},{9... | collective-permute-start | bytes 663560 | tf_op jit(solution)/shard_map/ppermute | solution.py:579
  44.0 9.6 %collective-permute-start.19 = (bf16[96,1152]{1,0:T(8,128)(2,1)S(1)}, bf16[96,1152]{1,0:T(8,128)(2,1)S(1)}, u32[]{:S(2)}, u32[]{:S(2)}) collective-permute-start(bf16[96,1152]{1,0:T(8,128)(2,1)S(1)} %collective-permute-done.14.refs_6_), channel_id=1, source_target_pairs={{8,0},{16,8},{24,16},{28,24},{20,28},{12,20},{4,12},{0,4},{9,1},{1... | collective-permute-start | bytes 663560 | tf_op jit(solution)/shard_map/ppermute | solution.py:583
  44.3 9.3 %collective-permute-start.22 = (bf16[512,192]{1,0:T(8,128)(2,1)S(1)}, bf16[512,192]{1,0:T(8,128)(2,1)S(1)}, u32[]{:S(2)}, u32[]{:S(2)}) collective-permute-start(bf16[512,192]{1,0:T(8,128)(2,1)S(1)} %get-tuple-element.243.c0.refs_6_.refs_4_), channel_id=1, source_target_pairs={{0,2},{1,3},{2,0},{3,1},{4,6},{5,7},{6,4},{7,5},{8,10},{9,11},{10,... | collective-permute-start | bytes 589832 | tf_op jit(solution)/shard_map/ppermute | solution.py:567
  44.7 7.5 %collective-permute-start.20 = (bf16[96,768]{1,0:T(8,128)(2,1)S(1)}, bf16[96,768]{1,0:T(8,128)(2,1)S(1)}, u32[]{:S(2)}, u32[]{:S(2)}) collective-permute-start(bf16[96,768]{1,0:T(8,128)(2,1)S(1)} %collective-permute-done.15.refs_1_), channel_id=1, source_target_pairs={{0,8},{8,16},{16,24},{24,28},{28,20},{20,12},{12,4},{4,0},{1,9},{9... | collective-permute-start | bytes 442376 | tf_op jit(solution)/shard_map/ppermute | solution.py:579
  46.2 7.3 %collective-permute-start.21 = (bf16[96,768]{1,0:T(8,128)(2,1)S(1)}, bf16[96,768]{1,0:T(8,128)(2,1)S(1)}, u32[]{:S(2)}, u32[]{:S(2)}) collective-permute-start(bf16[96,768]{1,0:T(8,128)(2,1)S(1)} %collective-permute-done.16.refs_5_), channel_id=1, source_target_pairs={{8,0},{16,8},{24,16},{28,24},{20,28},{12,20},{4,12},{0,4},{9,1},{1... | collective-permute-start | bytes 442376 | tf_op jit(solution)/shard_map/ppermute | solution.py:583
  53.6 8.9 %collective-permute-start.25 = (bf16[96,1152]{1,0:T(8,128)(2,1)S(1)}, bf16[96,1152]{1,0:T(8,128)(2,1)S(1)}, u32[]{:S(2)}, u32[]{:S(2)}) collective-permute-start(bf16[96,1152]{1,0:T(8,128)(2,1)S(1)} %collective-permute-done.18.refs_3_), channel_id=1, source_target_pairs={{0,8},{8,16},{16,24},{24,28},{28,20},{20,12},{12,4},{4,0},{1,9},{9... | collective-permute-start | bytes 663560 | tf_op jit(solution)/shard_map/ppermute | solution.py:579
  54.6 7.8 %collective-permute-start.24 = (bf16[512,192]{1,0:T(8,128)(2,1)S(1)}, bf16[512,192]{1,0:T(8,128)(2,1)S(1)}, u32[]{:S(2)}, u32[]{:S(2)}) collective-permute-start(bf16[512,192]{1,0:T(8,128)(2,1)S(1)} %get-tuple-element.255.c0.refs_6_.refs_5_), channel_id=1, source_target_pairs={{0,2},{1,3},{2,0},{3,1},{4,6},{5,7},{6,4},{7,5},{8,10},{9,11},{10,... | collective-permute-start | bytes 589832 | tf_op jit(solution)/shard_map/ppermute | solution.py:567
  55.1 7.1 %collective-permute-start.26 = (bf16[96,768]{1,0:T(8,128)(2,1)S(1)}, bf16[96,768]{1,0:T(8,128)(2,1)S(1)}, u32[]{:S(2)}, u32[]{:S(2)}) collective-permute-start(bf16[96,768]{1,0:T(8,128)(2,1)S(1)} %collective-permute-done.20.refs_2_), channel_id=1, source_target_pairs={{0,8},{8,16},{16,24},{24,28},{28,20},{20,12},{12,4},{4,0},{1,9},{9... | collective-permute-start | bytes 442376 | tf_op jit(solution)/shard_map/ppermute | solution.py:579
  56.1 6.3 %collective-permute-start.27 = (bf16[96,768]{1,0:T(8,128)(2,1)S(1)}, bf16[96,768]{1,0:T(8,128)(2,1)S(1)}, u32[]{:S(2)}, u32[]{:S(2)}) collective-permute-start(bf16[96,768]{1,0:T(8,128)(2,1)S(1)} %collective-permute-done.21.refs_6_), channel_id=1, source_target_pairs={{8,0},{16,8},{24,16},{28,24},{20,28},{12,20},{4,12},{0,4},{9,1},{1... | collective-permute-start | bytes 442376 | tf_op jit(solution)/shard_map/ppermute | solution.py:583
  57.2 6.8 %collective-permute-start.17 = (bf16[512,192]{1,0:T(8,128)(2,1)S(1)}, bf16[512,192]{1,0:T(8,128)(2,1)S(1)}, u32[]{:S(2)}, u32[]{:S(2)}) collective-permute-start(bf16[512,192]{1,0:T(8,128)(2,1)S(1)} %get-tuple-element.243.c0.refs_6_.refs_4_), channel_id=1, source_target_pairs={{0,1},{1,0},{2,3},{3,2},{4,5},{5,4},{6,7},{7,6},{8,9},{9,8},{10,11... | collective-permute-start | bytes 589832 | tf_op jit(solution)/shard_map/ppermute | solution.py:563
  62.3 1.7 %collective-permute-start.23 = (bf16[512,192]{1,0:T(8,128)(2,1)S(1)}, bf16[512,192]{1,0:T(8,128)(2,1)S(1)}, u32[]{:S(2)}, u32[]{:S(2)}) collective-permute-start(bf16[512,192]{1,0:T(8,128)(2,1)S(1)} %collective-permute-done.22.c2), channel_id=1, source_target_pairs={{0,1},{1,0},{2,3},{3,2},{4,5},{5,4},{6,7},{7,6},{8,9},{9,8},{10,11... | collective-permute-start | bytes 589832 | tf_op jit(solution)/shard_map/ppermute | solution.py:563
  62.9 2.3 %collective-permute-start.29 = (bf16[192,768]{1,0:T(8,128)(2,1)S(1)}, bf16[192,768]{1,0:T(8,128)(2,1)S(1)}, u32[]{:S(2)}, u32[]{:S(2)}) collective-permute-start(bf16[192,768]{1,0:T(8,128)(2,1)S(1)} %get-tuple-element.264.w2), channel_id=1, source_target_pairs={{0,1},{1,0},{2,3},{3,2},{4,5},{5,4},{6,7},{7,6},{8,9},{9,8},{10,11... | collective-permute-start | bytes 884744 | tf_op jit(solution)/shard_map/ppermute | solution.py:563
  63.4 1.7 %collective-permute-start.28 = (bf16[192,768]{1,0:T(8,128)(2,1)S(1)}, bf16[192,768]{1,0:T(8,128)(2,1)S(1)}, u32[]{:S(2)}, u32[]{:S(2)}) collective-permute-start(bf16[192,768]{1,0:T(8,128)(2,1)S(1)} %get-tuple-element.263.w0.refs_4_), channel_id=1, source_target_pairs={{0,1},{1,0},{2,3},{3,2},{4,5},{5,4},{6,7},{7,6},{8,9},{9,8},{10,11... | collective-permute-start | bytes 884744 | tf_op jit(solution)/shard_map/ppermute | solution.py:563
  63.5 5.1 %collective-permute-start.30 = (bf16[512,192]{1,0:T(8,128)(2,1)S(1)}, bf16[512,192]{1,0:T(8,128)(2,1)S(1)}, u32[]{:S(2)}, u32[]{:S(2)}) collective-permute-start(bf16[512,192]{1,0:T(8,128)(2,1)S(1)} %get-tuple-element.255.c0.refs_6_.refs_5_), channel_id=1, source_target_pairs={{0,1},{1,0},{2,3},{3,2},{4,5},{5,4},{6,7},{7,6},{8,9},{9,8},{10,11... | collective-permute-start | bytes 589832 | tf_op jit(solution)/shard_map/ppermute | solution.py:563
  63.9 4.7 %collective-permute-start.31 = (bf16[512,192]{1,0:T(8,128)(2,1)S(1)}, bf16[512,192]{1,0:T(8,128)(2,1)S(1)}, u32[]{:S(2)}, u32[]{:S(2)}) collective-permute-start(bf16[512,192]{1,0:T(8,128)(2,1)S(1)} %collective-permute-done.24.c2), channel_id=1, source_target_pairs={{0,1},{1,0},{2,3},{3,2},{4,5},{5,4},{6,7},{7,6},{8,9},{9,8},{10,11... | collective-permute-start | bytes 589832 | tf_op jit(solution)/shard_map/ppermute | solution.py:563
  64.0 8.0 %collective-permute-start.32 = (bf16[96,768]{1,0:T(8,128)(2,1)S(1)}, bf16[96,768]{1,0:T(8,128)(2,1)S(1)}, u32[]{:S(2)}, u32[]{:S(2)}) collective-permute-start(bf16[96,768]{1,0:T(8,128)(2,1)S(1)} %collective-permute-done.26.refs_3_), channel_id=1, source_target_pairs={{0,8},{8,16},{16,24},{24,28},{28,20},{20,12},{12,4},{4,0},{1,9},{9... | collective-permute-start | bytes 442376 | tf_op jit(solution)/shard_map/ppermute | solution.py:579
  73.8 2.2 %collective-permute-start.33 = (bf16[128,768]{1,0:T(8,128)(2,1)S(1)}, bf16[128,768]{1,0:T(8,128)(2,1)S(1)}, u32[]{:S(2)}, u32[]{:S(2)}) collective-permute-start(bf16[128,768]{1,0:T(8,128)(2,1)S(1)} %get-tuple-element.286), channel_id=1, source_target_pairs={{0,1},{1,0},{2,3},{3,2},{4,5},{5,4},{6,7},{7,6},{8,9},{9,8},{10,11... | collective-permute-start | bytes 589832 | tf_op jit(solution)/shard_map/ppermute | solution.py:563
  74.1 1.9 %collective-permute-start.34 = (bf16[128,768]{1,0:T(8,128)(2,1)S(1)}, bf16[128,768]{1,0:T(8,128)(2,1)S(1)}, u32[]{:S(2)}, u32[]{:S(2)}) collective-permute-start(bf16[128,768]{1,0:T(8,128)(2,1)S(1)} %get-tuple-element.287), channel_id=1, source_target_pairs={{0,1},{1,0},{2,3},{3,2},{4,5},{5,4},{6,7},{7,6},{8,9},{9,8},{10,11... | collective-permute-start | bytes 589832 | tf_op jit(solution)/shard_map/ppermute | solution.py:563
  76.0 12.0 %collective-permute-start.39 = (bf16[256,768]{1,0:T(8,128)(2,1)S(1)}, bf16[256,768]{1,0:T(8,128)(2,1)S(1)}, u32[]{:S(2)}, u32[]{:S(2)}) collective-permute-start(bf16[256,768]{1,0:T(8,128)(2,1)S(1)} %add0.1.refs_1_), channel_id=1, source_target_pairs={{0,2},{1,3},{2,0},{3,1},{4,6},{5,7},{6,4},{7,5},{8,10},{9,11},{10,... | collective-permute-start | bytes 1179656 | tf_op jit(solution)/shard_map/ppermute | solution.py:567
  76.6 5.3 %collective-permute-start.35 = (bf16[128,768]{1,0:T(8,128)(2,1)S(1)}, bf16[128,768]{1,0:T(8,128)(2,1)S(1)}, u32[]{:S(2)}, u32[]{:S(2)}) collective-permute-start(bf16[128,768]{1,0:T(8,128)(2,1)S(1)} %get-tuple-element.293), channel_id=1, source_target_pairs={{0,1},{1,0},{2,3},{3,2},{4,5},{5,4},{6,7},{7,6},{8,9},{9,8},{10,11... | collective-permute-start | bytes 589832 | tf_op jit(solution)/shard_map/ppermute | solution.py:563
  76.6 5.3 %collective-permute-start.36 = (bf16[128,768]{1,0:T(8,128)(2,1)S(1)}, bf16[128,768]{1,0:T(8,128)(2,1)S(1)}, u32[]{:S(2)}, u32[]{:S(2)}) collective-permute-start(bf16[128,768]{1,0:T(8,128)(2,1)S(1)} %get-tuple-element.294), channel_id=1, source_target_pairs={{0,1},{1,0},{2,3},{3,2},{4,5},{5,4},{6,7},{7,6},{8,9},{9,8},{10,11... | collective-permute-start | bytes 589832 | tf_op jit(solution)/shard_map/ppermute | solution.py:563
  79.8 14.3 %collective-permute-start.37 = (bf16[96,1536]{1,0:T(8,128)(2,1)S(1)}, bf16[96,1536]{1,0:T(8,128)(2,1)S(1)}, u32[]{:S(2)}, u32[]{:S(2)}) collective-permute-start(bf16[96,1536]{1,0:T(8,128)(2,1)S(1)} %get-tuple-element.295), channel_id=1, source_target_pairs={{0,8},{8,16},{16,24},{24,28},{28,20},{20,12},{12,4},{4,0},{1,9},{9... | collective-permute-start | bytes 884744 | tf_op jit(solution)/shard_map/ppermute | solution.py:579
  80.7 13.4 %collective-permute-start.38 = (bf16[96,1536]{1,0:T(8,128)(2,1)S(1)}, bf16[96,1536]{1,0:T(8,128)(2,1)S(1)}, u32[]{:S(2)}, u32[]{:S(2)}) collective-permute-start(bf16[96,1536]{1,0:T(8,128)(2,1)S(1)} %get-tuple-element.296), channel_id=1, source_target_pairs={{8,0},{16,8},{24,16},{28,24},{20,28},{12,20},{4,12},{0,4},{9,1},{1... | collective-permute-start | bytes 884744 | tf_op jit(solution)/shard_map/ppermute | solution.py:583
  82.0 14.9 %collective-permute-start.40 = (bf16[256,768]{1,0:T(8,128)(2,1)S(1)}, bf16[256,768]{1,0:T(8,128)(2,1)S(1)}, u32[]{:S(2)}, u32[]{:S(2)}) collective-permute-start(bf16[256,768]{1,0:T(8,128)(2,1)S(1)} %add1.1.refs_1_), channel_id=1, source_target_pairs={{0,2},{1,3},{2,0},{3,1},{4,6},{5,7},{6,4},{7,5},{8,10},{9,11},{10,... | collective-permute-start | bytes 1179656 | tf_op jit(solution)/shard_map/ppermute | solution.py:567
  94.1 3.4 %collective-permute-start.45 = (bf16[256,768]{1,0:T(8,128)(2,1)S(1)}, bf16[256,768]{1,0:T(8,128)(2,1)S(1)}, u32[]{:S(2)}, u32[]{:S(2)}) collective-permute-start(bf16[256,768]{1,0:T(8,128)(2,1)S(1)} %get-tuple-element.339), channel_id=1, source_target_pairs={{0,1},{1,0},{2,3},{3,2},{4,5},{5,4},{6,7},{7,6},{8,9},{9,8},{10,11... | collective-permute-start | bytes 1179656 | tf_op jit(solution)/shard_map/ppermute | solution.py:563
  94.3 3.2 %collective-permute-start.46 = (bf16[256,768]{1,0:T(8,128)(2,1)S(1)}, bf16[256,768]{1,0:T(8,128)(2,1)S(1)}, u32[]{:S(2)}, u32[]{:S(2)}) collective-permute-start(bf16[256,768]{1,0:T(8,128)(2,1)S(1)} %get-tuple-element.309), channel_id=1, source_target_pairs={{0,1},{1,0},{2,3},{3,2},{4,5},{5,4},{6,7},{7,6},{8,9},{9,8},{10,11... | collective-permute-start | bytes 1179656 | tf_op jit(solution)/shard_map/ppermute | solution.py:563
  94.8 9.1 %collective-permute-start.41 = (bf16[96,1536]{1,0:T(8,128)(2,1)S(1)}, bf16[96,1536]{1,0:T(8,128)(2,1)S(1)}, u32[]{:S(2)}, u32[]{:S(2)}) collective-permute-start(bf16[96,1536]{1,0:T(8,128)(2,1)S(1)} %get-tuple-element.318), channel_id=1, source_target_pairs={{0,8},{8,16},{16,24},{24,28},{28,20},{20,12},{12,4},{4,0},{1,9},{9... | collective-permute-start | bytes 884744 | tf_op jit(solution)/shard_map/ppermute | solution.py:579
  95.7 8.8 %collective-permute-start.42 = (bf16[96,1536]{1,0:T(8,128)(2,1)S(1)}, bf16[96,1536]{1,0:T(8,128)(2,1)S(1)}, u32[]{:S(2)}, u32[]{:S(2)}) collective-permute-start(bf16[96,1536]{1,0:T(8,128)(2,1)S(1)} %get-tuple-element.319), channel_id=1, source_target_pairs={{8,0},{16,8},{24,16},{28,24},{20,28},{12,20},{4,12},{0,4},{9,1},{1... | collective-permute-start | bytes 884744 | tf_op jit(solution)/shard_map/ppermute | solution.py:583
  97.7 16.2 %collective-permute-start.47 = (bf16[256,768]{1,0:T(8,128)(2,1)S(1)}, bf16[256,768]{1,0:T(8,128)(2,1)S(1)}, u32[]{:S(2)}, u32[]{:S(2)}) collective-permute-start(bf16[256,768]{1,0:T(8,128)(2,1)S(1)} %get-tuple-element.342), channel_id=1, source_target_pairs={{0,2},{1,3},{2,0},{3,1},{4,6},{5,7},{6,4},{7,5},{8,10},{9,11},{10,... | collective-permute-start | bytes 1179656 | tf_op jit(solution)/shard_map/ppermute | solution.py:567
  104.7 9.3 %collective-permute-start.44 = (bf16[96,1536]{1,0:T(8,128)(2,1)S(1)}, bf16[96,1536]{1,0:T(8,128)(2,1)S(1)}, u32[]{:S(2)}, u32[]{:S(2)}) collective-permute-start(bf16[96,1536]{1,0:T(8,128)(2,1)S(1)} %get-tuple-element.334), channel_id=1, source_target_pairs={{8,0},{16,8},{24,16},{28,24},{20,28},{12,20},{4,12},{0,4},{9,1},{1... | collective-permute-start | bytes 884744 | tf_op jit(solution)/shard_map/ppermute | solution.py:583
  105.9 8.1 %collective-permute-start.43 = (bf16[96,1536]{1,0:T(8,128)(2,1)S(1)}, bf16[96,1536]{1,0:T(8,128)(2,1)S(1)}, u32[]{:S(2)}, u32[]{:S(2)}) collective-permute-start(bf16[96,1536]{1,0:T(8,128)(2,1)S(1)} %get-tuple-element.323), channel_id=1, source_target_pairs={{0,8},{8,16},{16,24},{24,28},{28,20},{20,12},{12,4},{4,0},{1,9},{9... | collective-permute-start | bytes 884744 | tf_op jit(solution)/shard_map/ppermute | solution.py:579
  111.3 6.0 %collective-permute-start.50 = (bf16[256,768]{1,0:T(8,128)(2,1)S(1)}, bf16[256,768]{1,0:T(8,128)(2,1)S(1)}, u32[]{:S(2)}, u32[]{:S(2)}) collective-permute-start(bf16[256,768]{1,0:T(8,128)(2,1)S(1)} %get-tuple-element.346), channel_id=1, source_target_pairs={{0,1},{1,0},{2,3},{3,2},{4,5},{5,4},{6,7},{7,6},{8,9},{9,8},{10,11... | collective-permute-start | bytes 1179656 | tf_op jit(solution)/shard_map/ppermute | solution.py:563
  111.4 6.9 %collective-permute-start.51 = (bf16[256,768]{1,0:T(8,128)(2,1)S(1)}, bf16[256,768]{1,0:T(8,128)(2,1)S(1)}, u32[]{:S(2)}, u32[]{:S(2)}) collective-permute-start(bf16[256,768]{1,0:T(8,128)(2,1)S(1)} %get-tuple-element.347), channel_id=1, source_target_pairs={{0,1},{1,0},{2,3},{3,2},{4,5},{5,4},{6,7},{7,6},{8,9},{9,8},{10,11... | collective-permute-start | bytes 1179656 | tf_op jit(solution)/shard_map/ppermute | solution.py:563
  114.0 7.3 %collective-permute-start.48 = (bf16[96,896]{1,0:T(8,128)(2,1)S(1)}, bf16[96,896]{1,0:T(8,128)(2,1)S(1)}, u32[]{:S(2)}, u32[]{:S(2)}) collective-permute-start(bf16[96,896]{1,0:T(8,128)(2,1)S(1)} %get-tuple-element.343), channel_id=1, source_target_pairs={{0,8},{8,16},{16,24},{24,28},{28,20},{20,12},{12,4},{4,0},{1,9},{9... | collective-permute-start | bytes 516104 | tf_op jit(solution)/shard_map/ppermute | solution.py:579
  114.9 6.4 %collective-permute-start.49 = (bf16[96,896]{1,0:T(8,128)(2,1)S(1)}, bf16[96,896]{1,0:T(8,128)(2,1)S(1)}, u32[]{:S(2)}, u32[]{:S(2)}) collective-permute-start(bf16[96,896]{1,0:T(8,128)(2,1)S(1)} %get-tuple-element.344), channel_id=1, source_target_pairs={{8,0},{16,8},{24,16},{28,24},{20,28},{12,20},{4,12},{0,4},{9,1},{1... | collective-permute-start | bytes 516104 | tf_op jit(solution)/shard_map/ppermute | solution.py:583
  116.2 11.4 %collective-permute-start.54 = (bf16[96,1536]{1,0:T(8,128)(2,1)S(1)}, bf16[96,1536]{1,0:T(8,128)(2,1)S(1)}, u32[]{:S(2)}, u32[]{:S(2)}) collective-permute-start(bf16[96,1536]{1,0:T(8,128)(2,1)S(1)} %mlp_hop1.1), channel_id=1, source_target_pairs={{0,8},{8,16},{16,24},{24,28},{28,20},{20,12},{12,4},{4,0},{1,9},{9... | collective-permute-start | bytes 884744 | tf_op jit(solution)/shard_map/ppermute | solution.py:579
  117.3 16.9 %collective-permute-start.58 = (bf16[192,1024]{1,0:T(8,128)(2,1)S(1)}, bf16[192,1024]{1,0:T(8,128)(2,1)S(1)}, u32[]{:S(2)}, u32[]{:S(2)}) collective-permute-start(bf16[192,1024]{1,0:T(8,128)(2,1)S(1)} %get-tuple-element.372.refs_1_), channel_id=1, source_target_pairs={{0,2},{1,3},{2,0},{3,1},{4,6},{5,7},{6,4},{7,5},{8,10},{9,11},{10,... | collective-permute-start | bytes 1179656 | tf_op jit(solution)/shard_map/ppermute | solution.py:567
  118.5 17.5 %collective-permute-start.57 = (bf16[256,768]{1,0:T(8,128)(2,1)S(1)}, bf16[256,768]{1,0:T(8,128)(2,1)S(1)}, u32[]{:S(2)}, u32[]{:S(2)}) collective-permute-start(bf16[256,768]{1,0:T(8,128)(2,1)S(1)} %get-tuple-element.348), channel_id=1, source_target_pairs={{0,2},{1,3},{2,0},{3,1},{4,6},{5,7},{6,4},{7,5},{8,10},{9,11},{10,... | collective-permute-start | bytes 1179656 | tf_op jit(solution)/shard_map/ppermute | solution.py:567
  121.4 9.0 %collective-permute-start.52 = (bf16[96,896]{1,0:T(8,128)(2,1)S(1)}, bf16[96,896]{1,0:T(8,128)(2,1)S(1)}, u32[]{:S(2)}, u32[]{:S(2)}) collective-permute-start(bf16[96,896]{1,0:T(8,128)(2,1)S(1)} %get-tuple-element.351), channel_id=1, source_target_pairs={{0,8},{8,16},{16,24},{24,28},{28,20},{20,12},{12,4},{4,0},{1,9},{9... | collective-permute-start | bytes 516104 | tf_op jit(solution)/shard_map/ppermute | solution.py:579
  122.3 8.1 %collective-permute-start.53 = (bf16[96,896]{1,0:T(8,128)(2,1)S(1)}, bf16[96,896]{1,0:T(8,128)(2,1)S(1)}, u32[]{:S(2)}, u32[]{:S(2)}) collective-permute-start(bf16[96,896]{1,0:T(8,128)(2,1)S(1)} %get-tuple-element.352), channel_id=1, source_target_pairs={{8,0},{16,8},{24,16},{28,24},{20,28},{12,20},{4,12},{0,4},{9,1},{1... | collective-permute-start | bytes 516104 | tf_op jit(solution)/shard_map/ppermute | solution.py:583
  130.5 5.6 %collective-permute-start.55 = (bf16[96,896]{1,0:T(8,128)(2,1)S(1)}, bf16[96,896]{1,0:T(8,128)(2,1)S(1)}, u32[]{:S(2)}, u32[]{:S(2)}) collective-permute-start(bf16[96,896]{1,0:T(8,128)(2,1)S(1)} %get-tuple-element.359), channel_id=1, source_target_pairs={{0,8},{8,16},{16,24},{24,28},{28,20},{20,12},{12,4},{4,0},{1,9},{9... | collective-permute-start | bytes 516104 | tf_op jit(solution)/shard_map/ppermute | solution.py:579
  131.4 5.4 %collective-permute-start.56 = (bf16[96,896]{1,0:T(8,128)(2,1)S(1)}, bf16[96,896]{1,0:T(8,128)(2,1)S(1)}, u32[]{:S(2)}, u32[]{:S(2)}) collective-permute-start(bf16[96,896]{1,0:T(8,128)(2,1)S(1)} %get-tuple-element.360), channel_id=1, source_target_pairs={{8,0},{16,8},{24,16},{28,24},{20,28},{12,20},{4,12},{0,4},{9,1},{1... | collective-permute-start | bytes 516104 | tf_op jit(solution)/shard_map/ppermute | solution.py:583
  136.8 2.8 %collective-permute-start.60 = (bf16[192,1024]{1,0:T(8,128)(2,1)S(1)}, bf16[192,1024]{1,0:T(8,128)(2,1)S(1)}, u32[]{:S(2)}, u32[]{:S(2)}) collective-permute-start(bf16[192,1024]{1,0:T(8,128)(2,1)S(1)} %get-tuple-element.372.refs_1_), channel_id=1, source_target_pairs={{0,1},{1,0},{2,3},{3,2},{4,5},{5,4},{6,7},{7,6},{8,9},{9,8},{10,11... | collective-permute-start | bytes 1179656 | tf_op jit(solution)/shard_map/ppermute | solution.py:563
  136.8 2.8 %collective-permute-start.61 = (bf16[192,1024]{1,0:T(8,128)(2,1)S(1)}, bf16[192,1024]{1,0:T(8,128)(2,1)S(1)}, u32[]{:S(2)}, u32[]{:S(2)}) collective-permute-start(bf16[192,1024]{1,0:T(8,128)(2,1)S(1)} %collective-permute-done.58.refs_3_), channel_id=1, source_target_pairs={{0,1},{1,0},{2,3},{3,2},{4,5},{5,4},{6,7},{7,6},{8,9},{9,8},{10,11... | collective-permute-start | bytes 1179656 | tf_op jit(solution)/shard_map/ppermute | solution.py:563
  137.4 6.3 %collective-permute-start.59 = (bf16[96,896]{1,0:T(8,128)(2,1)S(1)}, bf16[96,896]{1,0:T(8,128)(2,1)S(1)}, u32[]{:S(2)}, u32[]{:S(2)}) collective-permute-start(bf16[96,896]{1,0:T(8,128)(2,1)S(1)} %qkv_hop1.1), channel_id=1, source_target_pairs={{0,8},{8,16},{16,24},{24,28},{28,20},{20,12},{12,4},{4,0},{1,9},{9... | collective-permute-start | bytes 516104 | tf_op jit(solution)/shard_map/ppermute | solution.py:579
  143.8 1.2 collective-permute-start.62
  145.0 3.6 %collective-permute-start.63 = (f32[8,128]{1,0:T(8,128)S(1)}, f32[8,128]{1,0:T(8,128)S(1)}, u32[]{:S(2)}, u32[]{:S(2)}) collective-permute-start(f32[8,128]{1,0:T(8,128)S(1)} %sum.1.sums), channel_id=1, source_target_pairs={{0,2},{1,3},{2,0},{3,1},{4,6},{5,7},{6,4},{7,5},{8,10},{9,11},{10,... | collective-permute-start | bytes 12296 | tf_op jit(solution)/shard_map/ppermute | solution.py:567
  (24 other events, 183.0 us)
